TPU v7x, 256 devices: a whole 4x4x8 slice. The times are simulated.
256 devices in a mesh: dp: 8 (over y, core), queue: 32 (over z, x).
Axes of the slice: x: 4, y: 4, z: 8, core: 2. Of those that a mesh axis runs over, the one named last changes fastest.
Arguments:
- features: bfloat16 [131072, 1024], P(('dp', 'queue')), may hold values from -1 to 1
- weight: bfloat16 [1024, 256], replicated, may hold values from -2 to 2
- support_queue: bfloat16 [262144, 256], P('queue'), may hold values from -100 to 100
- owner_shard: int32 [131072, 1], P(('dp', 'queue')), may hold values from 0 to 31; in each aligned block of 512 rows (0 to 511, 512 to 1023, ...) at most 64 rows name the same one
- slot_row: int32 [131072], P(('dp', 'queue')), may hold values from 0 to 8191
- loss_weight: bfloat16 [131072], P(('dp', 'queue')), may hold values from 0.5 to 2
Outputs:
- grad_feats: bfloat16 [131072, 1024], P(('dp', 'queue'))
- grad_weight: float32 [1024, 256], replicated
Inputs may be any that keep to these rules, and one draw needn't show every extreme that they name: `owner_shard`: among the rows of one device no shard is named by more than 64 rows, a bound that some block reaches.
All inputs are finite; a program needn't handle non-finite values.
Results may differ from a plain program's by a relative error of at most 0.0035.
Values may be sent and summed in bfloat16 or wider, within the bound.
No kernel may reach another device: no remote copies, remote signals or barrier semaphores. Data moves between devices by JAX's collectives and lax.ppermute only.
A program may use at most 128 MiB of HBM per device.

v0:
```python
import math

import jax
import jax.numpy as jnp
from jax import lax
from jax.experimental import pallas as pl
from jax.experimental.pallas import tpu as pltpu
from jax.sharding import Mesh
from jax.sharding import PartitionSpec as P

TEMPER = 0.1
EPSILON = 1e-06
NZ, NX, NY, NC = 8, 4, 4, 2
CAP = 64
BF = jnp.bfloat16
F32 = jnp.float32
VMEM_LIMIT = 48 * 1024 * 1024
EXPONENT = math.log2(math.e) / TEMPER
QUEUE = ("z", "x")


def shift(size, by):
    return [(i, (i + by) % size) for i in range(size)]


def flip(size, mask):
    return [(i, i ^ mask) for i in range(size)]


def vmem_call(kernel, out_shape, name, limit=VMEM_LIMIT, **kw):
    return pl.pallas_call(
        kernel,
        out_shape=out_shape,
        compiler_params=pltpu.CompilerParams(vmem_limit_bytes=limit),
        name=name,
        **kw,
    )


def plan_kernel(owner_ref, slot_ref, wanted_ref, places_ref):
    n = owner_ref.shape[0]
    owner = owner_ref[...]
    slot = slot_ref[...]
    shard = lax.broadcasted_iota(jnp.int32, (n, 128), 1)
    onehot = (owner == shard).astype(F32)
    below = (
        lax.broadcasted_iota(jnp.int32, (n, n), 1) < lax.broadcasted_iota(jnp.int32, (n, n), 0)
    ).astype(F32).astype(BF)
    before = jnp.dot(below, onehot.astype(BF), preferred_element_type=F32)
    rank = jnp.sum(before * onehot, axis=1, keepdims=True).astype(jnp.int32)
    places_ref[...] = owner * CAP + rank
    chosen = rank == lax.broadcasted_iota(jnp.int32, (n, 128), 1)
    high = jnp.where(chosen, (slot >> 7).astype(F32), 0.0).astype(BF)
    low = jnp.where(chosen, (slot & 127).astype(F32), 0.0).astype(BF)
    across = (((0,), (0,)), ((), ()))
    hot = onehot.astype(BF)
    upper = lax.dot_general(hot, high, across, preferred_element_type=F32)
    lower = lax.dot_general(hot, low, across, preferred_element_type=F32)
    full = upper.astype(jnp.int32) * 128 + lower.astype(jnp.int32)
    wanted_ref[...] = full[: wanted_ref.shape[0], :CAP]


def plan(owner, slot):
    n = owner.shape[0]
    return vmem_call(
        plan_kernel,
        (
            jax.ShapeDtypeStruct((NZ * NX, CAP), jnp.int32),
            jax.ShapeDtypeStruct((n, 1), jnp.int32),
        ),
        "plan",
    )(owner, slot)


def pick_kernel(rows_ref, places_ref, extra_ref, out_ref):
    n = places_ref.shape[0]
    places = places_ref[...]
    column = lax.broadcasted_iota(jnp.int32, (n, n), 1)
    total = None
    for at in range(0, rows_ref.shape[0], n):
        onehot = jnp.where(places == column + at, 1.0, 0.0).astype(BF)
        term = jnp.dot(onehot, rows_ref[at : at + n, :], preferred_element_type=F32)
        total = term if total is None else total + term
    unit = total * lax.rsqrt(jnp.sum(total * total, axis=1, keepdims=True) + EPSILON)
    out_ref[:n, :] = unit.astype(BF)
    out_ref[n:, :] = extra_ref[...]


def pick(rows, places, extra):
    n = places.shape[0]
    return vmem_call(
        pick_kernel, jax.ShapeDtypeStruct((n + extra.shape[0], rows.shape[1]), BF), "pick"
    )(rows, places, extra)


def exps_kernel(a_ref, v_ref, e_ref, t_ref, sum_ref):
    step = pl.program_id(0)
    n = e_ref.shape[2]
    a = a_ref[:n, :]
    half = v_ref.shape[1] // 2
    total = jnp.zeros((8, n), F32)
    for k in range(v_ref.shape[0]):
        for at in (0, half):
            dots = lax.dot_general(
                v_ref[k, at : at + half, :], a, (((1,), (1,)), ((), ())), preferred_element_type=F32
            )
            e = jnp.exp2(dots * EXPONENT)
            total = total + jnp.sum(e.reshape(half // 8, 8, n), axis=0)
            e_ref[k, at : at + half, :] = e.astype(BF)

    @pl.when(step == 0)
    def _():
        sum_ref[...] = total

    @pl.when(step > 0)
    def _():
        sum_ref[...] += total

    @pl.when(step == pl.num_programs(0) - 1)
    def _():
        t_ref[...] = jnp.sum(sum_ref[...], axis=0, keepdims=True)


def exps(anchors, views):
    many, n, width = views.shape
    each = 2
    return vmem_call(
        exps_kernel,
        (jax.ShapeDtypeStruct((many, n, n), BF), jax.ShapeDtypeStruct((1, n), F32)),
        "exps",
        grid=(many // each,),
        in_specs=[
            pl.BlockSpec(anchors.shape, lambda i: (0, 0)),
            pl.BlockSpec((each, n, width), lambda i: (i, 0, 0)),
        ],
        out_specs=(
            pl.BlockSpec((each, n, n), lambda i: (i, 0, 0)),
            pl.BlockSpec((1, n), lambda i: (0, 0)),
        ),
        scratch_shapes=[pltpu.VMEM((8, n), F32)],
    )(anchors, views)


def scale_kernel(*refs):
    anchors = refs[:NX]
    totals = refs[NX : 2 * NX]
    out_ref = refs[2 * NX]
    n = out_ref.shape[0] // NX
    width = out_ref.shape[1]
    for b in range(NX):
        t = None
        for k in range(NX):
            at = ((b - k) % NX) * n
            piece = totals[k][:, at : at + n]
            t = piece if t is None else t + piece
        w = anchors[b][n : n + 16, :].astype(F32)
        w = jnp.concatenate([w[k : k + 1, :] for k in range(n // width)], axis=1)
        c = (1.0 / TEMPER) * w / t
        column = jnp.broadcast_to(c, (8, n)).T[:, :1]
        out_ref[b * n : (b + 1) * n, :] = (anchors[b][:n, :].astype(F32) * column).astype(BF)


def scale(anchors, totals, n):
    return vmem_call(
        scale_kernel,
        jax.ShapeDtypeStruct((NX * n, anchors[0].shape[1]), BF),
        "scale",
    )(*anchors, *totals)


def product(a_ref, parts):
    total = None
    for b, part in enumerate(parts):
        size = part.shape[2]
        term = jnp.dot(part[0], a_ref[b * size : (b + 1) * size, :], preferred_element_type=F32)
        total = term if total is None else total + term
    return total


def first_kernel(order_ref, a_ref, *refs):
    value = product(a_ref, refs[:NX]).astype(BF)
    for i in range(2):

        @pl.when(pl.program_id(0) == i)
        def _():
            refs[NX + i][...] = value


def rest_kernel(order_ref, a_ref, *refs):
    refs[NX][0] = product(a_ref, refs[:NX])


def mix(kernel, order, scaled, parts, out_shape, out_specs, name):
    n = parts[0].shape[1]
    return vmem_call(
        kernel,
        out_shape,
        name,
        grid_spec=pltpu.PrefetchScalarGridSpec(
            num_scalar_prefetch=1,
            grid=order.shape,
            in_specs=[pl.BlockSpec(scaled.shape, lambda i, order: (0, 0))]
            + [pl.BlockSpec((1, n, p.shape[2]), lambda i, order: (order[i], 0, 0)) for p in parts],
            out_specs=out_specs,
        ),
    )(order, scaled, *parts)


def mix_first(order, scaled, parts):
    n, width = parts[0].shape[1], scaled.shape[1]
    one = jax.ShapeDtypeStruct((n, width), BF)
    spec = pl.BlockSpec((n, width), lambda i, order: (0, 0))
    return mix(first_kernel, order, scaled, parts, (one, one), (spec, spec), "mix_first")


def mix_rest(order, scaled, parts):
    n, width = parts[0].shape[1], scaled.shape[1]
    shape = jax.ShapeDtypeStruct(order.shape + (n, width), F32)
    spec = pl.BlockSpec((1, n, width), lambda i, order: (i, 0, 0))
    return mix(rest_kernel, order, scaled, parts, shape, spec, "mix_rest")


def finish_kernel(
    up_ref, down_ref, own_ref, anchors_ref, w_ref, unit_ref, inv_ref, feats_ref, grad_ref, part_ref
):
    n = up_ref.shape[0]
    unit = unit_ref[...]
    mixed = own_ref[0] + up_ref[...].astype(F32) + down_ref[...].astype(F32)
    grad = mixed - (1.0 / TEMPER) * w_ref[...] * anchors_ref[:n, :].astype(F32)
    along = jnp.sum(unit * grad, axis=1, keepdims=True)
    grad = ((grad - unit * along) * inv_ref[...]).astype(BF)
    grad_ref[...] = grad
    part_ref[...] = jnp.dot(feats_ref[...], grad, preferred_element_type=F32)


def finish(up, down, rest, anchors, w, unit, inv, feats_t):
    n, width = up.shape
    whole = lambda v: pl.BlockSpec(v.shape, lambda i: (0,) * v.ndim)
    last = rest.shape[0] - 1
    depth = feats_t.shape[0]
    return vmem_call(
        finish_kernel,
        (jax.ShapeDtypeStruct((n, width), BF), jax.ShapeDtypeStruct((depth, width), F32)),
        "finish",
        grid=(1,),
        in_specs=[
            whole(up),
            whole(down),
            pl.BlockSpec((1, n, width), lambda i: (last, 0, 0)),
            whole(anchors),
            whole(w),
            whole(unit),
            whole(inv),
            whole(feats_t),
        ],
        out_specs=(
            pl.BlockSpec((n, width), lambda i: (0, 0)),
            pl.BlockSpec((depth, width), lambda i: (0, 0)),
        ),
    )(up, down, rest, anchors, w, unit, inv, feats_t)


def block_of(v, index, rows):
    return lax.dynamic_slice(v, (index * rows, 0), (rows, v.shape[1]))


def sum_everywhere(v):
    width = v.shape[1]
    core = lax.axis_index("core")
    rows = v.shape[0] // NC
    v = block_of(v, core, rows) + lax.ppermute(block_of(v, 1 - core, rows), "core", flip(NC, 1))
    many = NY * NX
    v = lax.all_to_all(v, ("y", "x"), 0, 0, tiled=True)
    v = jnp.sum(v.reshape(many, rows // many, width), axis=0)
    got = [lax.ppermute(v, "z", flip(NZ, m)) for m in (1, 2, 3)]
    v = (v + got[0]) + (got[1] + got[2])
    v = v + lax.ppermute(v, "z", flip(NZ, 4))
    v = lax.optimization_barrier(jnp.broadcast_to(v[None], (many,) + v.shape))
    v = lax.all_to_all(v.reshape(rows, width), ("y", "x"), 0, 0, tiled=True)
    other = lax.ppermute(v, "core", flip(NC, 1))
    return jnp.where(
        core == 0, jnp.concatenate([v, other], axis=0), jnp.concatenate([other, v], axis=0)
    )


def local(features, weight, support_queue, owner_shard, slot_row, loss_weight):
    n = features.shape[0]
    width = weight.shape[1]
    z = lax.axis_index("z")

    wanted, places = plan(owner_shard, slot_row[:, None])
    asked = lax.all_to_all(wanted, QUEUE, split_axis=0, concat_axis=0, tiled=True)

    projected = jnp.dot(features, weight, preferred_element_type=F32)
    inv_norm = lax.rsqrt(jnp.sum(projected * projected, axis=1, keepdims=True) + EPSILON)
    unit_view = projected * inv_norm
    views = lax.all_gather(unit_view.astype(BF), "z", axis=0, tiled=False)
    feats_t = lax.optimization_barrier(features.T)

    picked = support_queue[asked]
    answered = lax.all_to_all(picked, QUEUE, split_axis=0, concat_axis=0, tiled=True)
    extra = jnp.zeros((16, width), BF).at[: n // width].set(loss_weight.reshape(n // width, width))
    message = pick(answered.reshape(NZ * NX * CAP, width), places, extra)

    blocks = [message] + [lax.ppermute(message, "x", shift(NX, k)) for k in (1, 2, 3)]
    parts, totals = {}, {}
    for b in (0, 1, 3, 2):
        parts[b], totals[b] = exps(blocks[b], views)
    parts = [parts[b] for b in range(NX)]
    total = jnp.concatenate([totals[b] for b in range(NX)], axis=1)
    everyone = [total] + [lax.ppermute(total, "x", shift(NX, k)) for k in (1, 2, 3)]
    scaled = scale(blocks, everyone, n)

    up, down = mix_first((z + jnp.array([4, 5], jnp.int32)) % NZ, scaled, parts)
    rest = mix_rest((z + jnp.array([3, 6, 2, 7, 1, 0], jnp.int32)) % NZ, scaled, parts)
    for k in range(3):
        up = lax.ppermute(up, "z", shift(NZ, 1)).astype(F32)
        up = (up + rest[2 * k]).astype(BF)
        if k < 2:
            down = lax.ppermute(down, "z", shift(NZ, -1)).astype(F32)
            down = (down + rest[2 * k + 1]).astype(BF)
    up = lax.ppermute(up, "z", shift(NZ, 1))
    down = lax.ppermute(down, "z", shift(NZ, -1))

    weights = loss_weight.astype(F32)[:, None]
    grad_proj, partial_weight = finish(
        up, down, rest, message, weights, unit_view, inv_norm, feats_t
    )
    grad_feats = jnp.dot(grad_proj, weight.T, preferred_element_type=F32).astype(BF)
    grad_weight = sum_everywhere(partial_weight)
    return (grad_feats, grad_weight)


def solution(mesh):
    mesh = Mesh(mesh.devices.reshape(NY, NC, NZ, NX), ("y", "core", "z", "x"))
    views = ("y", "core", "z", "x")
    in_specs = (
        P(views, None),
        P(),
        P(QUEUE, None),
        P(views, None),
        P(views),
        P(views),
    )
    out_specs = (P(views, None), P())
    return jax.shard_map(local, mesh=mesh, in_specs=in_specs, out_specs=out_specs, check_vma=False)
```

profile of v0, /device:TPU:1, one launch (start us, length us, event | category | flops | bytes accessed | tf_op | source)
XLA Modules:
  0.0 217.8 jit_solution(5995464206102716988)
XLA Ops:
  8.2 1.7 multiply_reduce_fusion
  12.1 20.3 %all_to_all.35 = s32[32,1,64]{2,1,0:T(1,128)S(1)} all-to-all(s32[32,1,64]{2,1,0:T(1,128)S(1)} %bitcast.55), channel_id=1, replica_groups=mesh['y'=4,'core'=2,'z'=8,'x'=4] {'z','x'}, dimensions={0} | all-to-all | bytes 16384 | tf_op jit(solution)/shard_map/all_to_all | solution.py:292
  32.4 11.3 %gather_fusion = bf16[2048,256]{1,0:T(8,128)(2,1)} fusion(bf16[8192,256]{1,0:T(8,128)(2,1)} %param.12, s32[2048]{0:T(1024)S(1)} %broadcast_clamp_fusion), kind=kCustom, calls=%fused_computation | custom fusion | bytes 2105344 | tf_op jit(solution)/shard_map/gather | solution.py:300
  43.7 3.9 %all-to-all-start.1 = ((bf16[32,64,256]{2,1,0:T(8,128)(2,1)}), bf16[32,64,256]{2,1,0:T(8,128)(2,1)S(1)}, u32[]{:S(2)}, u32[]{:S(2)}) async-start(bf16[32,64,256]{2,1,0:T(8,128)(2,1)} %bitcast.56), calls=%async_computation.1 | async-start | bytes 2097152 | tf_op jit(solution)/shard_map/all_to_all | solution.py:301
  47.7 27.0 %all-to-all-done.1 = bf16[32,64,256]{2,1,0:T(8,128)(2,1)S(1)} async-done(((bf16[32,64,256]{2,1,0:T(8,128)(2,1)}), bf16[32,64,256]{2,1,0:T(8,128)(2,1)S(1)}, u32[]{:S(2)}, u32[]{:S(2)}) %all-to-all-start.1) | async-done | bytes 1048608 | tf_op jit(solution)/shard_map/all_to_all | solution.py:301
  75.6 2.0 collective-permute-start
  77.6 3.0 %collective-permute-start.1 = (bf16[528,256]{1,0:T(8,128)(2,1)S(1)}, bf16[528,256]{1,0:T(8,128)(2,1)S(1)}, u32[]{:S(2)}, u32[]{:S(2)}) collective-permute-start(bf16[528,256]{1,0:T(8,128)(2,1)S(1)} %pick.1.a_ref.refs_0_.anchors_ref), channel_id=1, source_target_pairs={{0,2},{1,3},{2,0},{3,1},{4,6},{5,7},{6,4},{7,5},{8,10},{9,11},{10,... | collective-permute-start | bytes 811016 | tf_op jit(solution)/shard_map/ppermute | solution.py:305
  81.1 1.6 copy-done.1
  82.7 3.5 %exps.4 = (bf16[8,512,512]{2,1,0:T(8,128)(2,1)}, f32[1,512]{1,0:T(1,128)S(1)}) custom-call(bf16[528,256]{1,0:T(8,128)(2,1)S(1)} %pick.1.a_ref.refs_0_.anchors_ref, bf16[8,512,256]{2,1,0:T(8,128)(2,1)S(1)} %bitcast.49), custom_call_target="tpu_custom_call" | custom-call | tf_op jit(solution)/shard_map/exps/pallas_call | solution.py:127
  86.2 1.6 copy-done.2
  87.8 3.6 %exps.5 = (bf16[8,512,512]{2,1,0:T(8,128)(2,1)}, f32[1,512]{1,0:T(1,128)S(1)}) custom-call(bf16[528,256]{1,0:T(8,128)(2,1)S(1)} %collective-permute-done.a_ref.refs_1_, bf16[8,512,256]{2,1,0:T(8,128)(2,1)S(1)} %bitcast.50), custom_call_target="tpu_custom_call" | custom-call | tf_op jit(solution)/shard_map/exps/pallas_call | solution.py:127
  91.4 3.5 %exps.6 = (bf16[8,512,512]{2,1,0:T(8,128)(2,1)}, f32[1,512]{1,0:T(1,128)S(1)}) custom-call(bf16[528,256]{1,0:T(8,128)(2,1)S(1)} %collective-permute-done.1.a_ref.refs_2_, bf16[8,512,256]{2,1,0:T(8,128)(2,1)S(1)} %bitcast.51), custom_call_target="tpu_custom_call" | custom-call | tf_op jit(solution)/shard_map/exps/pallas_call | solution.py:127
  94.9 3.5 %exps.7 = (bf16[8,512,512]{2,1,0:T(8,128)(2,1)}, f32[1,512]{1,0:T(1,128)S(1)}) custom-call(bf16[528,256]{1,0:T(8,128)(2,1)S(1)} %collective-permute-done.2.a_ref.refs_3_, bf16[8,512,256]{2,1,0:T(8,128)(2,1)S(1)} %bitcast.52), custom_call_target="tpu_custom_call" | custom-call | tf_op jit(solution)/shard_map/exps/pallas_call | solution.py:127
  99.6 2.1 collective-permute-start.5
  104.0 3.5 %mix_first.1 = (bf16[512,256]{1,0:T(8,128)(2,1)S(1)}, bf16[512,256]{1,0:T(8,128)(2,1)S(1)}) custom-call(s32[2]{0:T(128)S(1)} %and_select_fusion.1.order_ref, bf16[2048,256]{1,0:T(8,128)(2,1)S(1)} %scale.1.a_ref, bf16[8,512,512]{2,1,0:T(8,128)(2,1)S(1)} %copy-done.4, bf16[8,512,512]{2,1,0:T(8,128)(2,1)} %get-tuple-element.35.refs_1_, ...), custom_call_target="tpu_custom_call" | custom-call | tf_op jit(solution)/shard_map/mix_first/pallas_call | solution.py:195
  107.4 1.5 collective-permute-start.6
  109.0 8.4 %mix_rest.1.own_ref = f32[6,512,256]{2,1,0:T(8,128)S(1)} custom-call(s32[6]{0:T(128)S(1)} %and_select_fusion.order_ref, bf16[2048,256]{1,0:T(8,128)(2,1)S(1)} %scale.1.a_ref, bf16[8,512,512]{2,1,0:T(8,128)(2,1)} %get-tuple-element.34.refs_0_, bf16[8,512,512]{2,1,0:T(8,128)(2,1)} %get-tuple-element.35.refs_1_, ...), custom_call_target="tpu_custom_call" | custom-call | tf_op jit(solution)/shard_map/mix_rest/pallas_call | solution.py:195
  119.1 3.6 %collective-permute-done.10 = bf16[512,256]{1,0:T(8,128)(2,1)S(1)} collective-permute-done((bf16[512,256]{1,0:T(8,128)(2,1)S(1)}, bf16[512,256]{1,0:T(8,128)(2,1)S(1)}, u32[]{:S(2)}, u32[]{:S(2)}) %collective-permute-start.10) | collective-permute-done | bytes 262176 | tf_op jit(solution)/shard_map/ppermute | solution.py:320
  122.7 2.8 %collective-permute-done.7 = bf16[512,256]{1,0:T(8,128)(2,1)S(1)} collective-permute-done((bf16[512,256]{1,0:T(8,128)(2,1)S(1)}, bf16[512,256]{1,0:T(8,128)(2,1)S(1)}, u32[]{:S(2)}, u32[]{:S(2)}) %collective-permute-start.7) | collective-permute-done | bytes 262176 | tf_op jit(solution)/shard_map/ppermute | solution.py:317
  127.1 4.1 %collective-permute-done.11 = bf16[512,256]{1,0:T(8,128)(2,1)S(1)} collective-permute-done((bf16[512,256]{1,0:T(8,128)(2,1)S(1)}, bf16[512,256]{1,0:T(8,128)(2,1)S(1)}, u32[]{:S(2)}, u32[]{:S(2)}) %collective-permute-start.11) | collective-permute-done | bytes 262176 | tf_op jit(solution)/shard_map/ppermute | solution.py:320
  131.2 3.2 %collective-permute-done.8 = bf16[512,256]{1,0:T(8,128)(2,1)S(1)} collective-permute-done((bf16[512,256]{1,0:T(8,128)(2,1)S(1)}, bf16[512,256]{1,0:T(8,128)(2,1)S(1)}, u32[]{:S(2)}, u32[]{:S(2)}) %collective-permute-start.8) | collective-permute-done | bytes 262176 | tf_op jit(solution)/shard_map/ppermute | solution.py:317
  136.7 1.5 copy.23
  138.5 4.9 %collective-permute-done.12.down_ref = bf16[512,256]{1,0:T(8,128)(2,1)S(1)} collective-permute-done((bf16[512,256]{1,0:T(8,128)(2,1)}, bf16[512,256]{1,0:T(8,128)(2,1)S(1)}, u32[]{:S(2)}, u32[]{:S(2)}) %collective-permute-start.12) | collective-permute-done | bytes 262176 | tf_op jit(solution)/shard_map/ppermute | solution.py:323
  146.1 1.8 finish.1
  148.9 9.2 %collective-permute-start.13 = (f32[512,256]{1,0:T(8,128)S(1)}, f32[512,256]{1,0:T(8,128)S(1)}, u32[]{:S(2)}, u32[]{:S(2)}) collective-permute-start(f32[512,256]{1,0:T(8,128)S(1)} %constant_dynamic-slice_fusion), channel_id=1, source_target_pairs={{0,32},{32,0},{1,33},{33,1},{2,34},{34,2},{3,35},{35,3},{4,36},{36... | collective-permute-start | bytes 1572872 | tf_op jit(solution)/shard_map/ppermute | solution.py:271
  158.1 1.5 collective-permute-done.13
  160.8 18.0 %all_to_all.36 = f32[16,32,256]{2,1,0:T(8,128)S(1)} all-to-all(f32[16,32,256]{2,1,0:T(8,128)S(1)} %bitcast.59), channel_id=1, replica_groups=mesh['y'=4,'core'=2,'z'=8,'x'=4] {'y','x'}, dimensions={0} | all-to-all | bytes 1048576 | tf_op jit(solution)/shard_map/all_to_all | solution.py:273
  179.2 3.2 %collective-permute-start.16 = (f32[32,256]{1,0:T(8,128)S(1)}, f32[32,256]{1,0:T(8,128)S(1)}, u32[]{:S(2)}, u32[]{:S(2)}) collective-permute-start(f32[32,256]{1,0:T(8,128)S(1)} %reduce_sum.19), channel_id=1, source_target_pairs={{0,12},{4,8},{8,4},{12,0},{16,28},{20,24},{24,20},{28,16},{1,13},{... | collective-permute-start | bytes 98312 | tf_op jit(solution)/shard_map/ppermute | solution.py:275
  184.2 2.8 %collective-permute-start.17 = (f32[32,256]{1,0:T(8,128)S(1)}, f32[32,256]{1,0:T(8,128)S(1)}, u32[]{:S(2)}, u32[]{:S(2)}) collective-permute-start(f32[32,256]{1,0:T(8,128)S(1)} %add_add_fusion), channel_id=1, source_target_pairs={{0,16},{4,20},{8,24},{12,28},{16,0},{20,4},{24,8},{28,12},{1,17},{... | collective-permute-start | bytes 98312 | tf_op jit(solution)/shard_map/ppermute | solution.py:277
  187.0 4.4 %collective-permute-done.17 = f32[32,256]{1,0:T(8,128)S(1)} collective-permute-done((f32[32,256]{1,0:T(8,128)S(1)}, f32[32,256]{1,0:T(8,128)S(1)}, u32[]{:S(2)}, u32[]{:S(2)}) %collective-permute-start.17) | collective-permute-done | bytes 32800 | tf_op jit(solution)/shard_map/ppermute | solution.py:277
  191.4 11.9 %all_to_all.37 = f32[16,32,256]{2,1,0:T(8,128)S(1)} all-to-all(f32[16,32,256]{2,1,0:T(8,128)S(1)} %broadcast_in_dim.20), channel_id=1, replica_groups=mesh['y'=4,'core'=2,'z'=8,'x'=4] {'y','x'}, dimensions={0} | all-to-all | bytes 1048576 | tf_op jit(solution)/shard_map/all_to_all | solution.py:279
  203.2 5.1 %collective-permute-start.18 = (f32[512,256]{1,0:T(8,128)S(1)}, f32[512,256]{1,0:T(8,128)S(1)}, u32[]{:S(2)}, u32[]{:S(2)}) collective-permute-start(f32[512,256]{1,0:T(8,128)S(1)} %bitcast.57), channel_id=1, source_target_pairs={{0,32},{32,0},{1,33},{33,1},{2,34},{34,2},{3,35},{35,3},{4,36},{36... | collective-permute-start | bytes 1572872 | tf_op jit(solution)/shard_map/ppermute | solution.py:280
  (83 shorter events, 23.9 us)
Async XLA Ops:
  7.2 1.0 copy-start
  7.2 3.8 %copy-start.9 = (s32[512,1]{0,1:T(1,128)S(1)}, s32[512,1]{0,1:T(1,128)}, u32[]{:S(2)}) copy-start(s32[512,1]{0,1:T(1,128)} %param.13) | copy-start | bytes 6148
  7.2 4.0 %copy-start.10 = (s32[512]{0:T(512)S(1)}, s32[512]{0:T(512)}, u32[]{:S(2)}) copy-start(s32[512]{0:T(512)} %param.14) | copy-start | bytes 6148
  7.2 73.9 %all-gather.3.cloned.1.call-start = ((), (), s32[]{:S(2)}) async-start(), calls=%async_computation.4 | async-start | bytes 2359296 | tf_op jit(solution)/shard_map/all_gather | solution.py:297
  32.4 15.2 %copy-start.8 = (bf16[512]{0:T(512)(128)(2,1)S(1)}, bf16[512]{0:T(512)(128)(2,1)}, u32[]{:S(2)}) copy-start(bf16[512]{0:T(512)(128)(2,1)} %param.15) | copy-start | bytes 3076
  43.7 31.0 %all-to-all-start.1 = ((bf16[32,64,256]{2,1,0:T(8,128)(2,1)}), bf16[32,64,256]{2,1,0:T(8,128)(2,1)S(1)}, u32[]{:S(2)}, u32[]{:S(2)}) async-start(bf16[32,64,256]{2,1,0:T(8,128)(2,1)} %bitcast.56), calls=%async_computation.1 | async-start | bytes 2097152 | tf_op jit(solution)/shard_map/all_to_all | solution.py:301
  75.6 10.6 %collective-permute-start = (bf16[528,256]{1,0:T(8,128)(2,1)S(1)}, bf16[528,256]{1,0:T(8,128)(2,1)S(1)}, u32[]{:S(2)}, u32[]{:S(2)}) collective-permute-start(bf16[528,256]{1,0:T(8,128)(2,1)S(1)} %pick.1.a_ref.refs_0_.anchors_ref), channel_id=1, source_target_pairs={{0,1},{1,2},{2,3},{3,0},{4,5},{5,6},{6,7},{7,4},{8,9},{9,10},{10,1... | collective-permute-start | bytes 811016 | tf_op jit(solution)/shard_map/ppermute | solution.py:305
  77.6 13.8 %collective-permute-start.1 = (bf16[528,256]{1,0:T(8,128)(2,1)S(1)}, bf16[528,256]{1,0:T(8,128)(2,1)S(1)}, u32[]{:S(2)}, u32[]{:S(2)}) collective-permute-start(bf16[528,256]{1,0:T(8,128)(2,1)S(1)} %pick.1.a_ref.refs_0_.anchors_ref), channel_id=1, source_target_pairs={{0,2},{1,3},{2,0},{3,1},{4,6},{5,7},{6,4},{7,5},{8,10},{9,11},{10,... | collective-permute-start | bytes 811016 | tf_op jit(solution)/shard_map/ppermute | solution.py:305
  80.5 14.3 %collective-permute-start.2 = (bf16[528,256]{1,0:T(8,128)(2,1)S(1)}, bf16[528,256]{1,0:T(8,128)(2,1)S(1)}, u32[]{:S(2)}, u32[]{:S(2)}) collective-permute-start(bf16[528,256]{1,0:T(8,128)(2,1)S(1)} %pick.1.a_ref.refs_0_.anchors_ref), channel_id=1, source_target_pairs={{0,3},{1,0},{2,1},{3,2},{4,7},{5,4},{6,5},{7,6},{8,11},{9,8},{10,9... | collective-permute-start | bytes 811016 | tf_op jit(solution)/shard_map/ppermute | solution.py:305
  81.1 1.6 copy-start.1
  82.7 18.9 %copy-start.12 = (s32[2]{0:T(128)S(1)}, s32[2]{0:T(128)}, u32[]{:S(2)}) copy-start(s32[2]{0:T(128)} %constant.81.clone) | copy-start | bytes 28
  86.2 1.6 copy-start.2
  87.8 16.1 %copy-start.4 = (bf16[8,512,512]{2,1,0:T(8,128)(2,1)S(1)}, bf16[8,512,512]{2,1,0:T(8,128)(2,1)}, u32[]{:S(2)}) copy-start(bf16[8,512,512]{2,1,0:T(8,128)(2,1)} %get-tuple-element.34.refs_0_) | copy-start | bytes 12582916
  98.4 3.7 %collective-permute-start.3 = (f32[1,2048]{1,0:T(1,128)S(1)}, f32[1,2048]{1,0:T(1,128)S(1)}, u32[]{:S(2)}, u32[]{:S(2)}) collective-permute-start(f32[1,2048]{1,0:T(1,128)S(1)} %constant_dynamic-update-slice_fusion.refs_4_), channel_id=1, source_target_pairs={{0,1},{1,2},{2,3},{3,0},{4,5},{5,6},{6,7},{7,4},{8,9},{9,10},{10,1... | collective-permute-start | bytes 24584 | tf_op jit(solution)/shard_map/ppermute | solution.py:311
  99.3 4.0 %collective-permute-start.4 = (f32[1,2048]{1,0:T(1,128)S(1)}, f32[1,2048]{1,0:T(1,128)S(1)}, u32[]{:S(2)}, u32[]{:S(2)}) collective-permute-start(f32[1,2048]{1,0:T(1,128)S(1)} %constant_dynamic-update-slice_fusion.refs_4_), channel_id=1, source_target_pairs={{0,2},{1,3},{2,0},{3,1},{4,6},{5,7},{6,4},{7,5},{8,10},{9,11},{10,... | collective-permute-start | bytes 24584 | tf_op jit(solution)/shard_map/ppermute | solution.py:311
  99.6 3.7 %collective-permute-start.5 = (f32[1,2048]{1,0:T(1,128)S(1)}, f32[1,2048]{1,0:T(1,128)S(1)}, u32[]{:S(2)}, u32[]{:S(2)}) collective-permute-start(f32[1,2048]{1,0:T(1,128)S(1)} %constant_dynamic-update-slice_fusion.refs_4_), channel_id=1, source_target_pairs={{0,3},{1,0},{2,1},{3,2},{4,7},{5,4},{6,5},{7,6},{8,11},{9,8},{10,9... | collective-permute-start | bytes 24584 | tf_op jit(solution)/shard_map/ppermute | solution.py:311
  104.0 5.0 %copy-start.11 = (s32[6]{0:T(128)S(1)}, s32[6]{0:T(128)}, u32[]{:S(2)}) copy-start(s32[6]{0:T(128)} %constant.82.clone) | copy-start | bytes 76
  107.4 11.4 %collective-permute-start.6 = (bf16[512,256]{1,0:T(8,128)(2,1)S(1)}, bf16[512,256]{1,0:T(8,128)(2,1)S(1)}, u32[]{:S(2)}, u32[]{:S(2)}) collective-permute-start(bf16[512,256]{1,0:T(8,128)(2,1)S(1)} %get-tuple-element.38), channel_id=1, source_target_pairs={{0,4},{4,8},{8,12},{12,16},{16,20},{20,24},{24,28},{28,0},{1,5},{5... | collective-permute-start | bytes 786440 | tf_op jit(solution)/shard_map/ppermute | solution.py:317
  117.4 17.0 %copy-start.3 = (f32[6,512,256]{2,1,0:T(8,128)}, f32[6,512,256]{2,1,0:T(8,128)S(1)}, u32[]{:S(2)}) copy-start(f32[6,512,256]{2,1,0:T(8,128)S(1)} %mix_rest.1.own_ref) | copy-start | bytes 9437188
  117.4 5.3 %collective-permute-start.10 = (bf16[512,256]{1,0:T(8,128)(2,1)S(1)}, bf16[512,256]{1,0:T(8,128)(2,1)S(1)}, u32[]{:S(2)}, u32[]{:S(2)}) collective-permute-start(bf16[512,256]{1,0:T(8,128)(2,1)S(1)} %get-tuple-element.39), channel_id=1, source_target_pairs={{0,28},{4,0},{8,4},{12,8},{16,12},{20,16},{24,20},{28,24},{1,29},{... | collective-permute-start | bytes 786440 | tf_op jit(solution)/shard_map/ppermute | solution.py:320
  118.9 6.5 %collective-permute-start.7 = (bf16[512,256]{1,0:T(8,128)(2,1)S(1)}, bf16[512,256]{1,0:T(8,128)(2,1)S(1)}, u32[]{:S(2)}, u32[]{:S(2)}) collective-permute-start(bf16[512,256]{1,0:T(8,128)(2,1)S(1)} %fusion.9), channel_id=1, source_target_pairs={{0,4},{4,8},{8,12},{12,16},{16,20},{20,24},{24,28},{28,0},{1,5},{5... | collective-permute-start | bytes 786440 | tf_op jit(solution)/shard_map/ppermute | solution.py:317
  125.6 5.6 %collective-permute-start.11 = (bf16[512,256]{1,0:T(8,128)(2,1)S(1)}, bf16[512,256]{1,0:T(8,128)(2,1)S(1)}, u32[]{:S(2)}, u32[]{:S(2)}) collective-permute-start(bf16[512,256]{1,0:T(8,128)(2,1)S(1)} %get-tuple-element.46), channel_id=1, source_target_pairs={{0,28},{4,0},{8,4},{12,8},{16,12},{20,16},{24,20},{28,24},{1,29},{... | collective-permute-start | bytes 786440 | tf_op jit(solution)/shard_map/ppermute | solution.py:320
  125.7 8.7 %collective-permute-start.8 = (bf16[512,256]{1,0:T(8,128)(2,1)S(1)}, bf16[512,256]{1,0:T(8,128)(2,1)S(1)}, u32[]{:S(2)}, u32[]{:S(2)}) collective-permute-start(bf16[512,256]{1,0:T(8,128)(2,1)S(1)} %get-tuple-element.47), channel_id=1, source_target_pairs={{0,4},{4,8},{8,12},{12,16},{16,20},{20,24},{24,28},{28,0},{1,5},{5... | collective-permute-start | bytes 786440 | tf_op jit(solution)/shard_map/ppermute | solution.py:317
  135.3 8.2 %collective-permute-start.12 = (bf16[512,256]{1,0:T(8,128)(2,1)}, bf16[512,256]{1,0:T(8,128)(2,1)S(1)}, u32[]{:S(2)}, u32[]{:S(2)}) collective-permute-start(bf16[512,256]{1,0:T(8,128)(2,1)} %get-tuple-element.44), channel_id=1, source_target_pairs={{0,28},{4,0},{8,4},{12,8},{16,12},{20,16},{24,20},{28,24},{1,29},{... | collective-permute-start | bytes 786440 | tf_op jit(solution)/shard_map/ppermute | solution.py:323
  135.3 9.2 %collective-permute-start.9 = (bf16[512,256]{1,0:T(8,128)(2,1)}, bf16[512,256]{1,0:T(8,128)(2,1)S(1)}, u32[]{:S(2)}, u32[]{:S(2)}) collective-permute-start(bf16[512,256]{1,0:T(8,128)(2,1)} %get-tuple-element.45), channel_id=1, source_target_pairs={{0,4},{4,8},{8,12},{12,16},{16,20},{20,24},{24,28},{28,0},{1,5},{5... | collective-permute-start | bytes 786440 | tf_op jit(solution)/shard_map/ppermute | solution.py:322
  147.9 1.0 copy-start.5
  148.9 10.7 %collective-permute-start.13 = (f32[512,256]{1,0:T(8,128)S(1)}, f32[512,256]{1,0:T(8,128)S(1)}, u32[]{:S(2)}, u32[]{:S(2)}) collective-permute-start(f32[512,256]{1,0:T(8,128)S(1)} %constant_dynamic-slice_fusion), channel_id=1, source_target_pairs={{0,32},{32,0},{1,33},{33,1},{2,34},{34,2},{3,35},{35,3},{4,36},{36... | collective-permute-start | bytes 1572872 | tf_op jit(solution)/shard_map/ppermute | solution.py:271
  178.8 3.6 %collective-permute-start.14 = (f32[32,256]{1,0:T(8,128)S(1)}, f32[32,256]{1,0:T(8,128)S(1)}, u32[]{:S(2)}, u32[]{:S(2)}) collective-permute-start(f32[32,256]{1,0:T(8,128)S(1)} %reduce_sum.19), channel_id=1, source_target_pairs={{0,4},{4,0},{8,12},{12,8},{16,20},{20,16},{24,28},{28,24},{1,5},{5... | collective-permute-start | bytes 98312 | tf_op jit(solution)/shard_map/ppermute | solution.py:275
  179.1 3.7 %collective-permute-start.15 = (f32[32,256]{1,0:T(8,128)S(1)}, f32[32,256]{1,0:T(8,128)S(1)}, u32[]{:S(2)}, u32[]{:S(2)}) collective-permute-start(f32[32,256]{1,0:T(8,128)S(1)} %reduce_sum.19), channel_id=1, source_target_pairs={{0,8},{4,12},{8,0},{12,4},{16,24},{20,28},{24,16},{28,20},{1,9},{5... | collective-permute-start | bytes 98312 | tf_op jit(solution)/shard_map/ppermute | solution.py:275
  179.2 5.0 %collective-permute-start.16 = (f32[32,256]{1,0:T(8,128)S(1)}, f32[32,256]{1,0:T(8,128)S(1)}, u32[]{:S(2)}, u32[]{:S(2)}) collective-permute-start(f32[32,256]{1,0:T(8,128)S(1)} %reduce_sum.19), channel_id=1, source_target_pairs={{0,12},{4,8},{8,4},{12,0},{16,28},{20,24},{24,20},{28,16},{1,13},{... | collective-permute-start | bytes 98312 | tf_op jit(solution)/shard_map/ppermute | solution.py:275
  184.2 7.1 %collective-permute-start.17 = (f32[32,256]{1,0:T(8,128)S(1)}, f32[32,256]{1,0:T(8,128)S(1)}, u32[]{:S(2)}, u32[]{:S(2)}) collective-permute-start(f32[32,256]{1,0:T(8,128)S(1)} %add_add_fusion), channel_id=1, source_target_pairs={{0,16},{4,20},{8,24},{12,28},{16,0},{20,4},{24,8},{28,12},{1,17},{... | collective-permute-start | bytes 98312 | tf_op jit(solution)/shard_map/ppermute | solution.py:277
  203.2 6.6 %collective-permute-start.18 = (f32[512,256]{1,0:T(8,128)S(1)}, f32[512,256]{1,0:T(8,128)S(1)}, u32[]{:S(2)}, u32[]{:S(2)}) collective-permute-start(f32[512,256]{1,0:T(8,128)S(1)} %bitcast.57), channel_id=1, source_target_pairs={{0,32},{32,0},{1,33},{33,1},{2,34},{34,2},{3,35},{35,3},{4,36},{36... | collective-permute-start | bytes 1572872 | tf_op jit(solution)/shard_map/ppermute | solution.py:280
  (2 other events, 1.7 us)
Sparse Core Ops, SparseCore 0:
  11.1 42.9 all-gather.2
where the time goes:
time: 218 us
  waiting for transfers between devices  55.9 us (26%)
  blocking collectives  50.1 us (23%)
  starting transfers between devices  39.6 us (18%)
  Pallas kernels  29.9 us (14%)
  local copies, waits for them, and re-layouts  20.6 us (9%)
  between operations  14.3 us (7%)
  other arithmetic  4.17 us (2%)
  matrix products  3.18 us (1%)
    all_to_all x1, waiting for transfers between devices, local(): lax.all_to_all(picked, QUEUE, split_axis=0, concat_axis=0, tiled=True)  27 us
    all_to_all x1, blocking collectives, local(): lax.all_to_all(wanted, QUEUE, split_axis=0, concat_axis=0, tiled=True)  20.3 us
    all_to_all x1, blocking collectives, sum_everywhere(): v = lax.all_to_all(v, ('y', 'x'), 0, 0, tiled=True)  18 us
    pallas_call x4, Pallas kernels, exps(): vmem_call(exps_kernel, (jax.ShapeDtypeStruct((many, n, n), BF), jax.Shape...  14 us
    pallas_call x2, Pallas kernels, mix(): vmem_call(kernel, out_shape, name, grid_spec=pltpu.PrefetchScalarGridSpec...  11.9 us
    all_to_all x1, blocking collectives, sum_everywhere(): v = lax.all_to_all(v.reshape(rows, width), ('y', 'x'), 0, 0, tiled=True)  11.9 us
    gather x1, local copies, waits for them, and re-layouts, local(): picked = support_queue[asked]  11.3 us
    ppermute x1, starting transfers between devices, sum_everywhere(): lax.ppermute(block_of(v, 1 - core, rows), 'core', flip(NC, 1))  9.19 us
  transfers between devices with their start and end apart: 21, of which 14 were waited for; matrix products, arithmetic and copies ran while one was open for 7% of the time, Pallas kernels for 9%

commit v1 on v0

v1 whole, which is shorter than its diff:
```python
import functools
import math

import jax
import jax.numpy as jnp
from jax import lax
from jax.experimental import pallas as pl
from jax.experimental.pallas import tpu as pltpu
from jax.sharding import Mesh
from jax.sharding import PartitionSpec as P

TEMPER = 0.1
EPSILON = 1e-06
NZ, NX, NY, NC = 8, 4, 4, 2
CAP = 64
BF = jnp.bfloat16
F32 = jnp.float32
VMEM_LIMIT = 16 * 1024 * 1024
IN_VMEM = pl.BlockSpec(memory_space=pltpu.VMEM)
EXPONENT = math.log2(math.e) / TEMPER
QUEUE = ("z", "x")


def shift(size, by):
    return [(i, (i + by) % size) for i in range(size)]


def flip(size, mask):
    return [(i, i ^ mask) for i in range(size)]


def vmem_call(kernel, out_shape, name, limit=VMEM_LIMIT, **kw):
    return pl.pallas_call(
        kernel,
        out_shape=out_shape,
        compiler_params=pltpu.CompilerParams(vmem_limit_bytes=limit),
        name=name,
        **kw,
    )


def begin_kernel(
    feats_ref, weight_ref, owner_ref, slot_ref, unit_ref, inv_ref, view_ref, wanted_ref, places_ref
):
    n = feats_ref.shape[0]
    shards = wanted_ref.shape[0]
    owner = owner_ref[...]
    slot = slot_ref[...]
    onehot = jnp.where(owner == lax.broadcasted_iota(jnp.int32, (shards, n), 0), 1.0, 0.0)
    above = lax.broadcasted_iota(jnp.int32, (n, n), 0) < lax.broadcasted_iota(jnp.int32, (n, n), 1)
    above = jnp.where(above, 1.0, 0.0).astype(BF)
    before = jnp.dot(onehot.astype(BF), above, preferred_element_type=F32)
    rank = jnp.sum(before * onehot, axis=0, keepdims=True).astype(jnp.int32)
    chosen = jnp.where(rank == lax.broadcasted_iota(jnp.int32, (128, n), 0), 1.0, 0.0).astype(BF)
    both = (((1,), (1,)), ((), ()))
    high = (onehot * (slot >> 7).astype(F32)).astype(BF)
    low = (onehot * (slot & 127).astype(F32)).astype(BF)
    upper = lax.dot_general(high, chosen, both, preferred_element_type=F32)
    lower = lax.dot_general(low, chosen, both, preferred_element_type=F32)
    full = upper.astype(jnp.int32) * 128 + lower.astype(jnp.int32)
    wanted_ref[...] = full[:, :CAP]
    places_ref[...] = jnp.broadcast_to(owner * CAP + rank, (8, n)).T[:, :1]

    projected = jnp.dot(feats_ref[...], weight_ref[...], preferred_element_type=F32)
    inv = lax.rsqrt(jnp.sum(projected * projected, axis=1, keepdims=True) + EPSILON)
    unit = projected * inv
    inv_ref[...] = inv
    unit_ref[...] = unit
    view_ref[...] = unit.astype(BF)


def begin(features, weight, owner, slot):
    n, width = features.shape[0], weight.shape[1]
    return vmem_call(
        begin_kernel,
        (
            jax.ShapeDtypeStruct((n, width), F32),
            jax.ShapeDtypeStruct((n, 1), F32),
            jax.ShapeDtypeStruct((n, width), BF),
            jax.ShapeDtypeStruct((NZ * NX, CAP), jnp.int32),
            jax.ShapeDtypeStruct((n, 1), jnp.int32),
        ),
        "begin",
    )(features, weight, owner, slot)


def pick_kernel(rows_ref, places_ref, extra_ref, out_ref):
    n = places_ref.shape[0]
    places = places_ref[...]
    column = lax.broadcasted_iota(jnp.int32, (n, n), 1)
    total = None
    for at in range(0, rows_ref.shape[0], n):
        onehot = jnp.where(places == column + at, 1.0, 0.0).astype(BF)
        term = jnp.dot(onehot, rows_ref[at : at + n, :], preferred_element_type=F32)
        total = term if total is None else total + term
    unit = total * lax.rsqrt(jnp.sum(total * total, axis=1, keepdims=True) + EPSILON)
    out_ref[:n, :] = unit.astype(BF)
    out_ref[n:, :] = extra_ref[...]


def pick(rows, places, extra):
    n = places.shape[0]
    return vmem_call(
        pick_kernel, jax.ShapeDtypeStruct((n + extra.shape[0], rows.shape[1]), BF), "pick"
    )(rows, places, extra)


def exps_kernel(a_ref, *refs):
    views, (e_ref, t_ref) = refs[:NZ], refs[NZ:]
    n = t_ref.shape[1]
    a = a_ref[:n, :]
    total = jnp.zeros((8, n), F32)
    for k in range(NZ):
        dots = lax.dot_general(
            views[k][...], a, (((1,), (1,)), ((), ())), preferred_element_type=F32
        )
        e = jnp.exp2(dots * EXPONENT)
        total = total + jnp.sum(e.reshape(n // 8, 8, n), axis=0)
        e_ref[k] = e.astype(BF)
    t_ref[...] = jnp.sum(total, axis=0, keepdims=True)


def exps(anchors, views):
    n = views[0].shape[0]
    return vmem_call(
        exps_kernel,
        (jax.ShapeDtypeStruct((NZ, n, n), BF), jax.ShapeDtypeStruct((1, n), F32)),
        "exps",
        in_specs=[IN_VMEM] * (1 + NZ),
        out_specs=(IN_VMEM, IN_VMEM),
    )(anchors, *views)


def scale_kernel(*refs):
    anchors = refs[:NX]
    totals = refs[NX : 2 * NX]
    out_ref = refs[2 * NX]
    n = out_ref.shape[0] // NX
    width = out_ref.shape[1]
    for b in range(NX):
        t = None
        for k in range(NX):
            at = ((b - k) % NX) * n
            piece = totals[k][:, at : at + n]
            t = piece if t is None else t + piece
        w = anchors[b][n : n + 16, :].astype(F32)
        w = jnp.concatenate([w[k : k + 1, :] for k in range(n // width)], axis=1)
        c = (1.0 / TEMPER) * w / t
        column = jnp.broadcast_to(c, (8, n)).T[:, :1]
        out_ref[b * n : (b + 1) * n, :] = (anchors[b][:n, :].astype(F32) * column).astype(BF)


def scale(anchors, totals, n):
    return vmem_call(
        scale_kernel,
        jax.ShapeDtypeStruct((NX * n, anchors[0].shape[1]), BF),
        "scale",
    )(*anchors, *totals)


def mix_kernel(which, a_ref, *refs):
    parts, outs = refs[:NX], refs[NX:]
    for k, out in zip(which, outs):
        total = None
        for b, part in enumerate(parts):
            size = part.shape[2]
            term = jnp.dot(part[k], a_ref[b * size : (b + 1) * size, :], preferred_element_type=F32)
            total = term if total is None else total + term
        out[...] = total.astype(out.dtype)


def mix(which, scaled, parts, dtype):
    shape = jax.ShapeDtypeStruct((parts[0].shape[1], scaled.shape[1]), dtype)
    return vmem_call(
        functools.partial(mix_kernel, which),
        tuple(shape for _ in which),
        "mix",
        in_specs=[IN_VMEM] * (1 + NX),
        out_specs=tuple(IN_VMEM for _ in which),
    )(scaled, *parts)


def finish_kernel(
    up_ref, down_ref, own_ref, anchors_ref, w_ref, unit_ref, inv_ref, feats_ref, grad_ref, part_ref
):
    n = up_ref.shape[0]
    unit = unit_ref[...]
    mixed = own_ref[...] + up_ref[...].astype(F32) + down_ref[...].astype(F32)
    grad = mixed - (1.0 / TEMPER) * w_ref[...] * anchors_ref[:n, :].astype(F32)
    along = jnp.sum(unit * grad, axis=1, keepdims=True)
    grad = ((grad - unit * along) * inv_ref[...]).astype(BF)
    grad_ref[...] = grad
    part_ref[...] = jnp.dot(feats_ref[...], grad, preferred_element_type=F32)


def finish(up, down, own, anchors, w, unit, inv, feats_t):
    n, width = up.shape
    return vmem_call(
        finish_kernel,
        (
            jax.ShapeDtypeStruct((n, width), BF),
            jax.ShapeDtypeStruct((feats_t.shape[0], width), F32),
        ),
        "finish",
    )(up, down, own, anchors, w, unit, inv, feats_t)


def block_of(v, index, rows):
    return lax.dynamic_slice(v, (index * rows, 0), (rows, v.shape[1]))


def sum_everywhere(v):
    width = v.shape[1]
    core = lax.axis_index("core")
    rows = v.shape[0] // NC
    v = block_of(v, core, rows) + lax.ppermute(block_of(v, 1 - core, rows), "core", flip(NC, 1))
    many = NY * NX
    v = lax.all_to_all(v, ("y", "x"), 0, 0, tiled=True)
    v = jnp.sum(v.reshape(many, rows // many, width), axis=0)
    got = [lax.ppermute(v, "z", flip(NZ, m)) for m in (1, 2, 3)]
    v = (v + got[0]) + (got[1] + got[2])
    v = v + lax.ppermute(v, "z", flip(NZ, 4))
    v = lax.optimization_barrier(jnp.broadcast_to(v[None], (many,) + v.shape))
    v = lax.all_to_all(v.reshape(rows, width), ("y", "x"), 0, 0, tiled=True)
    other = lax.ppermute(v, "core", flip(NC, 1))
    return jnp.where(
        core == 0, jnp.concatenate([v, other], axis=0), jnp.concatenate([other, v], axis=0)
    )


def local(features, weight, support_queue, owner_shard, slot_row, loss_weight):
    n = features.shape[0]
    width = weight.shape[1]

    unit_view, inv_norm, view_bf, wanted, places = begin(
        features, weight, owner_shard.reshape(1, n), slot_row.reshape(1, n)
    )
    views = {0: view_bf}
    views[7] = lax.ppermute(view_bf, "z", shift(NZ, 1))
    views[1] = lax.ppermute(view_bf, "z", shift(NZ, -1))
    asked = lax.all_to_all(wanted, QUEUE, split_axis=0, concat_axis=0, tiled=True)
    asked, views[7], views[1] = lax.optimization_barrier((asked, views[7], views[1]))
    views[6] = lax.ppermute(views[7], "z", shift(NZ, 1))
    views[2] = lax.ppermute(views[1], "z", shift(NZ, -1))
    picked = support_queue[asked]
    picked, views[6], views[2] = lax.optimization_barrier((picked, views[6], views[2]))
    views[5] = lax.ppermute(views[6], "z", shift(NZ, 1))
    views[3] = lax.ppermute(views[2], "z", shift(NZ, -1))
    views[4] = lax.ppermute(views[5], "z", shift(NZ, 1))
    views = [views[d] for d in range(NZ)]
    feats_t = lax.optimization_barrier(features.T)

    answered = lax.all_to_all(picked, QUEUE, split_axis=0, concat_axis=0, tiled=True)
    extra = jnp.zeros((16, width), BF).at[: n // width].set(loss_weight.reshape(n // width, width))
    message = pick(answered.reshape(NZ * NX * CAP, width), places, extra)

    blocks = [message] + [lax.ppermute(message, "x", shift(NX, k)) for k in (1, 2, 3)]
    parts, totals = {}, {}
    for b in (0, 1, 3, 2):
        parts[b], totals[b] = exps(blocks[b], views)
    parts = [parts[b] for b in range(NX)]
    total = jnp.concatenate([totals[b] for b in range(NX)], axis=1)
    everyone = [total] + [lax.ppermute(total, "x", shift(NX, k)) for k in (1, 2, 3)]
    scaled = scale(blocks, everyone, n)

    up, down = mix((4, 5), scaled, parts, BF)
    for ahead, behind in ((3, 6), (2, 7), (1, 0)):
        up_part, down_part = mix((ahead, behind), scaled, parts, F32)
        up = (lax.ppermute(up, "z", shift(NZ, 1)).astype(F32) + up_part).astype(BF)
        if behind:
            down = (lax.ppermute(down, "z", shift(NZ, -1)).astype(F32) + down_part).astype(BF)
    up = lax.ppermute(up, "z", shift(NZ, 1))
    down = lax.ppermute(down, "z", shift(NZ, -1))

    weights = loss_weight.astype(F32)[:, None]
    grad_proj, partial_weight = finish(
        up, down, down_part, message, weights, unit_view, inv_norm, feats_t
    )
    grad_feats = jnp.dot(grad_proj, weight.T, preferred_element_type=F32).astype(BF)
    grad_weight = sum_everywhere(partial_weight)
    return (grad_feats, grad_weight)


def solution(mesh):
    mesh = Mesh(mesh.devices.reshape(NY, NC, NZ, NX), ("y", "core", "z", "x"))
    views = ("y", "core", "z", "x")
    in_specs = (
        P(views, None),
        P(),
        P(QUEUE, None),
        P(views, None),
        P(views),
        P(views),
    )
    out_specs = (P(views, None), P())
    return jax.shard_map(local, mesh=mesh, in_specs=in_specs, out_specs=out_specs, check_vma=False)
```

time: 218 us -> 202 us (0.927)
  Pallas kernels: 29.9 us -> 13.2 us
  starting transfers between devices: 39.6 us -> 54.5 us
  between operations: 14.3 us -> 0.92 us
  local copies, waits for them, and re-layouts: 20.6 us -> 25.3 us
  blocking collectives: 50.1 us -> 45.8 us
  waiting for transfers between devices: 55.9 us -> 58.2 us
    all_to_all x1, waiting for transfers between devices: 27 us -> 0.01 us  [local(): lax.all_to_all(picked, QUEUE, split_axis=0, concat_axis=0, tiled=True)]
    ppermute x5 -> x12, waiting for transfers between devices: 13.6 us -> 34.9 us  [the longest x1 26.8 us: local(): views[5] = lax.ppermute(views[6], 'z', shift(NZ, 1))]
    pallas_call x7 -> x9, Pallas kernels: 26.6 us -> 11 us  [the longest x4 5.18 us: exps(): vmem_call(exps_kernel, (jax.ShapeDtypeStruct((NZ, n, n), BF), jax.ShapeDt...]
    ppermute x5 -> x12, starting transfers between devices: 4.68 us -> 17.7 us  [the longest x2 4.53 us: local(): lax.ppermute(down, 'z', shift(NZ, -1)).astype(F32) + down_part]
    ppermute x3, waiting for transfers between devices: 0.01 us -> 6.11 us  [local(): lax.ppermute(message, 'x', shift(NX, k))]
    ppermute x1, waiting for transfers between devices: 1.02 us -> 6.25 us  [local(): up = lax.ppermute(up, 'z', shift(NZ, 1))]
    unnamed x31 -> x42, local copies, waits for them, and re-layouts: 8.46 us -> 13.7 us
    ppermute x1, waiting for transfers between devices: 4.87 us -> 0.35 us  [local(): down = lax.ppermute(down, 'z', shift(NZ, -1))]
  transfers between devices with their start and end apart: 21 -> 27, of which waited for: 14 -> 16; matrix products, arithmetic and copies ran while one was open for 7% -> 7% of each run, Pallas kernels for 9% -> 4%
where the time goes in v1:
time: 202 us
  waiting for transfers between devices  58.2 us (29%)
  starting transfers between devices  54.5 us (27%)
  blocking collectives  45.8 us (23%)
  local copies, waits for them, and re-layouts  25.3 us (13%)
  Pallas kernels  13.2 us (7%)
  other arithmetic  2.19 us (1%)
    ppermute x1, waiting for transfers between devices, local(): views[5] = lax.ppermute(views[6], 'z', shift(NZ, 1))  26.8 us
    all_to_all x1, blocking collectives, sum_everywhere(): v = lax.all_to_all(v, ('y', 'x'), 0, 0, tiled=True)  16.8 us
    all_to_all x1, blocking collectives, local(): lax.all_to_all(wanted, QUEUE, split_axis=0, concat_axis=0, tiled=True)  16.5 us
    unnamed x42, local copies, waits for them, and re-layouts  13.7 us
    all_to_all x1, blocking collectives, sum_everywhere(): v = lax.all_to_all(v.reshape(rows, width), ('y', 'x'), 0, 0, tiled=True)  12.5 us
    gather x1, local copies, waits for them, and re-layouts, local(): picked = support_queue[asked]  11.2 us
    ppermute x3, waiting for transfers between devices, local(): up = (lax.ppermute(up, 'z', shift(NZ, 1)).astype(F32) + up_part).astype(BF)  7.94 us
    ppermute x1, starting transfers between devices, sum_everywhere(): lax.ppermute(block_of(v, 1 - core, rows), 'core', flip(NC, 1))  7.86 us
  transfers between devices with their start and end apart: 27, of which 16 were waited for; matrix products, arithmetic and copies ran while one was open for 7% of the time, Pallas kernels for 4%

profile of v1, /device:TPU:1, one launch (start us, length us, event | category | flops | bytes accessed | tf_op | source)
XLA Modules:
  0.0 201.5 jit_solution(11300620320770382112)
XLA Ops:
  7.3 2.5 %collective-permute-start = (bf16[512,256]{1,0:T(8,128)(2,1)S(1)}, bf16[512,256]{1,0:T(8,128)(2,1)S(1)}, u32[]{:S(2)}, u32[]{:S(2)}) collective-permute-start(bf16[512,256]{1,0:T(8,128)(2,1)S(1)} %get-tuple-element.44.refs_0_), channel_id=1, source_target_pairs={{0,4},{4,8},{8,12},{12,16},{16,20},{20,24},{24,28},{28,0},{1,5},{5... | collective-permute-start | bytes 786440 | tf_op jit(solution)/shard_map/ppermute | solution.py:239
  9.7 3.9 %collective-permute-start.1 = (bf16[512,256]{1,0:T(8,128)(2,1)S(1)}, bf16[512,256]{1,0:T(8,128)(2,1)S(1)}, u32[]{:S(2)}, u32[]{:S(2)}) collective-permute-start(bf16[512,256]{1,0:T(8,128)(2,1)S(1)} %get-tuple-element.44.refs_0_), channel_id=1, source_target_pairs={{0,28},{4,0},{8,4},{12,8},{16,12},{20,16},{24,20},{28,24},{1,29},{... | collective-permute-start | bytes 786440 | tf_op jit(solution)/shard_map/ppermute | solution.py:240
  13.7 16.5 %all_to_all.35 = s32[32,1,64]{2,1,0:T(1,128)S(1)} all-to-all(s32[32,1,64]{2,1,0:T(1,128)S(1)} %bitcast.16), channel_id=1, replica_groups=mesh['y'=4,'core'=2,'z'=8,'x'=4] {'z','x'}, dimensions={0} | all-to-all | bytes 16384 | tf_op jit(solution)/shard_map/all_to_all | solution.py:241
  30.5 2.3 %collective-permute-start.3 = (bf16[512,256]{1,0:T(8,128)(2,1)S(1)}, bf16[512,256]{1,0:T(8,128)(2,1)S(1)}, u32[]{:S(2)}, u32[]{:S(2)}) collective-permute-start(bf16[512,256]{1,0:T(8,128)(2,1)S(1)} %collective-permute-done.1.refs_1_), channel_id=1, source_target_pairs={{0,28},{4,0},{8,4},{12,8},{16,12},{20,16},{24,20},{28,24},{1,29},{... | collective-permute-start | bytes 786440 | tf_op jit(solution)/shard_map/ppermute | solution.py:244
  33.0 11.2 %gather_fusion = bf16[2048,256]{1,0:T(8,128)(2,1)} fusion(bf16[8192,256]{1,0:T(8,128)(2,1)} %param.10, s32[2048]{0:T(1024)S(1)} %broadcast_clamp_fusion), kind=kCustom, calls=%fused_computation | custom fusion | bytes 2105344 | tf_op jit(solution)/shard_map/gather | solution.py:245
  44.2 3.9 %all-to-all-start.1 = ((bf16[32,64,256]{2,1,0:T(8,128)(2,1)}), bf16[32,64,256]{2,1,0:T(8,128)(2,1)S(1)}, u32[]{:S(2)}, u32[]{:S(2)}) async-start(bf16[32,64,256]{2,1,0:T(8,128)(2,1)} %bitcast.19), calls=%async_computation.1 | async-start | bytes 2097152 | tf_op jit(solution)/shard_map/all_to_all | solution.py:253
  49.4 1.5 collective-permute-start.7
  50.9 26.8 %collective-permute-done.8.refs_5_ = bf16[512,256]{1,0:T(8,128)(2,1)S(1)} collective-permute-done((bf16[512,256]{1,0:T(8,128)(2,1)S(1)}, bf16[512,256]{1,0:T(8,128)(2,1)S(1)}, u32[]{:S(2)}, u32[]{:S(2)}) %collective-permute-start.8) | collective-permute-done | bytes 262176 | tf_op jit(solution)/shard_map/ppermute | solution.py:247
  79.6 2.7 %collective-permute-start.5 = (bf16[528,256]{1,0:T(8,128)(2,1)S(1)}, bf16[528,256]{1,0:T(8,128)(2,1)S(1)}, u32[]{:S(2)}, u32[]{:S(2)}) collective-permute-start(bf16[528,256]{1,0:T(8,128)(2,1)S(1)} %pick.1.a_ref.refs_0_.anchors_ref), channel_id=1, source_target_pairs={{0,2},{1,3},{2,0},{3,1},{4,6},{5,7},{6,4},{7,5},{8,10},{9,11},{10,... | collective-permute-start | bytes 811016 | tf_op jit(solution)/shard_map/ppermute | solution.py:257
  82.7 2.3 %collective-permute-start.6 = (bf16[528,256]{1,0:T(8,128)(2,1)S(1)}, bf16[528,256]{1,0:T(8,128)(2,1)S(1)}, u32[]{:S(2)}, u32[]{:S(2)}) collective-permute-start(bf16[528,256]{1,0:T(8,128)(2,1)S(1)} %pick.1.a_ref.refs_0_.anchors_ref), channel_id=1, source_target_pairs={{0,3},{1,0},{2,1},{3,2},{4,7},{5,4},{6,5},{7,6},{8,11},{9,8},{10,9... | collective-permute-start | bytes 811016 | tf_op jit(solution)/shard_map/ppermute | solution.py:257
  87.9 5.9 %collective-permute-done.4.a_ref.refs_1_ = bf16[528,256]{1,0:T(8,128)(2,1)S(1)} collective-permute-done((bf16[528,256]{1,0:T(8,128)(2,1)S(1)}, bf16[528,256]{1,0:T(8,128)(2,1)S(1)}, u32[]{:S(2)}, u32[]{:S(2)}) %collective-permute-start.4) | collective-permute-done | bytes 270368 | tf_op jit(solution)/shard_map/ppermute | solution.py:257
  95.1 1.3 exps.7
  97.4 1.7 collective-permute-start.11
  99.1 2.0 collective-permute-start.12
  106.2 1.7 collective-permute-start.17
  107.9 2.4 %collective-permute-done.13 = bf16[512,256]{1,0:T(8,128)(2,1)S(1)} collective-permute-done((bf16[512,256]{1,0:T(8,128)(2,1)S(1)}, bf16[512,256]{1,0:T(8,128)(2,1)S(1)}, u32[]{:S(2)}, u32[]{:S(2)}) %collective-permute-start.13) | collective-permute-done | bytes 262176 | tf_op jit(solution)/shard_map/ppermute | solution.py:269
  111.9 2.9 %collective-permute-start.18 = (bf16[512,256]{1,0:T(8,128)(2,1)S(1)}, bf16[512,256]{1,0:T(8,128)(2,1)S(1)}, u32[]{:S(2)}, u32[]{:S(2)}) collective-permute-start(bf16[512,256]{1,0:T(8,128)(2,1)S(1)} %add_convert_fusion.1), channel_id=1, source_target_pairs={{0,28},{4,0},{8,4},{12,8},{16,12},{20,16},{24,20},{28,24},{1,29},{... | collective-permute-start | bytes 786440 | tf_op jit(solution)/shard_map/ppermute | solution.py:271
  114.7 2.2 %collective-permute-done.14 = bf16[512,256]{1,0:T(8,128)(2,1)S(1)} collective-permute-done((bf16[512,256]{1,0:T(8,128)(2,1)S(1)}, bf16[512,256]{1,0:T(8,128)(2,1)S(1)}, u32[]{:S(2)}, u32[]{:S(2)}) %collective-permute-start.14) | collective-permute-done | bytes 262176 | tf_op jit(solution)/shard_map/ppermute | solution.py:269
  118.4 2.9 %collective-permute-start.19 = (bf16[512,256]{1,0:T(8,128)(2,1)S(1)}, bf16[512,256]{1,0:T(8,128)(2,1)S(1)}, u32[]{:S(2)}, u32[]{:S(2)}) collective-permute-start(bf16[512,256]{1,0:T(8,128)(2,1)S(1)} %add_convert_fusion), channel_id=1, source_target_pairs={{0,28},{4,0},{8,4},{12,8},{16,12},{20,16},{24,20},{28,24},{1,29},{... | collective-permute-start | bytes 786440 | tf_op jit(solution)/shard_map/ppermute | solution.py:273
  121.4 3.3 %collective-permute-done.15 = bf16[512,256]{1,0:T(8,128)(2,1)S(1)} collective-permute-done((bf16[512,256]{1,0:T(8,128)(2,1)S(1)}, bf16[512,256]{1,0:T(8,128)(2,1)S(1)}, u32[]{:S(2)}, u32[]{:S(2)}) %collective-permute-start.15) | collective-permute-done | bytes 262176 | tf_op jit(solution)/shard_map/ppermute | solution.py:269
  127.2 6.2 %collective-permute-done.16.up_ref = bf16[512,256]{1,0:T(8,128)(2,1)S(1)} collective-permute-done((bf16[512,256]{1,0:T(8,128)(2,1)}, bf16[512,256]{1,0:T(8,128)(2,1)S(1)}, u32[]{:S(2)}, u32[]{:S(2)}) %collective-permute-start.16) | collective-permute-done | bytes 262176 | tf_op jit(solution)/shard_map/ppermute | solution.py:272
  139.9 7.9 %collective-permute-start.20 = (f32[512,256]{1,0:T(8,128)S(1)}, f32[512,256]{1,0:T(8,128)S(1)}, u32[]{:S(2)}, u32[]{:S(2)}) collective-permute-start(f32[512,256]{1,0:T(8,128)S(1)} %constant_dynamic-slice_fusion), channel_id=1, source_target_pairs={{0,32},{32,0},{1,33},{33,1},{2,34},{34,2},{3,35},{35,3},{4,36},{36... | collective-permute-start | bytes 1572872 | tf_op jit(solution)/shard_map/ppermute | solution.py:216
  147.8 1.5 collective-permute-done.20
  149.4 16.8 %all_to_all.36 = f32[16,32,256]{2,1,0:T(8,128)S(1)} all-to-all(f32[16,32,256]{2,1,0:T(8,128)S(1)} %bitcast.22), channel_id=1, replica_groups=mesh['y'=4,'core'=2,'z'=8,'x'=4] {'y','x'}, dimensions={0} | all-to-all | bytes 1048576 | tf_op jit(solution)/shard_map/all_to_all | solution.py:218
  166.4 3.4 %collective-permute-start.22 = (f32[32,256]{1,0:T(8,128)S(1)}, f32[32,256]{1,0:T(8,128)S(1)}, u32[]{:S(2)}, u32[]{:S(2)}) collective-permute-start(f32[32,256]{1,0:T(8,128)S(1)} %reduce_sum.9), channel_id=1, source_target_pairs={{0,8},{4,12},{8,0},{12,4},{16,24},{20,28},{24,16},{28,20},{1,9},{5... | collective-permute-start | bytes 98312 | tf_op jit(solution)/shard_map/ppermute | solution.py:220
  169.9 1.6 collective-permute-done.22
  171.5 2.9 %collective-permute-done.23 = f32[32,256]{1,0:T(8,128)S(1)} collective-permute-done((f32[32,256]{1,0:T(8,128)S(1)}, f32[32,256]{1,0:T(8,128)S(1)}, u32[]{:S(2)}, u32[]{:S(2)}) %collective-permute-start.23) | collective-permute-done | bytes 32800 | tf_op jit(solution)/shard_map/ppermute | solution.py:220
  174.4 3.1 %collective-permute-start.24 = (f32[32,256]{1,0:T(8,128)S(1)}, f32[32,256]{1,0:T(8,128)S(1)}, u32[]{:S(2)}, u32[]{:S(2)}) collective-permute-start(f32[32,256]{1,0:T(8,128)S(1)} %add_add_fusion), channel_id=1, source_target_pairs={{0,16},{4,20},{8,24},{12,28},{16,0},{20,4},{24,8},{28,12},{1,17},{... | collective-permute-start | bytes 98312 | tf_op jit(solution)/shard_map/ppermute | solution.py:222
  177.4 3.7 %collective-permute-done.24 = f32[32,256]{1,0:T(8,128)S(1)} collective-permute-done((f32[32,256]{1,0:T(8,128)S(1)}, f32[32,256]{1,0:T(8,128)S(1)}, u32[]{:S(2)}, u32[]{:S(2)}) %collective-permute-start.24) | collective-permute-done | bytes 32800 | tf_op jit(solution)/shard_map/ppermute | solution.py:222
  181.2 12.5 %all_to_all.37 = f32[16,32,256]{2,1,0:T(8,128)S(1)} all-to-all(f32[16,32,256]{2,1,0:T(8,128)S(1)} %broadcast_in_dim.18), channel_id=1, replica_groups=mesh['y'=4,'core'=2,'z'=8,'x'=4] {'y','x'}, dimensions={0} | all-to-all | bytes 1048576 | tf_op jit(solution)/shard_map/all_to_all | solution.py:224
  193.7 5.2 %collective-permute-start.25 = (f32[512,256]{1,0:T(8,128)S(1)}, f32[512,256]{1,0:T(8,128)S(1)}, u32[]{:S(2)}, u32[]{:S(2)}) collective-permute-start(f32[512,256]{1,0:T(8,128)S(1)} %bitcast.20), channel_id=1, source_target_pairs={{0,32},{32,0},{1,33},{33,1},{2,34},{34,2},{3,35},{35,3},{4,36},{36... | collective-permute-start | bytes 1572872 | tf_op jit(solution)/shard_map/ppermute | solution.py:225
  198.9 1.4 convolution_convert_fusion
  (101 shorter events, 34.1 us)
Async XLA Ops:
  0.6 1.2 copy-start
  7.3 22.9 %collective-permute-start = (bf16[512,256]{1,0:T(8,128)(2,1)S(1)}, bf16[512,256]{1,0:T(8,128)(2,1)S(1)}, u32[]{:S(2)}, u32[]{:S(2)}) collective-permute-start(bf16[512,256]{1,0:T(8,128)(2,1)S(1)} %get-tuple-element.44.refs_0_), channel_id=1, source_target_pairs={{0,4},{4,8},{8,12},{12,16},{16,20},{20,24},{24,28},{28,0},{1,5},{5... | collective-permute-start | bytes 786440 | tf_op jit(solution)/shard_map/ppermute | solution.py:239
  9.7 20.5 %collective-permute-start.1 = (bf16[512,256]{1,0:T(8,128)(2,1)S(1)}, bf16[512,256]{1,0:T(8,128)(2,1)S(1)}, u32[]{:S(2)}, u32[]{:S(2)}) collective-permute-start(bf16[512,256]{1,0:T(8,128)(2,1)S(1)} %get-tuple-element.44.refs_0_), channel_id=1, source_target_pairs={{0,28},{4,0},{8,4},{12,8},{16,12},{20,16},{24,20},{28,24},{1,29},{... | collective-permute-start | bytes 786440 | tf_op jit(solution)/shard_map/ppermute | solution.py:240
  30.2 14.0 %collective-permute-start.2 = (bf16[512,256]{1,0:T(8,128)(2,1)S(1)}, bf16[512,256]{1,0:T(8,128)(2,1)S(1)}, u32[]{:S(2)}, u32[]{:S(2)}) collective-permute-start(bf16[512,256]{1,0:T(8,128)(2,1)S(1)} %collective-permute-done.refs_7_), channel_id=1, source_target_pairs={{0,4},{4,8},{8,12},{12,16},{16,20},{20,24},{24,28},{28,0},{1,5},{5... | collective-permute-start | bytes 786440 | tf_op jit(solution)/shard_map/ppermute | solution.py:243
  30.5 13.7 %collective-permute-start.3 = (bf16[512,256]{1,0:T(8,128)(2,1)S(1)}, bf16[512,256]{1,0:T(8,128)(2,1)S(1)}, u32[]{:S(2)}, u32[]{:S(2)}) collective-permute-start(bf16[512,256]{1,0:T(8,128)(2,1)S(1)} %collective-permute-done.1.refs_1_), channel_id=1, source_target_pairs={{0,28},{4,0},{8,4},{12,8},{16,12},{20,16},{24,20},{28,24},{1,29},{... | collective-permute-start | bytes 786440 | tf_op jit(solution)/shard_map/ppermute | solution.py:244
  33.0 44.8 %copy-start.18 = (bf16[512]{0:T(512)(128)(2,1)S(1)}, bf16[512]{0:T(512)(128)(2,1)}, u32[]{:S(2)}) copy-start(bf16[512]{0:T(512)(128)(2,1)} %param.13) | copy-start | bytes 3076
  44.2 33.6 %all-to-all-start.1 = ((bf16[32,64,256]{2,1,0:T(8,128)(2,1)}), bf16[32,64,256]{2,1,0:T(8,128)(2,1)S(1)}, u32[]{:S(2)}, u32[]{:S(2)}) async-start(bf16[32,64,256]{2,1,0:T(8,128)(2,1)} %bitcast.19), calls=%async_computation.1 | async-start | bytes 2097152 | tf_op jit(solution)/shard_map/all_to_all | solution.py:253
  48.2 29.6 %collective-permute-start.8 = (bf16[512,256]{1,0:T(8,128)(2,1)S(1)}, bf16[512,256]{1,0:T(8,128)(2,1)S(1)}, u32[]{:S(2)}, u32[]{:S(2)}) collective-permute-start(bf16[512,256]{1,0:T(8,128)(2,1)S(1)} %collective-permute-done.2.refs_6_), channel_id=1, source_target_pairs={{0,4},{4,8},{8,12},{12,16},{16,20},{20,24},{24,28},{28,0},{1,5},{5... | collective-permute-start | bytes 786440 | tf_op jit(solution)/shard_map/ppermute | solution.py:247
  49.4 35.6 %collective-permute-start.7 = (bf16[512,256]{1,0:T(8,128)(2,1)S(1)}, bf16[512,256]{1,0:T(8,128)(2,1)S(1)}, u32[]{:S(2)}, u32[]{:S(2)}) collective-permute-start(bf16[512,256]{1,0:T(8,128)(2,1)S(1)} %collective-permute-done.3.refs_2_), channel_id=1, source_target_pairs={{0,28},{4,0},{8,4},{12,8},{16,12},{20,16},{24,20},{28,24},{1,29},{... | collective-permute-start | bytes 786440 | tf_op jit(solution)/shard_map/ppermute | solution.py:248
  77.8 7.3 %collective-permute-start.9 = (bf16[512,256]{1,0:T(8,128)(2,1)S(1)}, bf16[512,256]{1,0:T(8,128)(2,1)S(1)}, u32[]{:S(2)}, u32[]{:S(2)}) collective-permute-start(bf16[512,256]{1,0:T(8,128)(2,1)S(1)} %collective-permute-done.8.refs_5_), channel_id=1, source_target_pairs={{0,4},{4,8},{8,12},{12,16},{16,20},{20,24},{24,28},{28,0},{1,5},{5... | collective-permute-start | bytes 786440 | tf_op jit(solution)/shard_map/ppermute | solution.py:249
  79.6 7.0 %collective-permute-start.5 = (bf16[528,256]{1,0:T(8,128)(2,1)S(1)}, bf16[528,256]{1,0:T(8,128)(2,1)S(1)}, u32[]{:S(2)}, u32[]{:S(2)}) collective-permute-start(bf16[528,256]{1,0:T(8,128)(2,1)S(1)} %pick.1.a_ref.refs_0_.anchors_ref), channel_id=1, source_target_pairs={{0,2},{1,3},{2,0},{3,1},{4,6},{5,7},{6,4},{7,5},{8,10},{9,11},{10,... | collective-permute-start | bytes 811016 | tf_op jit(solution)/shard_map/ppermute | solution.py:257
  82.3 11.4 %collective-permute-start.4 = (bf16[528,256]{1,0:T(8,128)(2,1)S(1)}, bf16[528,256]{1,0:T(8,128)(2,1)S(1)}, u32[]{:S(2)}, u32[]{:S(2)}) collective-permute-start(bf16[528,256]{1,0:T(8,128)(2,1)S(1)} %pick.1.a_ref.refs_0_.anchors_ref), channel_id=1, source_target_pairs={{0,1},{1,2},{2,3},{3,0},{4,5},{5,6},{6,7},{7,4},{8,9},{9,10},{10,1... | collective-permute-start | bytes 811016 | tf_op jit(solution)/shard_map/ppermute | solution.py:257
  82.7 12.4 %collective-permute-start.6 = (bf16[528,256]{1,0:T(8,128)(2,1)S(1)}, bf16[528,256]{1,0:T(8,128)(2,1)S(1)}, u32[]{:S(2)}, u32[]{:S(2)}) collective-permute-start(bf16[528,256]{1,0:T(8,128)(2,1)S(1)} %pick.1.a_ref.refs_0_.anchors_ref), channel_id=1, source_target_pairs={{0,3},{1,0},{2,1},{3,2},{4,7},{5,4},{6,5},{7,6},{8,11},{9,8},{10,9... | collective-permute-start | bytes 811016 | tf_op jit(solution)/shard_map/ppermute | solution.py:257
  96.4 4.7 %collective-permute-start.10 = (f32[1,2048]{1,0:T(1,128)S(1)}, f32[1,2048]{1,0:T(1,128)S(1)}, u32[]{:S(2)}, u32[]{:S(2)}) collective-permute-start(f32[1,2048]{1,0:T(1,128)S(1)} %constant_dynamic-update-slice_fusion.refs_4_), channel_id=1, source_target_pairs={{0,1},{1,2},{2,3},{3,0},{4,5},{5,6},{6,7},{7,4},{8,9},{9,10},{10,1... | collective-permute-start | bytes 24584 | tf_op jit(solution)/shard_map/ppermute | solution.py:263
  97.4 4.0 %collective-permute-start.11 = (f32[1,2048]{1,0:T(1,128)S(1)}, f32[1,2048]{1,0:T(1,128)S(1)}, u32[]{:S(2)}, u32[]{:S(2)}) collective-permute-start(f32[1,2048]{1,0:T(1,128)S(1)} %constant_dynamic-update-slice_fusion.refs_4_), channel_id=1, source_target_pairs={{0,2},{1,3},{2,0},{3,1},{4,6},{5,7},{6,4},{7,5},{8,10},{9,11},{10,... | collective-permute-start | bytes 24584 | tf_op jit(solution)/shard_map/ppermute | solution.py:263
  99.1 2.8 %collective-permute-start.12 = (f32[1,2048]{1,0:T(1,128)S(1)}, f32[1,2048]{1,0:T(1,128)S(1)}, u32[]{:S(2)}, u32[]{:S(2)}) collective-permute-start(f32[1,2048]{1,0:T(1,128)S(1)} %constant_dynamic-update-slice_fusion.refs_4_), channel_id=1, source_target_pairs={{0,3},{1,0},{2,1},{3,2},{4,7},{5,4},{6,5},{7,6},{8,11},{9,8},{10,9... | collective-permute-start | bytes 24584 | tf_op jit(solution)/shard_map/ppermute | solution.py:263
  103.8 6.5 %collective-permute-start.13 = (bf16[512,256]{1,0:T(8,128)(2,1)S(1)}, bf16[512,256]{1,0:T(8,128)(2,1)S(1)}, u32[]{:S(2)}, u32[]{:S(2)}) collective-permute-start(bf16[512,256]{1,0:T(8,128)(2,1)S(1)} %get-tuple-element.60), channel_id=1, source_target_pairs={{0,4},{4,8},{8,12},{12,16},{16,20},{20,24},{24,28},{28,0},{1,5},{5... | collective-permute-start | bytes 786440 | tf_op jit(solution)/shard_map/ppermute | solution.py:269
  106.2 5.6 %collective-permute-start.17 = (bf16[512,256]{1,0:T(8,128)(2,1)S(1)}, bf16[512,256]{1,0:T(8,128)(2,1)S(1)}, u32[]{:S(2)}, u32[]{:S(2)}) collective-permute-start(bf16[512,256]{1,0:T(8,128)(2,1)S(1)} %get-tuple-element.64), channel_id=1, source_target_pairs={{0,28},{4,0},{8,4},{12,8},{16,12},{20,16},{24,20},{28,24},{1,29},{... | collective-permute-start | bytes 786440 | tf_op jit(solution)/shard_map/ppermute | solution.py:271
  110.4 6.6 %collective-permute-start.14 = (bf16[512,256]{1,0:T(8,128)(2,1)S(1)}, bf16[512,256]{1,0:T(8,128)(2,1)S(1)}, u32[]{:S(2)}, u32[]{:S(2)}) collective-permute-start(bf16[512,256]{1,0:T(8,128)(2,1)S(1)} %add_convert_fusion.4), channel_id=1, source_target_pairs={{0,4},{4,8},{8,12},{12,16},{16,20},{20,24},{24,28},{28,0},{1,5},{5... | collective-permute-start | bytes 786440 | tf_op jit(solution)/shard_map/ppermute | solution.py:269
  111.9 6.5 %collective-permute-start.18 = (bf16[512,256]{1,0:T(8,128)(2,1)S(1)}, bf16[512,256]{1,0:T(8,128)(2,1)S(1)}, u32[]{:S(2)}, u32[]{:S(2)}) collective-permute-start(bf16[512,256]{1,0:T(8,128)(2,1)S(1)} %add_convert_fusion.1), channel_id=1, source_target_pairs={{0,28},{4,0},{8,4},{12,8},{16,12},{20,16},{24,20},{28,24},{1,29},{... | collective-permute-start | bytes 786440 | tf_op jit(solution)/shard_map/ppermute | solution.py:271
  117.0 8.4 %copy-start.1 = (bf16[512,1024]{1,0:T(8,128)(2,1)S(1)}, bf16[512,1024]{1,0:T(8,128)(2,1)}, u32[]{:S(2)}) copy-start(bf16[512,1024]{1,0:T(8,128)(2,1)} %feats_ref.1) | copy-start | bytes 3145732
  117.0 7.6 %collective-permute-start.15 = (bf16[512,256]{1,0:T(8,128)(2,1)S(1)}, bf16[512,256]{1,0:T(8,128)(2,1)S(1)}, u32[]{:S(2)}, u32[]{:S(2)}) collective-permute-start(bf16[512,256]{1,0:T(8,128)(2,1)S(1)} %add_convert_fusion.3), channel_id=1, source_target_pairs={{0,4},{4,8},{8,12},{12,16},{16,20},{20,24},{24,28},{28,0},{1,5},{5... | collective-permute-start | bytes 786440 | tf_op jit(solution)/shard_map/ppermute | solution.py:269
  118.4 7.1 %copy-start.6 = (f32[512,256]{1,0:T(8,128)}, f32[512,256]{1,0:T(8,128)S(1)}, u32[]{:S(2)}) copy-start(f32[512,256]{1,0:T(8,128)S(1)} %get-tuple-element.67.own_ref) | copy-start | bytes 1572868
  118.4 8.1 %collective-permute-start.19 = (bf16[512,256]{1,0:T(8,128)(2,1)S(1)}, bf16[512,256]{1,0:T(8,128)(2,1)S(1)}, u32[]{:S(2)}, u32[]{:S(2)}) collective-permute-start(bf16[512,256]{1,0:T(8,128)(2,1)S(1)} %add_convert_fusion), channel_id=1, source_target_pairs={{0,28},{4,0},{8,4},{12,8},{16,12},{20,16},{24,20},{28,24},{1,29},{... | collective-permute-start | bytes 786440 | tf_op jit(solution)/shard_map/ppermute | solution.py:273
  125.4 8.0 %collective-permute-start.16 = (bf16[512,256]{1,0:T(8,128)(2,1)}, bf16[512,256]{1,0:T(8,128)(2,1)S(1)}, u32[]{:S(2)}, u32[]{:S(2)}) collective-permute-start(bf16[512,256]{1,0:T(8,128)(2,1)} %add_convert_fusion.2), channel_id=1, source_target_pairs={{0,4},{4,8},{8,12},{12,16},{16,20},{20,24},{24,28},{28,0},{1,5},{5... | collective-permute-start | bytes 786440 | tf_op jit(solution)/shard_map/ppermute | solution.py:272
  139.1 59.8 %copy-start.3 = (bf16[1024,256]{1,0:T(8,128)(2,1)S(1)}, bf16[1024,256]{1,0:T(8,128)(2,1)}, u32[]{:S(2)}) copy-start(bf16[1024,256]{1,0:T(8,128)(2,1)} %weight_ref.1) | copy-start | bytes 1572868
  139.9 9.4 %collective-permute-start.20 = (f32[512,256]{1,0:T(8,128)S(1)}, f32[512,256]{1,0:T(8,128)S(1)}, u32[]{:S(2)}, u32[]{:S(2)}) collective-permute-start(f32[512,256]{1,0:T(8,128)S(1)} %constant_dynamic-slice_fusion), channel_id=1, source_target_pairs={{0,32},{32,0},{1,33},{33,1},{2,34},{34,2},{3,35},{35,3},{4,36},{36... | collective-permute-start | bytes 1572872 | tf_op jit(solution)/shard_map/ppermute | solution.py:216
  166.3 3.6 %collective-permute-start.21 = (f32[32,256]{1,0:T(8,128)S(1)}, f32[32,256]{1,0:T(8,128)S(1)}, u32[]{:S(2)}, u32[]{:S(2)}) collective-permute-start(f32[32,256]{1,0:T(8,128)S(1)} %reduce_sum.9), channel_id=1, source_target_pairs={{0,4},{4,0},{8,12},{12,8},{16,20},{20,16},{24,28},{28,24},{1,5},{5... | collective-permute-start | bytes 98312 | tf_op jit(solution)/shard_map/ppermute | solution.py:220
  166.4 5.1 %collective-permute-start.22 = (f32[32,256]{1,0:T(8,128)S(1)}, f32[32,256]{1,0:T(8,128)S(1)}, u32[]{:S(2)}, u32[]{:S(2)}) collective-permute-start(f32[32,256]{1,0:T(8,128)S(1)} %reduce_sum.9), channel_id=1, source_target_pairs={{0,8},{4,12},{8,0},{12,4},{16,24},{20,28},{24,16},{28,20},{1,9},{5... | collective-permute-start | bytes 98312 | tf_op jit(solution)/shard_map/ppermute | solution.py:220
  169.8 4.6 %collective-permute-start.23 = (f32[32,256]{1,0:T(8,128)S(1)}, f32[32,256]{1,0:T(8,128)S(1)}, u32[]{:S(2)}, u32[]{:S(2)}) collective-permute-start(f32[32,256]{1,0:T(8,128)S(1)} %reduce_sum.9), channel_id=1, source_target_pairs={{0,12},{4,8},{8,4},{12,0},{16,28},{20,24},{24,20},{28,16},{1,13},{... | collective-permute-start | bytes 98312 | tf_op jit(solution)/shard_map/ppermute | solution.py:220
  174.4 6.8 %collective-permute-start.24 = (f32[32,256]{1,0:T(8,128)S(1)}, f32[32,256]{1,0:T(8,128)S(1)}, u32[]{:S(2)}, u32[]{:S(2)}) collective-permute-start(f32[32,256]{1,0:T(8,128)S(1)} %add_add_fusion), channel_id=1, source_target_pairs={{0,16},{4,20},{8,24},{12,28},{16,0},{20,4},{24,8},{28,12},{1,17},{... | collective-permute-start | bytes 98312 | tf_op jit(solution)/shard_map/ppermute | solution.py:222
  193.7 6.8 %collective-permute-start.25 = (f32[512,256]{1,0:T(8,128)S(1)}, f32[512,256]{1,0:T(8,128)S(1)}, u32[]{:S(2)}, u32[]{:S(2)}) collective-permute-start(f32[512,256]{1,0:T(8,128)S(1)} %bitcast.20), channel_id=1, source_target_pairs={{0,32},{32,0},{1,33},{33,1},{2,34},{34,2},{3,35},{35,3},{4,36},{36... | collective-permute-start | bytes 1572872 | tf_op jit(solution)/shard_map/ppermute | solution.py:225
  (14 other events, 11.9 us)

commit v2 on v1

v2 whole, which is shorter than its diff:
```python
import functools
import math

import jax
import jax.numpy as jnp
from jax import lax
from jax.experimental import pallas as pl
from jax.experimental.pallas import tpu as pltpu
from jax.sharding import Mesh
from jax.sharding import PartitionSpec as P

TEMPER = 0.1
EPSILON = 1e-06
NZ, NX, NY, NC = 8, 4, 4, 2
CAP = 64
BF = jnp.bfloat16
F32 = jnp.float32
VMEM_LIMIT = 16 * 1024 * 1024
ALL_VMEM = 62 * 1024 * 1024
IN_VMEM = pl.BlockSpec(memory_space=pltpu.VMEM)
EXPONENT = math.log2(math.e) / TEMPER
QUEUE = ("z", "x")


def shift(size, by):
    return [(i, (i + by) % size) for i in range(size)]


def flip(size, mask):
    return [(i, i ^ mask) for i in range(size)]


def vmem_call(kernel, out_shape, name, limit=VMEM_LIMIT, **kw):
    return pl.pallas_call(
        kernel,
        out_shape=out_shape,
        compiler_params=pltpu.CompilerParams(vmem_limit_bytes=limit),
        name=name,
        **kw,
    )


def ranks(owner, shards):
    n = owner.shape[1]
    onehot = jnp.where(owner == lax.broadcasted_iota(jnp.int32, (shards, n), 0), 1.0, 0.0)
    above = lax.broadcasted_iota(jnp.int32, (n, n), 0) < lax.broadcasted_iota(jnp.int32, (n, n), 1)
    above = jnp.where(above, 1.0, 0.0).astype(BF)
    before = jnp.dot(onehot.astype(BF), above, preferred_element_type=F32)
    return onehot, jnp.sum(before * onehot, axis=0, keepdims=True).astype(jnp.int32)


def project(features, weight):
    projected = jnp.dot(features, weight, preferred_element_type=F32)
    inv = lax.rsqrt(jnp.sum(projected * projected, axis=1, keepdims=True) + EPSILON)
    return projected * inv, inv


def begin_kernel(
    feats_hbm,
    weight_hbm,
    owner_hbm,
    slot_hbm,
    view_ref,
    wanted_ref,
    feats_ref,
    weight_ref,
    owner_ref,
    slot_ref,
    sems,
):
    copies = [
        pltpu.make_async_copy(owner_hbm, owner_ref, sems.at[0]),
        pltpu.make_async_copy(slot_hbm, slot_ref, sems.at[1]),
        pltpu.make_async_copy(weight_hbm, weight_ref, sems.at[2]),
        pltpu.make_async_copy(feats_hbm, feats_ref, sems.at[3]),
    ]
    for copy in copies:
        copy.start()
    copies[0].wait()
    copies[1].wait()
    n = owner_ref.shape[1]
    slot = slot_ref[...]
    onehot, rank = ranks(owner_ref[...], wanted_ref.shape[0])
    chosen = jnp.where(rank == lax.broadcasted_iota(jnp.int32, (128, n), 0), 1.0, 0.0).astype(BF)
    both = (((1,), (1,)), ((), ()))
    high = (onehot * (slot >> 7).astype(F32)).astype(BF)
    low = (onehot * (slot & 127).astype(F32)).astype(BF)
    upper = lax.dot_general(high, chosen, both, preferred_element_type=F32)
    lower = lax.dot_general(low, chosen, both, preferred_element_type=F32)
    full = upper.astype(jnp.int32) * 128 + lower.astype(jnp.int32)
    wanted_ref[...] = full[:, :CAP]
    copies[2].wait()
    copies[3].wait()
    view_ref[...] = project(feats_ref[...], weight_ref[...])[0].astype(BF)


def begin(features, weight, owner, slot):
    n, width = features.shape[0], weight.shape[1]
    in_hbm = pl.BlockSpec(memory_space=pltpu.HBM)
    return vmem_call(
        begin_kernel,
        (
            jax.ShapeDtypeStruct((n, width), BF),
            jax.ShapeDtypeStruct((NZ * NX, CAP), jnp.int32),
        ),
        "begin",
        ALL_VMEM,
        in_specs=[in_hbm] * 4,
        out_specs=(IN_VMEM, IN_VMEM),
        scratch_shapes=[
            pltpu.VMEM(features.shape, BF),
            pltpu.VMEM(weight.shape, BF),
            pltpu.VMEM(owner.shape, jnp.int32),
            pltpu.VMEM(slot.shape, jnp.int32),
            pltpu.SemaphoreType.DMA((4,)),
        ],
    )(features, weight, owner, slot)


def column_of(row):
    return jnp.broadcast_to(row, (8, row.shape[1])).T[:, :1]


def pick_kernel(rows_ref, owner_ref, extra_ref, out_ref):
    n = owner_ref.shape[1]
    owner = owner_ref[...]
    places = column_of(owner * CAP + ranks(owner, rows_ref.shape[0] // CAP)[1])
    column = lax.broadcasted_iota(jnp.int32, (n, n), 1)
    total = None
    for at in range(0, rows_ref.shape[0], n):
        onehot = jnp.where(places == column + at, 1.0, 0.0).astype(BF)
        term = jnp.dot(onehot, rows_ref[at : at + n, :], preferred_element_type=F32)
        total = term if total is None else total + term
    unit = total * lax.rsqrt(jnp.sum(total * total, axis=1, keepdims=True) + EPSILON)
    out_ref[:n, :] = unit.astype(BF)
    out_ref[n:, :] = extra_ref[...]


def pick(rows, owner, extra):
    n = owner.shape[1]
    return vmem_call(
        pick_kernel,
        jax.ShapeDtypeStruct((n + extra.shape[0], rows.shape[1]), BF),
        "pick",
        in_specs=[IN_VMEM] * 3,
        out_specs=IN_VMEM,
    )(rows, owner, extra)


def exps_kernel(a_ref, *refs):
    views, (e_ref, t_ref) = refs[:NZ], refs[NZ:]
    n = t_ref.shape[1]
    a = a_ref[:n, :]
    total = jnp.zeros((8, n), F32)
    for k in range(NZ):
        dots = lax.dot_general(
            views[k][...], a, (((1,), (1,)), ((), ())), preferred_element_type=F32
        )
        e = jnp.exp2(dots * EXPONENT)
        total = total + jnp.sum(e.reshape(n // 8, 8, n), axis=0)
        e_ref[k] = e.astype(BF)
    t_ref[...] = jnp.sum(total, axis=0, keepdims=True)


def exps(anchors, views):
    n = views[0].shape[0]
    return vmem_call(
        exps_kernel,
        (jax.ShapeDtypeStruct((NZ, n, n), BF), jax.ShapeDtypeStruct((1, n), F32)),
        "exps",
        in_specs=[IN_VMEM] * (1 + NZ),
        out_specs=(IN_VMEM, IN_VMEM),
    )(anchors, *views)


def weights_of(message_ref, n):
    w = message_ref[n : n + 16, :].astype(F32)
    return jnp.concatenate([w[k : k + 1, :] for k in range(n // w.shape[1])], axis=1)


def scale_kernel(*refs):
    anchors = refs[:NX]
    totals = refs[NX : 2 * NX]
    out_ref = refs[2 * NX]
    n = out_ref.shape[0] // NX
    for b in range(NX):
        t = None
        for k in range(NX):
            at = ((b - k) % NX) * n
            piece = totals[k][:, at : at + n]
            t = piece if t is None else t + piece
        column = column_of((1.0 / TEMPER) * weights_of(anchors[b], n) / t)
        out_ref[b * n : (b + 1) * n, :] = (anchors[b][:n, :].astype(F32) * column).astype(BF)


def scale(anchors, totals, n):
    return vmem_call(
        scale_kernel,
        jax.ShapeDtypeStruct((NX * n, anchors[0].shape[1]), BF),
        "scale",
        in_specs=[IN_VMEM] * (2 * NX),
        out_specs=IN_VMEM,
    )(*anchors, *totals)


def mix_kernel(which, a_ref, *refs):
    parts, outs = refs[:NX], refs[NX:]
    for k, out in zip(which, outs):
        total = None
        for b, part in enumerate(parts):
            size = part.shape[2]
            term = jnp.dot(part[k], a_ref[b * size : (b + 1) * size, :], preferred_element_type=F32)
            total = term if total is None else total + term
        out[...] = total.astype(out.dtype)


def mix(which, scaled, parts, dtype):
    shape = jax.ShapeDtypeStruct((parts[0].shape[1], scaled.shape[1]), dtype)
    return vmem_call(
        functools.partial(mix_kernel, which),
        tuple(shape for _ in which),
        "mix",
        in_specs=[IN_VMEM] * (1 + NX),
        out_specs=tuple(IN_VMEM for _ in which),
    )(scaled, *parts)


def finish_kernel(
    core_ref,
    up_ref,
    down_ref,
    own_ref,
    message_ref,
    feats_ref,
    weight_ref,
    grad_ref,
    keep_ref,
    send_ref,
):
    n = up_ref.shape[0]
    feats = feats_ref[...]
    unit, inv = project(feats, weight_ref[...])
    mixed = own_ref[...] + up_ref[...].astype(F32) + down_ref[...].astype(F32)
    w = column_of((1.0 / TEMPER) * weights_of(message_ref, n))
    grad = mixed - w * message_ref[:n, :].astype(F32)
    along = jnp.sum(unit * grad, axis=1, keepdims=True)
    grad = ((grad - unit * along) * inv).astype(BF)
    grad_ref[...] = grad
    part = lax.dot_general(feats, grad, (((0,), (0,)), ((), ())), preferred_element_type=F32)
    half = keep_ref.shape[0]
    for core in range(NC):

        @pl.when(core_ref[0] == core)
        def _():
            keep_ref[...] = part[core * half : (core + 1) * half]
            send_ref[...] = part[(1 - core) * half : (2 - core) * half]


def finish(core, up, down, own, message, features, weight):
    n, width = up.shape
    half = jax.ShapeDtypeStruct((features.shape[1] // NC, width), F32)
    return vmem_call(
        finish_kernel,
        (jax.ShapeDtypeStruct((n, width), BF), half, half),
        "finish",
        in_specs=[pl.BlockSpec(memory_space=pltpu.SMEM)] + [IN_VMEM] * 6,
        out_specs=(IN_VMEM,) * 3,
    )(core.reshape(1), up, down, own, message, features, weight)


def sum_everywhere(keep, send, core, beside):
    rows, width = keep.shape
    v = keep + lax.ppermute(send, "core", flip(NC, 1))
    many = NY * NX
    v = lax.all_to_all(v, ("y", "x"), 0, 0, tiled=True)
    v = jnp.sum(v.reshape(many, rows // many, width), axis=0)
    got = [lax.ppermute(v, "z", flip(NZ, m)) for m in (1, 2, 3)]
    v = (v + got[0]) + (got[1] + got[2])
    v = v + lax.ppermute(v, "z", flip(NZ, 4))
    v, beside = lax.optimization_barrier((v, beside))
    v = lax.optimization_barrier(jnp.broadcast_to(v[None], (many,) + v.shape))
    v = lax.all_to_all(v.reshape(rows, width), ("y", "x"), 0, 0, tiled=True)
    other = lax.ppermute(v, "core", flip(NC, 1))
    low, high = jnp.where(core == 0, v, other), jnp.where(core == 0, other, v)
    return jnp.concatenate([low, high], axis=0), beside


def local(features, weight, support_queue, owner_shard, slot_row, loss_weight):
    n = features.shape[0]
    width = weight.shape[1]

    core = lax.axis_index("core")
    owner = owner_shard.reshape(1, n)
    view_bf, wanted = begin(features, weight, owner, slot_row.reshape(1, n))
    views = {0: view_bf}
    views[7] = lax.ppermute(view_bf, "z", shift(NZ, 1))
    views[1] = lax.ppermute(view_bf, "z", shift(NZ, -1))
    asked = lax.all_to_all(wanted, QUEUE, split_axis=0, concat_axis=0, tiled=True)
    asked, views[7], views[1] = lax.optimization_barrier((asked, views[7], views[1]))
    views[6] = lax.ppermute(views[7], "z", shift(NZ, 1))
    views[2] = lax.ppermute(views[1], "z", shift(NZ, -1))
    picked = support_queue[asked]
    picked, views[6], views[2] = lax.optimization_barrier((picked, views[6], views[2]))
    views[5] = lax.ppermute(views[6], "z", shift(NZ, 1))
    views[3] = lax.ppermute(views[2], "z", shift(NZ, -1))
    views[4] = lax.ppermute(views[5], "z", shift(NZ, 1))
    views = [views[d] for d in range(NZ)]

    answered = lax.all_to_all(picked, QUEUE, split_axis=0, concat_axis=0, tiled=True)
    extra = jnp.zeros((16, width), BF).at[: n // width].set(loss_weight.reshape(n // width, width))
    message = pick(answered.reshape(NZ * NX * CAP, width), owner, extra)

    blocks = [message] + [lax.ppermute(message, "x", shift(NX, k)) for k in (1, 2, 3)]
    parts, totals = {}, {}
    for b in (0, 1, 3, 2):
        parts[b], totals[b] = exps(blocks[b], views)
    parts = [parts[b] for b in range(NX)]
    total = jnp.concatenate([totals[b] for b in range(NX)], axis=1)
    everyone = [total] + [lax.ppermute(total, "x", shift(NX, k)) for k in (1, 2, 3)]
    scaled = scale(blocks, everyone, n)

    (far,) = mix((4,), scaled, parts, BF)
    up, down = far[: n // 2], far[n // 2 :]
    for d in (3, 2, 1):
        up_part, down_part = mix((d, NZ - d), scaled, parts, F32)
        up = lax.ppermute(up, "z", shift(NZ, 1)).astype(F32)
        down = lax.ppermute(down, "z", shift(NZ, -1)).astype(F32)
        if d == 3:
            up = jnp.concatenate([up + up_part[: n // 2], up_part[n // 2 :]], axis=0)
            down = jnp.concatenate([down_part[: n // 2], down + down_part[n // 2 :]], axis=0)
        else:
            up, down = up + up_part, down + down_part
        up, down = up.astype(BF), down.astype(BF)
    (own,) = mix((0,), scaled, parts, F32)
    up = lax.ppermute(up, "z", shift(NZ, 1))
    down = lax.ppermute(down, "z", shift(NZ, -1))

    grad_proj, keep, send = finish(core, up, down, own, message, features, weight)
    grad_feats = jnp.dot(grad_proj, weight.T, preferred_element_type=F32).astype(BF)
    grad_weight, grad_feats = sum_everywhere(keep, send, core, grad_feats)
    return (grad_feats, grad_weight)


def solution(mesh):
    mesh = Mesh(mesh.devices.reshape(NY, NC, NZ, NX), ("y", "core", "z", "x"))
    views = ("y", "core", "z", "x")
    in_specs = (
        P(views, None),
        P(),
        P(QUEUE, None),
        P(views, None),
        P(views),
        P(views),
    )
    out_specs = (P(views, None), P())
    return jax.shard_map(local, mesh=mesh, in_specs=in_specs, out_specs=out_specs, check_vma=False)
```

time: 202 us -> 201 us (level)
  starting transfers between devices: 54.5 us -> 60.3 us
  waiting for transfers between devices: 58.2 us -> 53 us
  local copies, waits for them, and re-layouts: 25.3 us -> 20.9 us
  Pallas kernels: 13.2 us -> 16.5 us
    ppermute x1, waiting for transfers between devices: 6.25 us -> 0.01 us  [local(): up = lax.ppermute(up, 'z', shift(NZ, 1))]
    ppermute x6 -> x7, starting transfers between devices: 13.7 us -> 19.2 us  [the longest x1 9.69 us: sum_everywhere(): v = keep + lax.ppermute(send, 'core', flip(NC, 1))]
    unnamed x42 -> x29, local copies, waits for them, and re-layouts: 13.7 us -> 9.45 us
    pallas_call x2, Pallas kernels: 1.59 us -> 4.28 us  [the longest x1 2.69 us: begin(): vmem_call(begin_kernel, (jax.ShapeDtypeStruct((n, width), BF), jax.ShapeD...]
    ppermute x1, starting transfers between devices: 3.07 us -> 0.9 us  [sum_everywhere(): v = v + lax.ppermute(v, 'z', flip(NZ, 4))]
    ppermute x6 -> x7, waiting for transfers between devices: 9.59 us -> 8.71 us  [the longest x3 4.48 us: local(): up = lax.ppermute(up, 'z', shift(NZ, 1)).astype(F32)]
    pallas_call x4 -> x5, Pallas kernels: 4.97 us -> 5.14 us  [mix(): vmem_call(functools.partial(mix_kernel, which), tuple((shape for _ in whi...]
  transfers between devices with their start and end apart: 27 -> 28, of which waited for: 16 -> 16; matrix products, arithmetic and copies ran while one was open for 7% -> 7% of each run, Pallas kernels for 4% -> 5%
where the time goes in v2:
time: 201 us; the launch traced here: 200 us
  starting transfers between devices  60.3 us (30%)
  waiting for transfers between devices  53 us (26%)
  blocking collectives  45.7 us (23%)
  local copies, waits for them, and re-layouts  20.9 us (10%)
  Pallas kernels  16.5 us (8%)
    ppermute x1, waiting for transfers between devices, local(): views[5] = lax.ppermute(views[6], 'z', shift(NZ, 1))  26.8 us
    all_to_all x1, blocking collectives, sum_everywhere(): v = lax.all_to_all(v, ('y', 'x'), 0, 0, tiled=True)  16.7 us
    all_to_all x1, blocking collectives, local(): lax.all_to_all(wanted, QUEUE, split_axis=0, concat_axis=0, tiled=True)  16.6 us
    all_to_all x1, blocking collectives, sum_everywhere(): v = lax.all_to_all(v.reshape(rows, width), ('y', 'x'), 0, 0, tiled=True)  12.5 us
    gather x1, local copies, waits for them, and re-layouts, local(): picked = support_queue[asked]  11.3 us
    ppermute x1, starting transfers between devices, sum_everywhere(): v = keep + lax.ppermute(send, 'core', flip(NC, 1))  9.69 us
    unnamed x29, local copies, waits for them, and re-layouts  9.45 us
    ppermute x3, starting transfers between devices, local(): down = lax.ppermute(down, 'z', shift(NZ, -1)).astype(F32)  9.08 us
  transfers between devices with their start and end apart: 28, of which 16 were waited for; matrix products, arithmetic and copies ran while one was open for 7% of the time, Pallas kernels for 5%

profile of v2, /device:TPU:1, one launch (start us, length us, event | category | flops | bytes accessed | tf_op | source)
XLA Modules:
  0.0 200.4 jit_solution(18155971280703866327)
XLA Ops:
  0.6 2.7 %begin.1 = (bf16[512,256]{1,0:T(8,128)(2,1)}, s32[32,64]{1,0:T(8,128)}) custom-call(bf16[512,1024]{1,0:T(8,128)(2,1)} %feats_ref.1, bf16[1024,256]{1,0:T(8,128)(2,1)} %weight_ref.1, s32[1,512]{1,0:T(1,128)} %bitcast.16, s32[1,512]{1,0:T(1,128)} %bitcast.23), custom_call_target="tpu_custom_call" | custom-call | tf_op jit(solution)/shard_map/begin/pallas_call | solution.py:100
  3.3 2.5 %collective-permute-start = (bf16[512,256]{1,0:T(8,128)(2,1)}, bf16[512,256]{1,0:T(8,128)(2,1)S(1)}, u32[]{:S(2)}, u32[]{:S(2)}) collective-permute-start(bf16[512,256]{1,0:T(8,128)(2,1)} %get-tuple-element.42.refs_0_), channel_id=1, source_target_pairs={{0,4},{4,8},{8,12},{12,16},{16,20},{20,24},{24,28},{28,0},{1,5},{5... | collective-permute-start | bytes 786440 | tf_op jit(solution)/shard_map/ppermute | solution.py:296
  5.9 4.0 %collective-permute-start.1 = (bf16[512,256]{1,0:T(8,128)(2,1)}, bf16[512,256]{1,0:T(8,128)(2,1)S(1)}, u32[]{:S(2)}, u32[]{:S(2)}) collective-permute-start(bf16[512,256]{1,0:T(8,128)(2,1)} %get-tuple-element.42.refs_0_), channel_id=1, source_target_pairs={{0,28},{4,0},{8,4},{12,8},{16,12},{20,16},{24,20},{28,24},{1,29},{... | collective-permute-start | bytes 786440 | tf_op jit(solution)/shard_map/ppermute | solution.py:297
  9.9 16.6 %all_to_all.35 = s32[32,1,64]{2,1,0:T(1,128)S(1)} all-to-all(s32[32,1,64]{2,1,0:T(1,128)} %bitcast.22), channel_id=1, replica_groups=mesh['y'=4,'core'=2,'z'=8,'x'=4] {'z','x'}, dimensions={0} | all-to-all | bytes 16384 | tf_op jit(solution)/shard_map/all_to_all | solution.py:298
  26.8 2.3 %collective-permute-start.3 = (bf16[512,256]{1,0:T(8,128)(2,1)S(1)}, bf16[512,256]{1,0:T(8,128)(2,1)S(1)}, u32[]{:S(2)}, u32[]{:S(2)}) collective-permute-start(bf16[512,256]{1,0:T(8,128)(2,1)S(1)} %collective-permute-done.1.refs_1_), channel_id=1, source_target_pairs={{0,28},{4,0},{8,4},{12,8},{16,12},{20,16},{24,20},{28,24},{1,29},{... | collective-permute-start | bytes 786440 | tf_op jit(solution)/shard_map/ppermute | solution.py:301
  29.2 11.3 %gather_fusion = bf16[2048,256]{1,0:T(8,128)(2,1)} fusion(bf16[8192,256]{1,0:T(8,128)(2,1)} %param.10, s32[2048]{0:T(1024)S(1)} %broadcast_clamp_fusion), kind=kCustom, calls=%fused_computation | custom fusion | bytes 2105344 | tf_op jit(solution)/shard_map/gather | solution.py:302
  40.5 3.9 %all-to-all-start.1 = ((bf16[32,64,256]{2,1,0:T(8,128)(2,1)}), bf16[32,64,256]{2,1,0:T(8,128)(2,1)S(1)}, u32[]{:S(2)}, u32[]{:S(2)}) async-start(bf16[32,64,256]{2,1,0:T(8,128)(2,1)} %bitcast.18), calls=%async_computation.1 | async-start | bytes 2097152 | tf_op jit(solution)/shard_map/all_to_all | solution.py:309
  47.2 26.8 %collective-permute-done.8.refs_5_ = bf16[512,256]{1,0:T(8,128)(2,1)S(1)} collective-permute-done((bf16[512,256]{1,0:T(8,128)(2,1)S(1)}, bf16[512,256]{1,0:T(8,128)(2,1)S(1)}, u32[]{:S(2)}, u32[]{:S(2)}) %collective-permute-start.8) | collective-permute-done | bytes 262176 | tf_op jit(solution)/shard_map/ppermute | solution.py:304
  75.4 2.7 %collective-permute-start.5 = (bf16[528,256]{1,0:T(8,128)(2,1)S(1)}, bf16[528,256]{1,0:T(8,128)(2,1)S(1)}, u32[]{:S(2)}, u32[]{:S(2)}) collective-permute-start(bf16[528,256]{1,0:T(8,128)(2,1)S(1)} %pick.1.a_ref.refs_0_.message_ref), channel_id=1, source_target_pairs={{0,2},{1,3},{2,0},{3,1},{4,6},{5,7},{6,4},{7,5},{8,10},{9,11},{10,... | collective-permute-start | bytes 811016 | tf_op jit(solution)/shard_map/ppermute | solution.py:313
  78.5 2.3 %collective-permute-start.6 = (bf16[528,256]{1,0:T(8,128)(2,1)S(1)}, bf16[528,256]{1,0:T(8,128)(2,1)S(1)}, u32[]{:S(2)}, u32[]{:S(2)}) collective-permute-start(bf16[528,256]{1,0:T(8,128)(2,1)S(1)} %pick.1.a_ref.refs_0_.message_ref), channel_id=1, source_target_pairs={{0,3},{1,0},{2,1},{3,2},{4,7},{5,4},{6,5},{7,6},{8,11},{9,8},{10,9... | collective-permute-start | bytes 811016 | tf_op jit(solution)/shard_map/ppermute | solution.py:313
  83.7 5.9 %collective-permute-done.4.a_ref.refs_1_ = bf16[528,256]{1,0:T(8,128)(2,1)S(1)} collective-permute-done((bf16[528,256]{1,0:T(8,128)(2,1)S(1)}, bf16[528,256]{1,0:T(8,128)(2,1)S(1)}, u32[]{:S(2)}, u32[]{:S(2)}) %collective-permute-start.4) | collective-permute-done | bytes 270368 | tf_op jit(solution)/shard_map/ppermute | solution.py:313
  93.2 1.8 collective-permute-start.11
  94.9 2.0 collective-permute-start.12
  99.1 2.7 %collective-permute-start.17 = (bf16[256,256]{1,0:T(8,128)(2,1)S(1)}, bf16[256,256]{1,0:T(8,128)(2,1)S(1)}, u32[]{:S(2)}, u32[]{:S(2)}) collective-permute-start(bf16[256,256]{1,0:T(8,128)(2,1)S(1)} %get-tuple-element.70), channel_id=1, source_target_pairs={{0,28},{4,0},{8,4},{12,8},{16,12},{20,16},{24,20},{28,24},{1,29},{... | collective-permute-start | bytes 393224 | tf_op jit(solution)/shard_map/ppermute | solution.py:327
  103.9 3.2 %collective-permute-start.18 = (bf16[512,256]{1,0:T(8,128)(2,1)S(1)}, bf16[512,256]{1,0:T(8,128)(2,1)S(1)}, u32[]{:S(2)}, u32[]{:S(2)}) collective-permute-start(bf16[512,256]{1,0:T(8,128)(2,1)S(1)} %pad_maximum_fusion.2), channel_id=1, source_target_pairs={{0,28},{4,0},{8,4},{12,8},{16,12},{20,16},{24,20},{28,24},{1,29},{... | collective-permute-start | bytes 786440 | tf_op jit(solution)/shard_map/ppermute | solution.py:327
  110.5 3.2 %collective-permute-start.19 = (bf16[512,256]{1,0:T(8,128)(2,1)S(1)}, bf16[512,256]{1,0:T(8,128)(2,1)S(1)}, u32[]{:S(2)}, u32[]{:S(2)}) collective-permute-start(bf16[512,256]{1,0:T(8,128)(2,1)S(1)} %add_convert_fusion.1), channel_id=1, source_target_pairs={{0,28},{4,0},{8,4},{12,8},{16,12},{20,16},{24,20},{28,24},{1,29},{... | collective-permute-start | bytes 786440 | tf_op jit(solution)/shard_map/ppermute | solution.py:327
  116.6 1.6 collective-permute-done.19
  118.2 3.2 %collective-permute-start.20 = (bf16[512,256]{1,0:T(8,128)(2,1)S(1)}, bf16[512,256]{1,0:T(8,128)(2,1)S(1)}, u32[]{:S(2)}, u32[]{:S(2)}) collective-permute-start(bf16[512,256]{1,0:T(8,128)(2,1)S(1)} %add_convert_fusion), channel_id=1, source_target_pairs={{0,28},{4,0},{8,4},{12,8},{16,12},{20,16},{24,20},{28,24},{1,29},{... | collective-permute-start | bytes 786440 | tf_op jit(solution)/shard_map/ppermute | solution.py:336
  121.4 1.8 collective-permute-done.15
  123.4 2.2 %copy-done.1 = bf16[8,512,512]{2,1,0:T(8,128)(2,1)S(1)} copy-done((bf16[8,512,512]{2,1,0:T(8,128)(2,1)S(1)}, bf16[8,512,512]{2,1,0:T(8,128)(2,1)}, u32[]{:S(2)}) %copy-start.1) | copy-done | bytes 4194328
  125.5 2.2 %copy-done.3 = bf16[8,512,512]{2,1,0:T(8,128)(2,1)S(1)} copy-done((bf16[8,512,512]{2,1,0:T(8,128)(2,1)S(1)}, bf16[8,512,512]{2,1,0:T(8,128)(2,1)}, u32[]{:S(2)}) %copy-start.3) | copy-done | bytes 4194328
  127.7 2.2 %copy-done.5 = bf16[8,512,512]{2,1,0:T(8,128)(2,1)S(1)} copy-done((bf16[8,512,512]{2,1,0:T(8,128)(2,1)S(1)}, bf16[8,512,512]{2,1,0:T(8,128)(2,1)}, u32[]{:S(2)}) %copy-start.5) | copy-done | bytes 4194328
  129.9 2.2 %copy-done.7 = bf16[8,512,512]{2,1,0:T(8,128)(2,1)S(1)} copy-done((bf16[8,512,512]{2,1,0:T(8,128)(2,1)S(1)}, bf16[8,512,512]{2,1,0:T(8,128)(2,1)}, u32[]{:S(2)}) %copy-start.7) | copy-done | bytes 4194328
  133.5 1.6 finish.1
  135.1 9.7 %collective-permute-start.21 = (f32[512,256]{1,0:T(8,128)S(1)}, f32[512,256]{1,0:T(8,128)S(1)}, u32[]{:S(2)}, u32[]{:S(2)}) collective-permute-start(f32[512,256]{1,0:T(8,128)S(1)} %get-tuple-element.64), channel_id=1, source_target_pairs={{0,32},{32,0},{1,33},{33,1},{2,34},{34,2},{3,35},{35,3},{4,36},{36... | collective-permute-start | bytes 1572872 | tf_op jit(solution)/shard_map/ppermute | solution.py:273
  146.4 16.7 %all_to_all.36 = f32[16,32,256]{2,1,0:T(8,128)S(1)} all-to-all(f32[16,32,256]{2,1,0:T(8,128)S(1)} %bitcast.20), channel_id=1, replica_groups=mesh['y'=4,'core'=2,'z'=8,'x'=4] {'y','x'}, dimensions={0} | all-to-all | bytes 1048576 | tf_op jit(solution)/shard_map/all_to_all | solution.py:275
  163.2 5.5 %collective-permute-start.23 = (f32[32,256]{1,0:T(8,128)S(1)}, f32[32,256]{1,0:T(8,128)S(1)}, u32[]{:S(2)}, u32[]{:S(2)}) collective-permute-start(f32[32,256]{1,0:T(8,128)S(1)} %reduce_sum.9), channel_id=1, source_target_pairs={{0,8},{4,12},{8,0},{12,4},{16,24},{20,28},{24,16},{28,20},{1,9},{5... | collective-permute-start | bytes 98312 | tf_op jit(solution)/shard_map/ppermute | solution.py:277
  168.7 1.6 collective-permute-done.23
  170.3 2.9 %collective-permute-done.24 = f32[32,256]{1,0:T(8,128)S(1)} collective-permute-done((f32[32,256]{1,0:T(8,128)S(1)}, f32[32,256]{1,0:T(8,128)S(1)}, u32[]{:S(2)}, u32[]{:S(2)}) %collective-permute-start.24) | collective-permute-done | bytes 32800 | tf_op jit(solution)/shard_map/ppermute | solution.py:277
  175.6 4.4 %collective-permute-done.25 = f32[32,256]{1,0:T(8,128)S(1)} collective-permute-done((f32[32,256]{1,0:T(8,128)S(1)}, f32[32,256]{1,0:T(8,128)S(1)}, u32[]{:S(2)}, u32[]{:S(2)}) %collective-permute-start.25) | collective-permute-done | bytes 32800 | tf_op jit(solution)/shard_map/ppermute | solution.py:279
  180.1 12.5 %all_to_all.37 = f32[16,32,256]{2,1,0:T(8,128)S(1)} all-to-all(f32[16,32,256]{2,1,0:T(8,128)S(1)} %broadcast_in_dim.5), channel_id=1, replica_groups=mesh['y'=4,'core'=2,'z'=8,'x'=4] {'y','x'}, dimensions={0} | all-to-all | bytes 1048576 | tf_op jit(solution)/shard_map/all_to_all | solution.py:282
  192.6 5.2 %collective-permute-start.26 = (f32[512,256]{1,0:T(8,128)S(1)}, f32[512,256]{1,0:T(8,128)S(1)}, u32[]{:S(2)}, u32[]{:S(2)}) collective-permute-start(f32[512,256]{1,0:T(8,128)S(1)} %bitcast.19), channel_id=1, source_target_pairs={{0,32},{32,0},{1,33},{33,1},{2,34},{34,2},{3,35},{35,3},{4,36},{36... | collective-permute-start | bytes 1572872 | tf_op jit(solution)/shard_map/ppermute | solution.py:283
  (95 shorter events, 30.1 us)
Async XLA Ops:
  3.3 23.1 %collective-permute-start = (bf16[512,256]{1,0:T(8,128)(2,1)}, bf16[512,256]{1,0:T(8,128)(2,1)S(1)}, u32[]{:S(2)}, u32[]{:S(2)}) collective-permute-start(bf16[512,256]{1,0:T(8,128)(2,1)} %get-tuple-element.42.refs_0_), channel_id=1, source_target_pairs={{0,4},{4,8},{8,12},{12,16},{16,20},{20,24},{24,28},{28,0},{1,5},{5... | collective-permute-start | bytes 786440 | tf_op jit(solution)/shard_map/ppermute | solution.py:296
  5.9 20.6 %collective-permute-start.1 = (bf16[512,256]{1,0:T(8,128)(2,1)}, bf16[512,256]{1,0:T(8,128)(2,1)S(1)}, u32[]{:S(2)}, u32[]{:S(2)}) collective-permute-start(bf16[512,256]{1,0:T(8,128)(2,1)} %get-tuple-element.42.refs_0_), channel_id=1, source_target_pairs={{0,28},{4,0},{8,4},{12,8},{16,12},{20,16},{24,20},{28,24},{1,29},{... | collective-permute-start | bytes 786440 | tf_op jit(solution)/shard_map/ppermute | solution.py:297
  26.5 14.1 %collective-permute-start.2 = (bf16[512,256]{1,0:T(8,128)(2,1)S(1)}, bf16[512,256]{1,0:T(8,128)(2,1)S(1)}, u32[]{:S(2)}, u32[]{:S(2)}) collective-permute-start(bf16[512,256]{1,0:T(8,128)(2,1)S(1)} %collective-permute-done.refs_7_), channel_id=1, source_target_pairs={{0,4},{4,8},{8,12},{12,16},{16,20},{20,24},{24,28},{28,0},{1,5},{5... | collective-permute-start | bytes 786440 | tf_op jit(solution)/shard_map/ppermute | solution.py:300
  26.8 13.7 %collective-permute-start.3 = (bf16[512,256]{1,0:T(8,128)(2,1)S(1)}, bf16[512,256]{1,0:T(8,128)(2,1)S(1)}, u32[]{:S(2)}, u32[]{:S(2)}) collective-permute-start(bf16[512,256]{1,0:T(8,128)(2,1)S(1)} %collective-permute-done.1.refs_1_), channel_id=1, source_target_pairs={{0,28},{4,0},{8,4},{12,8},{16,12},{20,16},{24,20},{28,24},{1,29},{... | collective-permute-start | bytes 786440 | tf_op jit(solution)/shard_map/ppermute | solution.py:301
  29.2 44.8 %copy-start.12 = (bf16[512]{0:T(512)(128)(2,1)S(1)}, bf16[512]{0:T(512)(128)(2,1)}, u32[]{:S(2)}) copy-start(bf16[512]{0:T(512)(128)(2,1)} %param.13) | copy-start | bytes 3076
  29.2 44.9 %copy-start.11 = (s32[512,1]{0,1:T(1,128)S(1)}, s32[512,1]{0,1:T(1,128)}, u32[]{:S(2)}) copy-start(s32[512,1]{0,1:T(1,128)} %param.11) | copy-start | bytes 6148
  29.2 51.6 %copy-start.9 = (bf16[512,256]{1,0:T(8,128)(2,1)S(1)}, bf16[512,256]{1,0:T(8,128)(2,1)}, u32[]{:S(2)}) copy-start(bf16[512,256]{1,0:T(8,128)(2,1)} %get-tuple-element.42.refs_0_) | copy-start | bytes 786436
  40.5 33.6 %all-to-all-start.1 = ((bf16[32,64,256]{2,1,0:T(8,128)(2,1)}), bf16[32,64,256]{2,1,0:T(8,128)(2,1)S(1)}, u32[]{:S(2)}, u32[]{:S(2)}) async-start(bf16[32,64,256]{2,1,0:T(8,128)(2,1)} %bitcast.18), calls=%async_computation.1 | async-start | bytes 2097152 | tf_op jit(solution)/shard_map/all_to_all | solution.py:309
  44.5 29.6 %collective-permute-start.8 = (bf16[512,256]{1,0:T(8,128)(2,1)S(1)}, bf16[512,256]{1,0:T(8,128)(2,1)S(1)}, u32[]{:S(2)}, u32[]{:S(2)}) collective-permute-start(bf16[512,256]{1,0:T(8,128)(2,1)S(1)} %collective-permute-done.2.refs_6_), channel_id=1, source_target_pairs={{0,4},{4,8},{8,12},{12,16},{16,20},{20,24},{24,28},{28,0},{1,5},{5... | collective-permute-start | bytes 786440 | tf_op jit(solution)/shard_map/ppermute | solution.py:304
  45.7 35.1 %collective-permute-start.7 = (bf16[512,256]{1,0:T(8,128)(2,1)S(1)}, bf16[512,256]{1,0:T(8,128)(2,1)S(1)}, u32[]{:S(2)}, u32[]{:S(2)}) collective-permute-start(bf16[512,256]{1,0:T(8,128)(2,1)S(1)} %collective-permute-done.3.refs_2_), channel_id=1, source_target_pairs={{0,28},{4,0},{8,4},{12,8},{16,12},{20,16},{24,20},{28,24},{1,29},{... | collective-permute-start | bytes 786440 | tf_op jit(solution)/shard_map/ppermute | solution.py:305
  74.1 6.8 %collective-permute-start.9 = (bf16[512,256]{1,0:T(8,128)(2,1)S(1)}, bf16[512,256]{1,0:T(8,128)(2,1)S(1)}, u32[]{:S(2)}, u32[]{:S(2)}) collective-permute-start(bf16[512,256]{1,0:T(8,128)(2,1)S(1)} %collective-permute-done.8.refs_5_), channel_id=1, source_target_pairs={{0,4},{4,8},{8,12},{12,16},{16,20},{20,24},{24,28},{28,0},{1,5},{5... | collective-permute-start | bytes 786440 | tf_op jit(solution)/shard_map/ppermute | solution.py:306
  75.4 7.0 %collective-permute-start.5 = (bf16[528,256]{1,0:T(8,128)(2,1)S(1)}, bf16[528,256]{1,0:T(8,128)(2,1)S(1)}, u32[]{:S(2)}, u32[]{:S(2)}) collective-permute-start(bf16[528,256]{1,0:T(8,128)(2,1)S(1)} %pick.1.a_ref.refs_0_.message_ref), channel_id=1, source_target_pairs={{0,2},{1,3},{2,0},{3,1},{4,6},{5,7},{6,4},{7,5},{8,10},{9,11},{10,... | collective-permute-start | bytes 811016 | tf_op jit(solution)/shard_map/ppermute | solution.py:313
  78.1 11.4 %collective-permute-start.4 = (bf16[528,256]{1,0:T(8,128)(2,1)S(1)}, bf16[528,256]{1,0:T(8,128)(2,1)S(1)}, u32[]{:S(2)}, u32[]{:S(2)}) collective-permute-start(bf16[528,256]{1,0:T(8,128)(2,1)S(1)} %pick.1.a_ref.refs_0_.message_ref), channel_id=1, source_target_pairs={{0,1},{1,2},{2,3},{3,0},{4,5},{5,6},{6,7},{7,4},{8,9},{9,10},{10,1... | collective-permute-start | bytes 811016 | tf_op jit(solution)/shard_map/ppermute | solution.py:313
  78.5 12.4 %collective-permute-start.6 = (bf16[528,256]{1,0:T(8,128)(2,1)S(1)}, bf16[528,256]{1,0:T(8,128)(2,1)S(1)}, u32[]{:S(2)}, u32[]{:S(2)}) collective-permute-start(bf16[528,256]{1,0:T(8,128)(2,1)S(1)} %pick.1.a_ref.refs_0_.message_ref), channel_id=1, source_target_pairs={{0,3},{1,0},{2,1},{3,2},{4,7},{5,4},{6,5},{7,6},{8,11},{9,8},{10,9... | collective-permute-start | bytes 811016 | tf_op jit(solution)/shard_map/ppermute | solution.py:313
  82.1 33.2 %copy-start = (bf16[8,512,512]{2,1,0:T(8,128)(2,1)}, bf16[8,512,512]{2,1,0:T(8,128)(2,1)S(1)}, u32[]{:S(2)}) copy-start(bf16[8,512,512]{2,1,0:T(8,128)(2,1)S(1)} %get-tuple-element.53.refs_0_) | copy-start | bytes 12582916
  92.2 4.7 %collective-permute-start.10 = (f32[1,2048]{1,0:T(1,128)S(1)}, f32[1,2048]{1,0:T(1,128)S(1)}, u32[]{:S(2)}, u32[]{:S(2)}) collective-permute-start(f32[1,2048]{1,0:T(1,128)S(1)} %constant_dynamic-update-slice_fusion.refs_4_), channel_id=1, source_target_pairs={{0,1},{1,2},{2,3},{3,0},{4,5},{5,6},{6,7},{7,4},{8,9},{9,10},{10,1... | collective-permute-start | bytes 24584 | tf_op jit(solution)/shard_map/ppermute | solution.py:319
  93.2 4.0 %collective-permute-start.11 = (f32[1,2048]{1,0:T(1,128)S(1)}, f32[1,2048]{1,0:T(1,128)S(1)}, u32[]{:S(2)}, u32[]{:S(2)}) collective-permute-start(f32[1,2048]{1,0:T(1,128)S(1)} %constant_dynamic-update-slice_fusion.refs_4_), channel_id=1, source_target_pairs={{0,2},{1,3},{2,0},{3,1},{4,6},{5,7},{6,4},{7,5},{8,10},{9,11},{10,... | collective-permute-start | bytes 24584 | tf_op jit(solution)/shard_map/ppermute | solution.py:319
  94.9 2.8 %collective-permute-start.12 = (f32[1,2048]{1,0:T(1,128)S(1)}, f32[1,2048]{1,0:T(1,128)S(1)}, u32[]{:S(2)}, u32[]{:S(2)}) collective-permute-start(f32[1,2048]{1,0:T(1,128)S(1)} %constant_dynamic-update-slice_fusion.refs_4_), channel_id=1, source_target_pairs={{0,3},{1,0},{2,1},{3,2},{4,7},{5,4},{6,5},{7,6},{8,11},{9,8},{10,9... | collective-permute-start | bytes 24584 | tf_op jit(solution)/shard_map/ppermute | solution.py:319
  99.1 4.7 %collective-permute-start.17 = (bf16[256,256]{1,0:T(8,128)(2,1)S(1)}, bf16[256,256]{1,0:T(8,128)(2,1)S(1)}, u32[]{:S(2)}, u32[]{:S(2)}) collective-permute-start(bf16[256,256]{1,0:T(8,128)(2,1)S(1)} %get-tuple-element.70), channel_id=1, source_target_pairs={{0,28},{4,0},{8,4},{12,8},{16,12},{20,16},{24,20},{28,24},{1,29},{... | collective-permute-start | bytes 393224 | tf_op jit(solution)/shard_map/ppermute | solution.py:327
  103.1 5.1 %collective-permute-start.13 = (bf16[256,256]{1,0:T(8,128)(2,1)S(1)}, bf16[256,256]{1,0:T(8,128)(2,1)S(1)}, u32[]{:S(2)}, u32[]{:S(2)}) collective-permute-start(bf16[256,256]{1,0:T(8,128)(2,1)S(1)} %get-tuple-element.71), channel_id=1, source_target_pairs={{0,4},{4,8},{8,12},{12,16},{16,20},{20,24},{24,28},{28,0},{1,5},{5... | collective-permute-start | bytes 393224 | tf_op jit(solution)/shard_map/ppermute | solution.py:326
  103.9 6.6 %collective-permute-start.18 = (bf16[512,256]{1,0:T(8,128)(2,1)S(1)}, bf16[512,256]{1,0:T(8,128)(2,1)S(1)}, u32[]{:S(2)}, u32[]{:S(2)}) collective-permute-start(bf16[512,256]{1,0:T(8,128)(2,1)S(1)} %pad_maximum_fusion.2), channel_id=1, source_target_pairs={{0,28},{4,0},{8,4},{12,8},{16,12},{20,16},{24,20},{28,24},{1,29},{... | collective-permute-start | bytes 786440 | tf_op jit(solution)/shard_map/ppermute | solution.py:327
  108.3 6.9 %collective-permute-start.14 = (bf16[512,256]{1,0:T(8,128)(2,1)S(1)}, bf16[512,256]{1,0:T(8,128)(2,1)S(1)}, u32[]{:S(2)}, u32[]{:S(2)}) collective-permute-start(bf16[512,256]{1,0:T(8,128)(2,1)S(1)} %pad_maximum_fusion.1), channel_id=1, source_target_pairs={{0,4},{4,8},{8,12},{12,16},{16,20},{20,24},{24,28},{28,0},{1,5},{5... | collective-permute-start | bytes 786440 | tf_op jit(solution)/shard_map/ppermute | solution.py:326
  110.5 7.7 %collective-permute-start.19 = (bf16[512,256]{1,0:T(8,128)(2,1)S(1)}, bf16[512,256]{1,0:T(8,128)(2,1)S(1)}, u32[]{:S(2)}, u32[]{:S(2)}) collective-permute-start(bf16[512,256]{1,0:T(8,128)(2,1)S(1)} %add_convert_fusion.1), channel_id=1, source_target_pairs={{0,28},{4,0},{8,4},{12,8},{16,12},{20,16},{24,20},{28,24},{1,29},{... | collective-permute-start | bytes 786440 | tf_op jit(solution)/shard_map/ppermute | solution.py:327
  115.2 8.0 %collective-permute-start.15 = (bf16[512,256]{1,0:T(8,128)(2,1)S(1)}, bf16[512,256]{1,0:T(8,128)(2,1)S(1)}, u32[]{:S(2)}, u32[]{:S(2)}) collective-permute-start(bf16[512,256]{1,0:T(8,128)(2,1)S(1)} %add_convert_fusion.3), channel_id=1, source_target_pairs={{0,4},{4,8},{8,12},{12,16},{16,20},{20,24},{24,28},{28,0},{1,5},{5... | collective-permute-start | bytes 786440 | tf_op jit(solution)/shard_map/ppermute | solution.py:326
  118.2 14.6 %collective-permute-start.20 = (bf16[512,256]{1,0:T(8,128)(2,1)S(1)}, bf16[512,256]{1,0:T(8,128)(2,1)S(1)}, u32[]{:S(2)}, u32[]{:S(2)}) collective-permute-start(bf16[512,256]{1,0:T(8,128)(2,1)S(1)} %add_convert_fusion), channel_id=1, source_target_pairs={{0,28},{4,0},{8,4},{12,8},{16,12},{20,16},{24,20},{28,24},{1,29},{... | collective-permute-start | bytes 786440 | tf_op jit(solution)/shard_map/ppermute | solution.py:336
  123.2 9.6 %collective-permute-start.16 = (bf16[512,256]{1,0:T(8,128)(2,1)S(1)}, bf16[512,256]{1,0:T(8,128)(2,1)S(1)}, u32[]{:S(2)}, u32[]{:S(2)}) collective-permute-start(bf16[512,256]{1,0:T(8,128)(2,1)S(1)} %add_convert_fusion.2), channel_id=1, source_target_pairs={{0,4},{4,8},{8,12},{12,16},{16,20},{20,24},{24,28},{28,0},{1,5},{5... | collective-permute-start | bytes 786440 | tf_op jit(solution)/shard_map/ppermute | solution.py:335
  135.1 11.2 %collective-permute-start.21 = (f32[512,256]{1,0:T(8,128)S(1)}, f32[512,256]{1,0:T(8,128)S(1)}, u32[]{:S(2)}, u32[]{:S(2)}) collective-permute-start(f32[512,256]{1,0:T(8,128)S(1)} %get-tuple-element.64), channel_id=1, source_target_pairs={{0,32},{32,0},{1,33},{33,1},{2,34},{34,2},{3,35},{35,3},{4,36},{36... | collective-permute-start | bytes 1572872 | tf_op jit(solution)/shard_map/ppermute | solution.py:273
  163.1 5.6 %collective-permute-start.22 = (f32[32,256]{1,0:T(8,128)S(1)}, f32[32,256]{1,0:T(8,128)S(1)}, u32[]{:S(2)}, u32[]{:S(2)}) collective-permute-start(f32[32,256]{1,0:T(8,128)S(1)} %reduce_sum.9), channel_id=1, source_target_pairs={{0,4},{4,0},{8,12},{12,8},{16,20},{20,16},{24,28},{28,24},{1,5},{5... | collective-permute-start | bytes 98312 | tf_op jit(solution)/shard_map/ppermute | solution.py:277
  163.2 7.1 %collective-permute-start.23 = (f32[32,256]{1,0:T(8,128)S(1)}, f32[32,256]{1,0:T(8,128)S(1)}, u32[]{:S(2)}, u32[]{:S(2)}) collective-permute-start(f32[32,256]{1,0:T(8,128)S(1)} %reduce_sum.9), channel_id=1, source_target_pairs={{0,8},{4,12},{8,0},{12,4},{16,24},{20,28},{24,16},{28,20},{1,9},{5... | collective-permute-start | bytes 98312 | tf_op jit(solution)/shard_map/ppermute | solution.py:277
  168.7 4.6 %collective-permute-start.24 = (f32[32,256]{1,0:T(8,128)S(1)}, f32[32,256]{1,0:T(8,128)S(1)}, u32[]{:S(2)}, u32[]{:S(2)}) collective-permute-start(f32[32,256]{1,0:T(8,128)S(1)} %reduce_sum.9), channel_id=1, source_target_pairs={{0,12},{4,8},{8,4},{12,0},{16,28},{20,24},{24,20},{28,16},{1,13},{... | collective-permute-start | bytes 98312 | tf_op jit(solution)/shard_map/ppermute | solution.py:277
  173.2 6.8 %collective-permute-start.25 = (f32[32,256]{1,0:T(8,128)S(1)}, f32[32,256]{1,0:T(8,128)S(1)}, u32[]{:S(2)}, u32[]{:S(2)}) collective-permute-start(f32[32,256]{1,0:T(8,128)S(1)} %add_add_fusion), channel_id=1, source_target_pairs={{0,16},{4,20},{8,24},{12,28},{16,0},{20,4},{24,8},{28,12},{1,17},{... | collective-permute-start | bytes 98312 | tf_op jit(solution)/shard_map/ppermute | solution.py:279
  192.6 6.8 %collective-permute-start.26 = (f32[512,256]{1,0:T(8,128)S(1)}, f32[512,256]{1,0:T(8,128)S(1)}, u32[]{:S(2)}, u32[]{:S(2)}) collective-permute-start(f32[512,256]{1,0:T(8,128)S(1)} %bitcast.19), channel_id=1, source_target_pairs={{0,32},{32,0},{1,33},{33,1},{2,34},{34,2},{3,35},{35,3},{4,36},{36... | collective-permute-start | bytes 1572872 | tf_op jit(solution)/shard_map/ppermute | solution.py:283
  (9 other events, 90.5 us)

commit v3 on v2

--- a/solution.py
+++ b/solution.py
@@ -121,30 +121,36 @@
     return jnp.broadcast_to(row, (8, row.shape[1])).T[:, :1]
 
 
-def pick_kernel(rows_ref, owner_ref, extra_ref, out_ref):
+def pick_kernel(first_ref, second_ref, owner_ref, extra_ref, out_ref):
     n = owner_ref.shape[1]
+    half = CAP // 2
+    slots = first_ref.shape[0]
     owner = owner_ref[...]
-    places = column_of(owner * CAP + ranks(owner, rows_ref.shape[0] // CAP)[1])
+    rank = ranks(owner, slots // half)[1]
+    late = rank >= half
+    places = owner * half + jnp.where(late, slots + rank - half, rank)
+    places = column_of(places)
     column = lax.broadcasted_iota(jnp.int32, (n, n), 1)
     total = None
-    for at in range(0, rows_ref.shape[0], n):
-        onehot = jnp.where(places == column + at, 1.0, 0.0).astype(BF)
-        term = jnp.dot(onehot, rows_ref[at : at + n, :], preferred_element_type=F32)
-        total = term if total is None else total + term
+    for k, rows_ref in enumerate((first_ref, second_ref)):
+        for at in range(0, slots, n):
+            onehot = jnp.where(places == column + (k * slots + at), 1.0, 0.0).astype(BF)
+            term = jnp.dot(onehot, rows_ref[at : at + n, :], preferred_element_type=F32)
+            total = term if total is None else total + term
     unit = total * lax.rsqrt(jnp.sum(total * total, axis=1, keepdims=True) + EPSILON)
     out_ref[:n, :] = unit.astype(BF)
     out_ref[n:, :] = extra_ref[...]
 
 
-def pick(rows, owner, extra):
+def pick(first, second, owner, extra):
     n = owner.shape[1]
     return vmem_call(
         pick_kernel,
-        jax.ShapeDtypeStruct((n + extra.shape[0], rows.shape[1]), BF),
+        jax.ShapeDtypeStruct((n + extra.shape[0], first.shape[1]), BF),
         "pick",
-        in_specs=[IN_VMEM] * 3,
+        in_specs=[IN_VMEM] * 4,
         out_specs=IN_VMEM,
-    )(rows, owner, extra)
+    )(first, second, owner, extra)
 
 
 def exps_kernel(a_ref, *refs):
@@ -299,16 +305,19 @@
     asked, views[7], views[1] = lax.optimization_barrier((asked, views[7], views[1]))
     views[6] = lax.ppermute(views[7], "z", shift(NZ, 1))
     views[2] = lax.ppermute(views[1], "z", shift(NZ, -1))
-    picked = support_queue[asked]
-    picked, views[6], views[2] = lax.optimization_barrier((picked, views[6], views[2]))
+    first = support_queue[asked[:, : CAP // 2]]
+    first, views[6], views[2] = lax.optimization_barrier((first, views[6], views[2]))
+    first = lax.all_to_all(first, QUEUE, split_axis=0, concat_axis=0, tiled=True)
+    second = support_queue[asked[:, CAP // 2 :]]
+    second = lax.all_to_all(second, QUEUE, split_axis=0, concat_axis=0, tiled=True)
     views[5] = lax.ppermute(views[6], "z", shift(NZ, 1))
     views[3] = lax.ppermute(views[2], "z", shift(NZ, -1))
     views[4] = lax.ppermute(views[5], "z", shift(NZ, 1))
     views = [views[d] for d in range(NZ)]
 
-    answered = lax.all_to_all(picked, QUEUE, split_axis=0, concat_axis=0, tiled=True)
     extra = jnp.zeros((16, width), BF).at[: n // width].set(loss_weight.reshape(n // width, width))
-    message = pick(answered.reshape(NZ * NX * CAP, width), owner, extra)
+    slots = NZ * NX * CAP // 2
+    message = pick(first.reshape(slots, width), second.reshape(slots, width), owner, extra)
 
     blocks = [message] + [lax.ppermute(message, "x", shift(NX, k)) for k in (1, 2, 3)]
     parts, totals = {}, {}
@@ -322,7 +331,8 @@
     (far,) = mix((4,), scaled, parts, BF)
     up, down = far[: n // 2], far[n // 2 :]
     for d in (3, 2, 1):
-        up_part, down_part = mix((d, NZ - d), scaled, parts, F32)
+        which = (d, NZ - d) if d > 1 else (d, NZ - d, 0)
+        up_part, down_part, *rest = mix(which, scaled, parts, F32)
         up = lax.ppermute(up, "z", shift(NZ, 1)).astype(F32)
         down = lax.ppermute(down, "z", shift(NZ, -1)).astype(F32)
         if d == 3:
@@ -331,7 +341,7 @@
         else:
             up, down = up + up_part, down + down_part
         up, down = up.astype(BF), down.astype(BF)
-    (own,) = mix((0,), scaled, parts, F32)
+    (own,) = rest
     up = lax.ppermute(up, "z", shift(NZ, 1))
     down = lax.ppermute(down, "z", shift(NZ, -1))
 

time: 201 us -> 203 us (level)
  starting transfers between devices: 60.3 us -> 66.2 us
  local copies, waits for them, and re-layouts: 20.9 us -> 15 us
  waiting for transfers between devices: 53 us -> 55.2 us
    ppermute x1, waiting for transfers between devices: 26.8 us -> 16.5 us  [local(): views[5] = lax.ppermute(views[6], 'z', shift(NZ, 1))]
    unnamed x29 -> x13, local copies, waits for them, and re-layouts: 9.45 us -> 0.04 us
    ppermute x1, waiting for transfers between devices: 0.01 us -> 8.65 us  [local(): views[6] = lax.ppermute(views[7], 'z', shift(NZ, 1))]
    all_to_all x1 -> x2, starting transfers between devices: 3.94 us -> 11.8 us  [the longest x1 7.79 us: local(): lax.all_to_all(first, QUEUE, split_axis=0, concat_axis=0, tiled=True)]
    ppermute x1, waiting for transfers between devices: 0.01 us -> 5.24 us  [local(): up = lax.ppermute(up, 'z', shift(NZ, 1))]
    ppermute x1, waiting for transfers between devices: 0.01 us -> 3.62 us  [local(): down = lax.ppermute(down, 'z', shift(NZ, -1))]
    gather x1 -> x2, local copies, waits for them, and re-layouts: 11.3 us -> 14.7 us  [the longest x1 7.34 us: local(): second = support_queue[asked[:, CAP // 2:]]]
    ppermute x3, waiting for transfers between devices: 4.56 us -> 1.75 us  [sum_everywhere(): got = [lax.ppermute(v, 'z', flip(NZ, m)) for m in (1, 2, 3)]]
  transfers between devices with their start and end apart: 28 -> 29, of which waited for: 16 -> 19; matrix products, arithmetic and copies ran while one was open for 7% -> 5% of each run, Pallas kernels for 5% -> 5%
where the time goes in v3:
time: 203 us
  starting transfers between devices  66.2 us (33%)
  waiting for transfers between devices  55.2 us (27%)
  blocking collectives  45.9 us (23%)
  Pallas kernels  16.4 us (8%)
  local copies, waits for them, and re-layouts  15 us (7%)
    all_to_all x1, blocking collectives, sum_everywhere(): v = lax.all_to_all(v, ('y', 'x'), 0, 0, tiled=True)  17 us
    all_to_all x1, blocking collectives, local(): lax.all_to_all(wanted, QUEUE, split_axis=0, concat_axis=0, tiled=True)  16.6 us
    ppermute x1, waiting for transfers between devices, local(): views[5] = lax.ppermute(views[6], 'z', shift(NZ, 1))  16.5 us
    all_to_all x1, blocking collectives, sum_everywhere(): v = lax.all_to_all(v.reshape(rows, width), ('y', 'x'), 0, 0, tiled=True)  12.3 us
    ppermute x3, starting transfers between devices, local(): down = lax.ppermute(down, 'z', shift(NZ, -1)).astype(F32)  9.09 us
    ppermute x1, waiting for transfers between devices, local(): views[6] = lax.ppermute(views[7], 'z', shift(NZ, 1))  8.65 us
    ppermute x1, starting transfers between devices, sum_everywhere(): v = keep + lax.ppermute(send, 'core', flip(NC, 1))  8.23 us
    all_to_all x1, starting transfers between devices, local(): lax.all_to_all(first, QUEUE, split_axis=0, concat_axis=0, tiled=True)  7.79 us
  transfers between devices with their start and end apart: 29, of which 19 were waited for; matrix products, arithmetic and copies ran while one was open for 5% of the time, Pallas kernels for 5%

profile of v3, /device:TPU:1, one launch (start us, length us, event | category | flops | bytes accessed | tf_op | source)
XLA Modules:
  0.0 202.8 jit_solution(7051452530780678048)
XLA Ops:
  0.6 2.7 %begin.1 = (bf16[512,256]{1,0:T(8,128)(2,1)}, s32[32,64]{1,0:T(8,128)}) custom-call(bf16[512,1024]{1,0:T(8,128)(2,1)} %feats_ref.1, bf16[1024,256]{1,0:T(8,128)(2,1)} %weight_ref.1, s32[1,512]{1,0:T(1,128)} %bitcast.19, s32[1,512]{1,0:T(1,128)} %bitcast.25), custom_call_target="tpu_custom_call" | custom-call | tf_op jit(solution)/shard_map/begin/pallas_call | solution.py:100
  3.3 2.5 %collective-permute-start = (bf16[512,256]{1,0:T(8,128)(2,1)}, bf16[512,256]{1,0:T(8,128)(2,1)S(1)}, u32[]{:S(2)}, u32[]{:S(2)}) collective-permute-start(bf16[512,256]{1,0:T(8,128)(2,1)} %get-tuple-element.43.refs_0_), channel_id=1, source_target_pairs={{0,4},{4,8},{8,12},{12,16},{16,20},{20,24},{24,28},{28,0},{1,5},{5... | collective-permute-start | bytes 786440 | tf_op jit(solution)/shard_map/ppermute | solution.py:302
  5.9 4.0 %collective-permute-start.1 = (bf16[512,256]{1,0:T(8,128)(2,1)}, bf16[512,256]{1,0:T(8,128)(2,1)S(1)}, u32[]{:S(2)}, u32[]{:S(2)}) collective-permute-start(bf16[512,256]{1,0:T(8,128)(2,1)} %get-tuple-element.43.refs_0_), channel_id=1, source_target_pairs={{0,28},{4,0},{8,4},{12,8},{16,12},{20,16},{24,20},{28,24},{1,29},{... | collective-permute-start | bytes 786440 | tf_op jit(solution)/shard_map/ppermute | solution.py:303
  9.9 16.6 %all_to_all.40 = s32[32,1,64]{2,1,0:T(1,128)S(1)} all-to-all(s32[32,1,64]{2,1,0:T(1,128)} %bitcast.24), channel_id=1, replica_groups=mesh['y'=4,'core'=2,'z'=8,'x'=4] {'z','x'}, dimensions={0} | all-to-all | bytes 16384 | tf_op jit(solution)/shard_map/all_to_all | solution.py:304
  26.7 7.3 %gather_fusion.1 = bf16[1024,256]{1,0:T(8,128)(2,1)} fusion(bf16[8192,256]{1,0:T(8,128)(2,1)} %param.10, s32[1024]{0:T(1024)S(1)} %get-tuple-element.76), kind=kCustom, calls=%fused_computation.1 | custom fusion | bytes 1052672 | tf_op jit(solution)/shard_map/gather | solution.py:311
  34.1 4.0 %all-to-all-start.2 = ((bf16[32,32,256]{2,1,0:T(8,128)(2,1)}), bf16[32,32,256]{2,1,0:T(8,128)(2,1)S(1)}, u32[]{:S(2)}, u32[]{:S(2)}) async-start(bf16[32,32,256]{2,1,0:T(8,128)(2,1)} %bitcast.8), calls=%async_computation.2 | async-start | bytes 1048576 | tf_op jit(solution)/shard_map/all_to_all | solution.py:312
  39.3 1.5 collective-permute-start.3
  40.9 7.3 %gather_fusion = bf16[1024,256]{1,0:T(8,128)(2,1)} fusion(bf16[8192,256]{1,0:T(8,128)(2,1)} %param.10, s32[1024]{0:T(1024)S(1)} %get-tuple-element.77), kind=kCustom, calls=%fused_computation | custom fusion | bytes 1052672 | tf_op jit(solution)/shard_map/gather | solution.py:308
  48.2 8.6 %collective-permute-done.2.refs_6_ = bf16[512,256]{1,0:T(8,128)(2,1)S(1)} collective-permute-done((bf16[512,256]{1,0:T(8,128)(2,1)S(1)}, bf16[512,256]{1,0:T(8,128)(2,1)S(1)}, u32[]{:S(2)}, u32[]{:S(2)}) %collective-permute-start.2) | collective-permute-done | bytes 262176 | tf_op jit(solution)/shard_map/ppermute | solution.py:306
  56.8 7.8 %all-to-all-start.1 = ((bf16[32,32,256]{2,1,0:T(8,128)(2,1)}), bf16[32,32,256]{2,1,0:T(8,128)(2,1)S(1)}, u32[]{:S(2)}, u32[]{:S(2)}) async-start(bf16[32,32,256]{2,1,0:T(8,128)(2,1)} %bitcast.6), calls=%async_computation.1 | async-start | bytes 1048576 | tf_op jit(solution)/shard_map/all_to_all | solution.py:310
  67.4 16.5 %collective-permute-done.8.refs_5_ = bf16[512,256]{1,0:T(8,128)(2,1)S(1)} collective-permute-done((bf16[512,256]{1,0:T(8,128)(2,1)S(1)}, bf16[512,256]{1,0:T(8,128)(2,1)S(1)}, u32[]{:S(2)}, u32[]{:S(2)}) %collective-permute-start.8) | collective-permute-done | bytes 262176 | tf_op jit(solution)/shard_map/ppermute | solution.py:313
  85.2 2.9 %collective-permute-start.5 = (bf16[528,256]{1,0:T(8,128)(2,1)S(1)}, bf16[528,256]{1,0:T(8,128)(2,1)S(1)}, u32[]{:S(2)}, u32[]{:S(2)}) collective-permute-start(bf16[528,256]{1,0:T(8,128)(2,1)S(1)} %pick.1.a_ref.refs_0_.message_ref), channel_id=1, source_target_pairs={{0,2},{1,3},{2,0},{3,1},{4,6},{5,7},{6,4},{7,5},{8,10},{9,11},{10,... | collective-permute-start | bytes 811016 | tf_op jit(solution)/shard_map/ppermute | solution.py:322
  88.3 2.4 %collective-permute-start.6 = (bf16[528,256]{1,0:T(8,128)(2,1)S(1)}, bf16[528,256]{1,0:T(8,128)(2,1)S(1)}, u32[]{:S(2)}, u32[]{:S(2)}) collective-permute-start(bf16[528,256]{1,0:T(8,128)(2,1)S(1)} %pick.1.a_ref.refs_0_.message_ref), channel_id=1, source_target_pairs={{0,3},{1,0},{2,1},{3,2},{4,7},{5,4},{6,5},{7,6},{8,11},{9,8},{10,9... | collective-permute-start | bytes 811016 | tf_op jit(solution)/shard_map/ppermute | solution.py:322
  94.2 6.0 %collective-permute-done.4.a_ref.refs_1_ = bf16[528,256]{1,0:T(8,128)(2,1)S(1)} collective-permute-done((bf16[528,256]{1,0:T(8,128)(2,1)S(1)}, bf16[528,256]{1,0:T(8,128)(2,1)S(1)}, u32[]{:S(2)}, u32[]{:S(2)}) %collective-permute-start.4) | collective-permute-done | bytes 270368 | tf_op jit(solution)/shard_map/ppermute | solution.py:322
  105.0 1.7 collective-permute-start.12
  109.2 2.7 %collective-permute-start.17 = (bf16[256,256]{1,0:T(8,128)(2,1)S(1)}, bf16[256,256]{1,0:T(8,128)(2,1)S(1)}, u32[]{:S(2)}, u32[]{:S(2)}) collective-permute-start(bf16[256,256]{1,0:T(8,128)(2,1)S(1)} %get-tuple-element.72), channel_id=1, source_target_pairs={{0,28},{4,0},{8,4},{12,8},{16,12},{20,16},{24,20},{28,24},{1,29},{... | collective-permute-start | bytes 393224 | tf_op jit(solution)/shard_map/ppermute | solution.py:337
  113.9 3.2 %collective-permute-start.18 = (bf16[512,256]{1,0:T(8,128)(2,1)S(1)}, bf16[512,256]{1,0:T(8,128)(2,1)S(1)}, u32[]{:S(2)}, u32[]{:S(2)}) collective-permute-start(bf16[512,256]{1,0:T(8,128)(2,1)S(1)} %pad_maximum_fusion.2), channel_id=1, source_target_pairs={{0,28},{4,0},{8,4},{12,8},{16,12},{20,16},{24,20},{28,24},{1,29},{... | collective-permute-start | bytes 786440 | tf_op jit(solution)/shard_map/ppermute | solution.py:337
  120.4 3.2 %collective-permute-start.19 = (bf16[512,256]{1,0:T(8,128)(2,1)S(1)}, bf16[512,256]{1,0:T(8,128)(2,1)S(1)}, u32[]{:S(2)}, u32[]{:S(2)}) collective-permute-start(bf16[512,256]{1,0:T(8,128)(2,1)S(1)} %add_convert_fusion.1), channel_id=1, source_target_pairs={{0,28},{4,0},{8,4},{12,8},{16,12},{20,16},{24,20},{28,24},{1,29},{... | collective-permute-start | bytes 786440 | tf_op jit(solution)/shard_map/ppermute | solution.py:337
  125.3 1.8 mix.7
  128.1 3.2 %collective-permute-start.20 = (bf16[512,256]{1,0:T(8,128)(2,1)S(1)}, bf16[512,256]{1,0:T(8,128)(2,1)S(1)}, u32[]{:S(2)}, u32[]{:S(2)}) collective-permute-start(bf16[512,256]{1,0:T(8,128)(2,1)S(1)} %add_convert_fusion), channel_id=1, source_target_pairs={{0,28},{4,0},{8,4},{12,8},{16,12},{20,16},{24,20},{28,24},{1,29},{... | collective-permute-start | bytes 786440 | tf_op jit(solution)/shard_map/ppermute | solution.py:346
  131.3 1.7 collective-permute-done.15
  133.2 3.6 %collective-permute-done.20.down_ref = bf16[512,256]{1,0:T(8,128)(2,1)S(1)} collective-permute-done((bf16[512,256]{1,0:T(8,128)(2,1)S(1)}, bf16[512,256]{1,0:T(8,128)(2,1)S(1)}, u32[]{:S(2)}, u32[]{:S(2)}) %collective-permute-start.20) | collective-permute-done | bytes 262176 | tf_op jit(solution)/shard_map/ppermute | solution.py:346
  136.8 5.2 %collective-permute-done.16.up_ref = bf16[512,256]{1,0:T(8,128)(2,1)S(1)} collective-permute-done((bf16[512,256]{1,0:T(8,128)(2,1)S(1)}, bf16[512,256]{1,0:T(8,128)(2,1)S(1)}, u32[]{:S(2)}, u32[]{:S(2)}) %collective-permute-start.16) | collective-permute-done | bytes 262176 | tf_op jit(solution)/shard_map/ppermute | solution.py:345
  142.0 1.6 finish.1
  143.6 8.2 %collective-permute-start.21 = (f32[512,256]{1,0:T(8,128)S(1)}, f32[512,256]{1,0:T(8,128)S(1)}, u32[]{:S(2)}, u32[]{:S(2)}) collective-permute-start(f32[512,256]{1,0:T(8,128)S(1)} %get-tuple-element.66), channel_id=1, source_target_pairs={{0,32},{32,0},{1,33},{33,1},{2,34},{34,2},{3,35},{35,3},{4,36},{36... | collective-permute-start | bytes 1572872 | tf_op jit(solution)/shard_map/ppermute | solution.py:279
  151.9 1.5 collective-permute-done.21
  153.5 17.0 %all_to_all.41 = f32[16,32,256]{2,1,0:T(8,128)S(1)} all-to-all(f32[16,32,256]{2,1,0:T(8,128)S(1)} %bitcast.22), channel_id=1, replica_groups=mesh['y'=4,'core'=2,'z'=8,'x'=4] {'y','x'}, dimensions={0} | all-to-all | bytes 1048576 | tf_op jit(solution)/shard_map/all_to_all | solution.py:281
  170.9 3.3 %collective-permute-start.24 = (f32[32,256]{1,0:T(8,128)S(1)}, f32[32,256]{1,0:T(8,128)S(1)}, u32[]{:S(2)}, u32[]{:S(2)}) collective-permute-start(f32[32,256]{1,0:T(8,128)S(1)} %reduce_sum.9), channel_id=1, source_target_pairs={{0,12},{4,8},{8,4},{12,0},{16,28},{20,24},{24,20},{28,16},{1,13},{... | collective-permute-start | bytes 98312 | tf_op jit(solution)/shard_map/ppermute | solution.py:283
  175.9 3.2 %collective-permute-start.25 = (f32[32,256]{1,0:T(8,128)S(1)}, f32[32,256]{1,0:T(8,128)S(1)}, u32[]{:S(2)}, u32[]{:S(2)}) collective-permute-start(f32[32,256]{1,0:T(8,128)S(1)} %add_add_fusion), channel_id=1, source_target_pairs={{0,16},{4,20},{8,24},{12,28},{16,0},{20,4},{24,8},{28,12},{1,17},{... | collective-permute-start | bytes 98312 | tf_op jit(solution)/shard_map/ppermute | solution.py:285
  180.6 2.1 %collective-permute-done.25 = f32[32,256]{1,0:T(8,128)S(1)} collective-permute-done((f32[32,256]{1,0:T(8,128)S(1)}, f32[32,256]{1,0:T(8,128)S(1)}, u32[]{:S(2)}, u32[]{:S(2)}) %collective-permute-start.25) | collective-permute-done | bytes 32800 | tf_op jit(solution)/shard_map/ppermute | solution.py:285
  182.8 12.3 %all_to_all.42 = f32[16,32,256]{2,1,0:T(8,128)S(1)} all-to-all(f32[16,32,256]{2,1,0:T(8,128)S(1)} %broadcast_in_dim.15), channel_id=1, replica_groups=mesh['y'=4,'core'=2,'z'=8,'x'=4] {'y','x'}, dimensions={0} | all-to-all | bytes 1048576 | tf_op jit(solution)/shard_map/all_to_all | solution.py:288
  195.1 5.1 %collective-permute-start.26 = (f32[512,256]{1,0:T(8,128)S(1)}, f32[512,256]{1,0:T(8,128)S(1)}, u32[]{:S(2)}, u32[]{:S(2)}) collective-permute-start(f32[512,256]{1,0:T(8,128)S(1)} %bitcast.21), channel_id=1, source_target_pairs={{0,32},{32,0},{1,33},{33,1},{2,34},{34,2},{3,35},{35,3},{4,36},{36... | collective-permute-start | bytes 1572872 | tf_op jit(solution)/shard_map/ppermute | solution.py:289
  (82 shorter events, 30.9 us)
Async XLA Ops:
  3.3 23.1 %collective-permute-start = (bf16[512,256]{1,0:T(8,128)(2,1)}, bf16[512,256]{1,0:T(8,128)(2,1)S(1)}, u32[]{:S(2)}, u32[]{:S(2)}) collective-permute-start(bf16[512,256]{1,0:T(8,128)(2,1)} %get-tuple-element.43.refs_0_), channel_id=1, source_target_pairs={{0,4},{4,8},{8,12},{12,16},{16,20},{20,24},{24,28},{28,0},{1,5},{5... | collective-permute-start | bytes 786440 | tf_op jit(solution)/shard_map/ppermute | solution.py:302
  5.9 20.6 %collective-permute-start.1 = (bf16[512,256]{1,0:T(8,128)(2,1)}, bf16[512,256]{1,0:T(8,128)(2,1)S(1)}, u32[]{:S(2)}, u32[]{:S(2)}) collective-permute-start(bf16[512,256]{1,0:T(8,128)(2,1)} %get-tuple-element.43.refs_0_), channel_id=1, source_target_pairs={{0,28},{4,0},{8,4},{12,8},{16,12},{20,16},{24,20},{28,24},{1,29},{... | collective-permute-start | bytes 786440 | tf_op jit(solution)/shard_map/ppermute | solution.py:303
  34.0 49.8 %copy-start.4 = (bf16[512]{0:T(512)(128)(2,1)S(1)}, bf16[512]{0:T(512)(128)(2,1)}, u32[]{:S(2)}) copy-start(bf16[512]{0:T(512)(128)(2,1)} %param.13) | copy-start | bytes 3076
  34.1 49.8 %copy-start.3 = (s32[512,1]{0,1:T(1,128)S(1)}, s32[512,1]{0,1:T(1,128)}, u32[]{:S(2)}) copy-start(s32[512,1]{0,1:T(1,128)} %param.11) | copy-start | bytes 6148
  34.1 56.9 %copy-start.1 = (bf16[512,256]{1,0:T(8,128)(2,1)S(1)}, bf16[512,256]{1,0:T(8,128)(2,1)}, u32[]{:S(2)}) copy-start(bf16[512,256]{1,0:T(8,128)(2,1)} %get-tuple-element.43.refs_0_) | copy-start | bytes 786436
  34.1 22.8 %all-to-all-start.2 = ((bf16[32,32,256]{2,1,0:T(8,128)(2,1)}), bf16[32,32,256]{2,1,0:T(8,128)(2,1)S(1)}, u32[]{:S(2)}, u32[]{:S(2)}) async-start(bf16[32,32,256]{2,1,0:T(8,128)(2,1)} %bitcast.8), calls=%async_computation.2 | async-start | bytes 1048576 | tf_op jit(solution)/shard_map/all_to_all | solution.py:312
  38.1 18.7 %collective-permute-start.2 = (bf16[512,256]{1,0:T(8,128)(2,1)S(1)}, bf16[512,256]{1,0:T(8,128)(2,1)S(1)}, u32[]{:S(2)}, u32[]{:S(2)}) collective-permute-start(bf16[512,256]{1,0:T(8,128)(2,1)S(1)} %collective-permute-done.refs_7_), channel_id=1, source_target_pairs={{0,4},{4,8},{8,12},{12,16},{16,20},{20,24},{24,28},{28,0},{1,5},{5... | collective-permute-start | bytes 786440 | tf_op jit(solution)/shard_map/ppermute | solution.py:306
  39.3 17.5 %collective-permute-start.3 = (bf16[512,256]{1,0:T(8,128)(2,1)S(1)}, bf16[512,256]{1,0:T(8,128)(2,1)S(1)}, u32[]{:S(2)}, u32[]{:S(2)}) collective-permute-start(bf16[512,256]{1,0:T(8,128)(2,1)S(1)} %collective-permute-done.1.refs_1_), channel_id=1, source_target_pairs={{0,28},{4,0},{8,4},{12,8},{16,12},{20,16},{24,20},{28,24},{1,29},{... | collective-permute-start | bytes 786440 | tf_op jit(solution)/shard_map/ppermute | solution.py:307
  56.8 27.0 %all-to-all-start.1 = ((bf16[32,32,256]{2,1,0:T(8,128)(2,1)}), bf16[32,32,256]{2,1,0:T(8,128)(2,1)S(1)}, u32[]{:S(2)}, u32[]{:S(2)}) async-start(bf16[32,32,256]{2,1,0:T(8,128)(2,1)} %bitcast.6), calls=%async_computation.1 | async-start | bytes 1048576 | tf_op jit(solution)/shard_map/all_to_all | solution.py:310
  64.6 19.2 %collective-permute-start.8 = (bf16[512,256]{1,0:T(8,128)(2,1)S(1)}, bf16[512,256]{1,0:T(8,128)(2,1)S(1)}, u32[]{:S(2)}, u32[]{:S(2)}) collective-permute-start(bf16[512,256]{1,0:T(8,128)(2,1)S(1)} %collective-permute-done.2.refs_6_), channel_id=1, source_target_pairs={{0,4},{4,8},{8,12},{12,16},{16,20},{20,24},{24,28},{28,0},{1,5},{5... | collective-permute-start | bytes 786440 | tf_op jit(solution)/shard_map/ppermute | solution.py:313
  66.0 24.8 %collective-permute-start.7 = (bf16[512,256]{1,0:T(8,128)(2,1)S(1)}, bf16[512,256]{1,0:T(8,128)(2,1)S(1)}, u32[]{:S(2)}, u32[]{:S(2)}) collective-permute-start(bf16[512,256]{1,0:T(8,128)(2,1)S(1)} %collective-permute-done.3.refs_2_), channel_id=1, source_target_pairs={{0,28},{4,0},{8,4},{12,8},{16,12},{20,16},{24,20},{28,24},{1,29},{... | collective-permute-start | bytes 786440 | tf_op jit(solution)/shard_map/ppermute | solution.py:314
  83.9 7.1 %collective-permute-start.9 = (bf16[512,256]{1,0:T(8,128)(2,1)S(1)}, bf16[512,256]{1,0:T(8,128)(2,1)S(1)}, u32[]{:S(2)}, u32[]{:S(2)}) collective-permute-start(bf16[512,256]{1,0:T(8,128)(2,1)S(1)} %collective-permute-done.8.refs_5_), channel_id=1, source_target_pairs={{0,4},{4,8},{8,12},{12,16},{16,20},{20,24},{24,28},{28,0},{1,5},{5... | collective-permute-start | bytes 786440 | tf_op jit(solution)/shard_map/ppermute | solution.py:315
  85.2 7.7 %collective-permute-start.5 = (bf16[528,256]{1,0:T(8,128)(2,1)S(1)}, bf16[528,256]{1,0:T(8,128)(2,1)S(1)}, u32[]{:S(2)}, u32[]{:S(2)}) collective-permute-start(bf16[528,256]{1,0:T(8,128)(2,1)S(1)} %pick.1.a_ref.refs_0_.message_ref), channel_id=1, source_target_pairs={{0,2},{1,3},{2,0},{3,1},{4,6},{5,7},{6,4},{7,5},{8,10},{9,11},{10,... | collective-permute-start | bytes 811016 | tf_op jit(solution)/shard_map/ppermute | solution.py:322
  88.1 12.1 %collective-permute-start.4 = (bf16[528,256]{1,0:T(8,128)(2,1)S(1)}, bf16[528,256]{1,0:T(8,128)(2,1)S(1)}, u32[]{:S(2)}, u32[]{:S(2)}) collective-permute-start(bf16[528,256]{1,0:T(8,128)(2,1)S(1)} %pick.1.a_ref.refs_0_.message_ref), channel_id=1, source_target_pairs={{0,1},{1,2},{2,3},{3,0},{4,5},{5,6},{6,7},{7,4},{8,9},{9,10},{10,1... | collective-permute-start | bytes 811016 | tf_op jit(solution)/shard_map/ppermute | solution.py:322
  88.3 13.2 %collective-permute-start.6 = (bf16[528,256]{1,0:T(8,128)(2,1)S(1)}, bf16[528,256]{1,0:T(8,128)(2,1)S(1)}, u32[]{:S(2)}, u32[]{:S(2)}) collective-permute-start(bf16[528,256]{1,0:T(8,128)(2,1)S(1)} %pick.1.a_ref.refs_0_.message_ref), channel_id=1, source_target_pairs={{0,3},{1,0},{2,1},{3,2},{4,7},{5,4},{6,5},{7,6},{8,11},{9,8},{10,9... | collective-permute-start | bytes 811016 | tf_op jit(solution)/shard_map/ppermute | solution.py:322
  102.8 3.8 %collective-permute-start.10 = (f32[1,2048]{1,0:T(1,128)S(1)}, f32[1,2048]{1,0:T(1,128)S(1)}, u32[]{:S(2)}, u32[]{:S(2)}) collective-permute-start(f32[1,2048]{1,0:T(1,128)S(1)} %constant_dynamic-update-slice_fusion.refs_4_), channel_id=1, source_target_pairs={{0,1},{1,2},{2,3},{3,0},{4,5},{5,6},{6,7},{7,4},{8,9},{9,10},{10,1... | collective-permute-start | bytes 24584 | tf_op jit(solution)/shard_map/ppermute | solution.py:328
  103.7 4.0 %collective-permute-start.11 = (f32[1,2048]{1,0:T(1,128)S(1)}, f32[1,2048]{1,0:T(1,128)S(1)}, u32[]{:S(2)}, u32[]{:S(2)}) collective-permute-start(f32[1,2048]{1,0:T(1,128)S(1)} %constant_dynamic-update-slice_fusion.refs_4_), channel_id=1, source_target_pairs={{0,2},{1,3},{2,0},{3,1},{4,6},{5,7},{6,4},{7,5},{8,10},{9,11},{10,... | collective-permute-start | bytes 24584 | tf_op jit(solution)/shard_map/ppermute | solution.py:328
  105.0 2.8 %collective-permute-start.12 = (f32[1,2048]{1,0:T(1,128)S(1)}, f32[1,2048]{1,0:T(1,128)S(1)}, u32[]{:S(2)}, u32[]{:S(2)}) collective-permute-start(f32[1,2048]{1,0:T(1,128)S(1)} %constant_dynamic-update-slice_fusion.refs_4_), channel_id=1, source_target_pairs={{0,3},{1,0},{2,1},{3,2},{4,7},{5,4},{6,5},{7,6},{8,11},{9,8},{10,9... | collective-permute-start | bytes 24584 | tf_op jit(solution)/shard_map/ppermute | solution.py:328
  109.2 4.7 %collective-permute-start.17 = (bf16[256,256]{1,0:T(8,128)(2,1)S(1)}, bf16[256,256]{1,0:T(8,128)(2,1)S(1)}, u32[]{:S(2)}, u32[]{:S(2)}) collective-permute-start(bf16[256,256]{1,0:T(8,128)(2,1)S(1)} %get-tuple-element.72), channel_id=1, source_target_pairs={{0,28},{4,0},{8,4},{12,8},{16,12},{20,16},{24,20},{28,24},{1,29},{... | collective-permute-start | bytes 393224 | tf_op jit(solution)/shard_map/ppermute | solution.py:337
  113.2 5.1 %collective-permute-start.13 = (bf16[256,256]{1,0:T(8,128)(2,1)S(1)}, bf16[256,256]{1,0:T(8,128)(2,1)S(1)}, u32[]{:S(2)}, u32[]{:S(2)}) collective-permute-start(bf16[256,256]{1,0:T(8,128)(2,1)S(1)} %get-tuple-element.73), channel_id=1, source_target_pairs={{0,4},{4,8},{8,12},{12,16},{16,20},{20,24},{24,28},{28,0},{1,5},{5... | collective-permute-start | bytes 393224 | tf_op jit(solution)/shard_map/ppermute | solution.py:336
  113.9 6.5 %collective-permute-start.18 = (bf16[512,256]{1,0:T(8,128)(2,1)S(1)}, bf16[512,256]{1,0:T(8,128)(2,1)S(1)}, u32[]{:S(2)}, u32[]{:S(2)}) collective-permute-start(bf16[512,256]{1,0:T(8,128)(2,1)S(1)} %pad_maximum_fusion.2), channel_id=1, source_target_pairs={{0,28},{4,0},{8,4},{12,8},{16,12},{20,16},{24,20},{28,24},{1,29},{... | collective-permute-start | bytes 786440 | tf_op jit(solution)/shard_map/ppermute | solution.py:337
  118.3 6.7 %collective-permute-start.14 = (bf16[512,256]{1,0:T(8,128)(2,1)S(1)}, bf16[512,256]{1,0:T(8,128)(2,1)S(1)}, u32[]{:S(2)}, u32[]{:S(2)}) collective-permute-start(bf16[512,256]{1,0:T(8,128)(2,1)S(1)} %pad_maximum_fusion.1), channel_id=1, source_target_pairs={{0,4},{4,8},{8,12},{12,16},{16,20},{20,24},{24,28},{28,0},{1,5},{5... | collective-permute-start | bytes 786440 | tf_op jit(solution)/shard_map/ppermute | solution.py:336
  120.4 7.6 %collective-permute-start.19 = (bf16[512,256]{1,0:T(8,128)(2,1)S(1)}, bf16[512,256]{1,0:T(8,128)(2,1)S(1)}, u32[]{:S(2)}, u32[]{:S(2)}) collective-permute-start(bf16[512,256]{1,0:T(8,128)(2,1)S(1)} %add_convert_fusion.1), channel_id=1, source_target_pairs={{0,28},{4,0},{8,4},{12,8},{16,12},{20,16},{24,20},{28,24},{1,29},{... | collective-permute-start | bytes 786440 | tf_op jit(solution)/shard_map/ppermute | solution.py:337
  125.2 7.8 %collective-permute-start.15 = (bf16[512,256]{1,0:T(8,128)(2,1)S(1)}, bf16[512,256]{1,0:T(8,128)(2,1)S(1)}, u32[]{:S(2)}, u32[]{:S(2)}) collective-permute-start(bf16[512,256]{1,0:T(8,128)(2,1)S(1)} %add_convert_fusion.3), channel_id=1, source_target_pairs={{0,4},{4,8},{8,12},{12,16},{16,20},{20,24},{24,28},{28,0},{1,5},{5... | collective-permute-start | bytes 786440 | tf_op jit(solution)/shard_map/ppermute | solution.py:336
  128.1 8.7 %collective-permute-start.20 = (bf16[512,256]{1,0:T(8,128)(2,1)S(1)}, bf16[512,256]{1,0:T(8,128)(2,1)S(1)}, u32[]{:S(2)}, u32[]{:S(2)}) collective-permute-start(bf16[512,256]{1,0:T(8,128)(2,1)S(1)} %add_convert_fusion), channel_id=1, source_target_pairs={{0,28},{4,0},{8,4},{12,8},{16,12},{20,16},{24,20},{28,24},{1,29},{... | collective-permute-start | bytes 786440 | tf_op jit(solution)/shard_map/ppermute | solution.py:346
  133.1 9.0 %collective-permute-start.16 = (bf16[512,256]{1,0:T(8,128)(2,1)S(1)}, bf16[512,256]{1,0:T(8,128)(2,1)S(1)}, u32[]{:S(2)}, u32[]{:S(2)}) collective-permute-start(bf16[512,256]{1,0:T(8,128)(2,1)S(1)} %add_convert_fusion.2), channel_id=1, source_target_pairs={{0,4},{4,8},{8,12},{12,16},{16,20},{20,24},{24,28},{28,0},{1,5},{5... | collective-permute-start | bytes 786440 | tf_op jit(solution)/shard_map/ppermute | solution.py:345
  143.6 9.8 %collective-permute-start.21 = (f32[512,256]{1,0:T(8,128)S(1)}, f32[512,256]{1,0:T(8,128)S(1)}, u32[]{:S(2)}, u32[]{:S(2)}) collective-permute-start(f32[512,256]{1,0:T(8,128)S(1)} %get-tuple-element.66), channel_id=1, source_target_pairs={{0,32},{32,0},{1,33},{33,1},{2,34},{34,2},{3,35},{35,3},{4,36},{36... | collective-permute-start | bytes 1572872 | tf_op jit(solution)/shard_map/ppermute | solution.py:279
  170.5 3.6 %collective-permute-start.22 = (f32[32,256]{1,0:T(8,128)S(1)}, f32[32,256]{1,0:T(8,128)S(1)}, u32[]{:S(2)}, u32[]{:S(2)}) collective-permute-start(f32[32,256]{1,0:T(8,128)S(1)} %reduce_sum.9), channel_id=1, source_target_pairs={{0,4},{4,0},{8,12},{12,8},{16,20},{20,16},{24,28},{28,24},{1,5},{5... | collective-permute-start | bytes 98312 | tf_op jit(solution)/shard_map/ppermute | solution.py:283
  170.6 3.8 %collective-permute-start.23 = (f32[32,256]{1,0:T(8,128)S(1)}, f32[32,256]{1,0:T(8,128)S(1)}, u32[]{:S(2)}, u32[]{:S(2)}) collective-permute-start(f32[32,256]{1,0:T(8,128)S(1)} %reduce_sum.9), channel_id=1, source_target_pairs={{0,8},{4,12},{8,0},{12,4},{16,24},{20,28},{24,16},{28,20},{1,9},{5... | collective-permute-start | bytes 98312 | tf_op jit(solution)/shard_map/ppermute | solution.py:283
  170.9 5.0 %collective-permute-start.24 = (f32[32,256]{1,0:T(8,128)S(1)}, f32[32,256]{1,0:T(8,128)S(1)}, u32[]{:S(2)}, u32[]{:S(2)}) collective-permute-start(f32[32,256]{1,0:T(8,128)S(1)} %reduce_sum.9), channel_id=1, source_target_pairs={{0,12},{4,8},{8,4},{12,0},{16,28},{20,24},{24,20},{28,16},{1,13},{... | collective-permute-start | bytes 98312 | tf_op jit(solution)/shard_map/ppermute | solution.py:283
  175.9 6.8 %collective-permute-start.25 = (f32[32,256]{1,0:T(8,128)S(1)}, f32[32,256]{1,0:T(8,128)S(1)}, u32[]{:S(2)}, u32[]{:S(2)}) collective-permute-start(f32[32,256]{1,0:T(8,128)S(1)} %add_add_fusion), channel_id=1, source_target_pairs={{0,16},{4,20},{8,24},{12,28},{16,0},{20,4},{24,8},{28,12},{1,17},{... | collective-permute-start | bytes 98312 | tf_op jit(solution)/shard_map/ppermute | solution.py:285
  195.1 6.6 %collective-permute-start.26 = (f32[512,256]{1,0:T(8,128)S(1)}, f32[512,256]{1,0:T(8,128)S(1)}, u32[]{:S(2)}, u32[]{:S(2)}) collective-permute-start(f32[512,256]{1,0:T(8,128)S(1)} %bitcast.21), channel_id=1, source_target_pairs={{0,32},{32,0},{1,33},{33,1},{2,34},{34,2},{3,35},{35,3},{4,36},{36... | collective-permute-start | bytes 1572872 | tf_op jit(solution)/shard_map/ppermute | solution.py:289
  (2 other events, 33.8 us)

commit v4 on v2

--- a/solution.py
+++ b/solution.py
@@ -203,15 +203,36 @@
     )(*anchors, *totals)
 
 
+def product(k, a_ref, parts):
+    total = None
+    for b, part in enumerate(parts):
+        size = part.shape[2]
+        term = jnp.dot(part[k], a_ref[b * size : (b + 1) * size, :], preferred_element_type=F32)
+        total = term if total is None else total + term
+    return total
+
+
 def mix_kernel(which, a_ref, *refs):
-    parts, outs = refs[:NX], refs[NX:]
-    for k, out in zip(which, outs):
-        total = None
-        for b, part in enumerate(parts):
-            size = part.shape[2]
-            term = jnp.dot(part[k], a_ref[b * size : (b + 1) * size, :], preferred_element_type=F32)
-            total = term if total is None else total + term
-        out[...] = total.astype(out.dtype)
+    for k, out in zip(which, refs[NX:]):
+        out[...] = product(k, a_ref, refs[:NX]).astype(out.dtype)
+
+
+def far_kernel(a_ref, *refs):
+    total = product(NZ // 2, a_ref, refs[:NX]).astype(BF)
+    half = total.shape[0] // 2
+    refs[NX][...] = total[:half]
+    refs[NX + 1][...] = total[half:]
+
+
+def mix_far(scaled, parts):
+    shape = jax.ShapeDtypeStruct((parts[0].shape[1] // 2, scaled.shape[1]), BF)
+    return vmem_call(
+        far_kernel,
+        (shape, shape),
+        "mix_far",
+        in_specs=[IN_VMEM] * (1 + NX),
+        out_specs=(IN_VMEM, IN_VMEM),
+    )(scaled, *parts)
 
 
 def mix(which, scaled, parts, dtype):
@@ -272,17 +293,17 @@
     rows, width = keep.shape
     v = keep + lax.ppermute(send, "core", flip(NC, 1))
     many = NY * NX
-    v = lax.all_to_all(v, ("y", "x"), 0, 0, tiled=True)
+    v = lax.all_to_all(v.astype(BF), ("y", "x"), 0, 0, tiled=True).astype(F32)
     v = jnp.sum(v.reshape(many, rows // many, width), axis=0)
     got = [lax.ppermute(v, "z", flip(NZ, m)) for m in (1, 2, 3)]
     v = (v + got[0]) + (got[1] + got[2])
     v = v + lax.ppermute(v, "z", flip(NZ, 4))
-    v, beside = lax.optimization_barrier((v, beside))
+    v, beside = lax.optimization_barrier((v.astype(BF), beside))
     v = lax.optimization_barrier(jnp.broadcast_to(v[None], (many,) + v.shape))
     v = lax.all_to_all(v.reshape(rows, width), ("y", "x"), 0, 0, tiled=True)
     other = lax.ppermute(v, "core", flip(NC, 1))
     low, high = jnp.where(core == 0, v, other), jnp.where(core == 0, other, v)
-    return jnp.concatenate([low, high], axis=0), beside
+    return jnp.concatenate([low, high], axis=0).astype(F32), beside
 
 
 def local(features, weight, support_queue, owner_shard, slot_row, loss_weight):
@@ -319,10 +340,10 @@
     everyone = [total] + [lax.ppermute(total, "x", shift(NX, k)) for k in (1, 2, 3)]
     scaled = scale(blocks, everyone, n)
 
-    (far,) = mix((4,), scaled, parts, BF)
-    up, down = far[: n // 2], far[n // 2 :]
+    up, down = mix_far(scaled, parts)
     for d in (3, 2, 1):
-        up_part, down_part = mix((d, NZ - d), scaled, parts, F32)
+        which = (d, NZ - d) if d > 1 else (d, NZ - d, 0)
+        up_part, down_part, *rest = mix(which, scaled, parts, F32)
         up = lax.ppermute(up, "z", shift(NZ, 1)).astype(F32)
         down = lax.ppermute(down, "z", shift(NZ, -1)).astype(F32)
         if d == 3:
@@ -330,8 +351,8 @@
             down = jnp.concatenate([down_part[: n // 2], down + down_part[n // 2 :]], axis=0)
         else:
             up, down = up + up_part, down + down_part
-        up, down = up.astype(BF), down.astype(BF)
-    (own,) = mix((0,), scaled, parts, F32)
+        up, down = lax.optimization_barrier((up.astype(BF), down.astype(BF)))
+    (own,) = rest
     up = lax.ppermute(up, "z", shift(NZ, 1))
     down = lax.ppermute(down, "z", shift(NZ, -1))
 

time: 201 us -> 193 us (0.960)
  waiting for transfers between devices: 53 us -> 65.2 us
  local copies, waits for them, and re-layouts: 20.9 us -> 11.5 us
  starting transfers between devices: 60.3 us -> 55.1 us
  blocking collectives: 45.7 us -> 40.9 us
    unnamed x29 -> x13, local copies, waits for them, and re-layouts: 9.45 us -> 0.05 us
    ppermute x1, waiting for transfers between devices: 0.01 us -> 6.3 us  [local(): up = lax.ppermute(up, 'z', shift(NZ, 1))]
    ppermute x3, starting transfers between devices: 9.08 us -> 2.92 us  [local(): down = lax.ppermute(down, 'z', shift(NZ, -1)).astype(F32)]
    ppermute x3, waiting for transfers between devices: 2.69 us -> 6.43 us  [local(): down = lax.ppermute(down, 'z', shift(NZ, -1)).astype(F32)]
    ppermute x3, waiting for transfers between devices: 4.48 us -> 7.05 us  [local(): up = lax.ppermute(up, 'z', shift(NZ, 1)).astype(F32)]
    ppermute x3, starting transfers between devices: 0.47 us -> 2.99 us  [local(): up = lax.ppermute(up, 'z', shift(NZ, 1)).astype(F32)]
    all_to_all x1, blocking collectives: 16.7 us -> 14.2 us  [sum_everywhere(): v = lax.all_to_all(v.astype(BF), ('y', 'x'), 0, 0, tiled=True).astype(F32)]
    all_to_all x1, blocking collectives: 12.5 us -> 10.1 us  [sum_everywhere(): v = lax.all_to_all(v.reshape(rows, width), ('y', 'x'), 0, 0, tiled=True)]
  transfers between devices with their start and end apart: 28 -> 28, of which waited for: 16 -> 17; matrix products, arithmetic and copies ran while one was open for 7% -> 7% of each run, Pallas kernels for 5% -> 5%
where the time goes in v4:
time: 193 us
  waiting for transfers between devices  65.2 us (34%)
  starting transfers between devices  55.1 us (29%)
  blocking collectives  40.9 us (21%)
  Pallas kernels  16.4 us (8%)
  local copies, waits for them, and re-layouts  11.5 us (6%)
    ppermute x1, waiting for transfers between devices, local(): views[5] = lax.ppermute(views[6], 'z', shift(NZ, 1))  26.8 us
    all_to_all x1, blocking collectives, local(): lax.all_to_all(wanted, QUEUE, split_axis=0, concat_axis=0, tiled=True)  16.6 us
    all_to_all x1, blocking collectives, sum_everywhere(): v = lax.all_to_all(v.astype(BF), ('y', 'x'), 0, 0, tiled=True).astype(F32)  14.2 us
    gather x1, local copies, waits for them, and re-layouts, local(): picked = support_queue[asked]  11.3 us
    all_to_all x1, blocking collectives, sum_everywhere(): v = lax.all_to_all(v.reshape(rows, width), ('y', 'x'), 0, 0, tiled=True)  10.1 us
    ppermute x1, starting transfers between devices, sum_everywhere(): v = keep + lax.ppermute(send, 'core', flip(NC, 1))  8.23 us
    ppermute x3, waiting for transfers between devices, local(): up = lax.ppermute(up, 'z', shift(NZ, 1)).astype(F32)  7.05 us
    ppermute x3, waiting for transfers between devices, local(): down = lax.ppermute(down, 'z', shift(NZ, -1)).astype(F32)  6.43 us
  transfers between devices with their start and end apart: 28, of which 17 were waited for; matrix products, arithmetic and copies ran while one was open for 7% of the time, Pallas kernels for 5%

profile of v4, /device:TPU:1, one launch (start us, length us, event | category | flops | bytes accessed | tf_op | source)
XLA Modules:
  0.0 193.1 jit_solution(2253555429291168818)
XLA Ops:
  0.6 2.7 %begin.1 = (bf16[512,256]{1,0:T(8,128)(2,1)}, s32[32,64]{1,0:T(8,128)}) custom-call(bf16[512,1024]{1,0:T(8,128)(2,1)} %feats_ref.1, bf16[1024,256]{1,0:T(8,128)(2,1)} %weight_ref.1, s32[1,512]{1,0:T(1,128)} %bitcast.16, s32[1,512]{1,0:T(1,128)} %bitcast.23), custom_call_target="tpu_custom_call" | custom-call | tf_op jit(solution)/shard_map/begin/pallas_call | solution.py:100
  3.3 2.5 %collective-permute-start = (bf16[512,256]{1,0:T(8,128)(2,1)}, bf16[512,256]{1,0:T(8,128)(2,1)S(1)}, u32[]{:S(2)}, u32[]{:S(2)}) collective-permute-start(bf16[512,256]{1,0:T(8,128)(2,1)} %get-tuple-element.51.refs_0_), channel_id=1, source_target_pairs={{0,4},{4,8},{8,12},{12,16},{16,20},{20,24},{24,28},{28,0},{1,5},{5... | collective-permute-start | bytes 786440 | tf_op jit(solution)/shard_map/ppermute | solution.py:317
  5.9 4.0 %collective-permute-start.1 = (bf16[512,256]{1,0:T(8,128)(2,1)}, bf16[512,256]{1,0:T(8,128)(2,1)S(1)}, u32[]{:S(2)}, u32[]{:S(2)}) collective-permute-start(bf16[512,256]{1,0:T(8,128)(2,1)} %get-tuple-element.51.refs_0_), channel_id=1, source_target_pairs={{0,28},{4,0},{8,4},{12,8},{16,12},{20,16},{24,20},{28,24},{1,29},{... | collective-permute-start | bytes 786440 | tf_op jit(solution)/shard_map/ppermute | solution.py:318
  9.9 16.6 %all_to_all.35 = s32[32,1,64]{2,1,0:T(1,128)S(1)} all-to-all(s32[32,1,64]{2,1,0:T(1,128)} %bitcast.22), channel_id=1, replica_groups=mesh['y'=4,'core'=2,'z'=8,'x'=4] {'z','x'}, dimensions={0} | all-to-all | bytes 16384 | tf_op jit(solution)/shard_map/all_to_all | solution.py:319
  26.8 2.3 %collective-permute-start.3 = (bf16[512,256]{1,0:T(8,128)(2,1)S(1)}, bf16[512,256]{1,0:T(8,128)(2,1)S(1)}, u32[]{:S(2)}, u32[]{:S(2)}) collective-permute-start(bf16[512,256]{1,0:T(8,128)(2,1)S(1)} %collective-permute-done.1.refs_1_), channel_id=1, source_target_pairs={{0,28},{4,0},{8,4},{12,8},{16,12},{20,16},{24,20},{28,24},{1,29},{... | collective-permute-start | bytes 786440 | tf_op jit(solution)/shard_map/ppermute | solution.py:322
  29.2 11.3 %gather_fusion = bf16[2048,256]{1,0:T(8,128)(2,1)} fusion(bf16[8192,256]{1,0:T(8,128)(2,1)} %param.10, s32[2048]{0:T(1024)S(1)} %broadcast_clamp_fusion), kind=kCustom, calls=%fused_computation | custom fusion | bytes 2105344 | tf_op jit(solution)/shard_map/gather | solution.py:323
  40.5 3.9 %all-to-all-start.1 = ((bf16[32,64,256]{2,1,0:T(8,128)(2,1)}), bf16[32,64,256]{2,1,0:T(8,128)(2,1)S(1)}, u32[]{:S(2)}, u32[]{:S(2)}) async-start(bf16[32,64,256]{2,1,0:T(8,128)(2,1)} %bitcast.18), calls=%async_computation.1 | async-start | bytes 2097152 | tf_op jit(solution)/shard_map/all_to_all | solution.py:330
  45.7 1.5 collective-permute-start.7
  47.2 26.8 %collective-permute-done.8.refs_5_ = bf16[512,256]{1,0:T(8,128)(2,1)S(1)} collective-permute-done((bf16[512,256]{1,0:T(8,128)(2,1)S(1)}, bf16[512,256]{1,0:T(8,128)(2,1)S(1)}, u32[]{:S(2)}, u32[]{:S(2)}) %collective-permute-start.8) | collective-permute-done | bytes 262176 | tf_op jit(solution)/shard_map/ppermute | solution.py:325
  75.4 2.7 %collective-permute-start.5 = (bf16[528,256]{1,0:T(8,128)(2,1)S(1)}, bf16[528,256]{1,0:T(8,128)(2,1)S(1)}, u32[]{:S(2)}, u32[]{:S(2)}) collective-permute-start(bf16[528,256]{1,0:T(8,128)(2,1)S(1)} %pick.1.a_ref.refs_0_.message_ref), channel_id=1, source_target_pairs={{0,2},{1,3},{2,0},{3,1},{4,6},{5,7},{6,4},{7,5},{8,10},{9,11},{10,... | collective-permute-start | bytes 811016 | tf_op jit(solution)/shard_map/ppermute | solution.py:334
  78.5 2.3 %collective-permute-start.6 = (bf16[528,256]{1,0:T(8,128)(2,1)S(1)}, bf16[528,256]{1,0:T(8,128)(2,1)S(1)}, u32[]{:S(2)}, u32[]{:S(2)}) collective-permute-start(bf16[528,256]{1,0:T(8,128)(2,1)S(1)} %pick.1.a_ref.refs_0_.message_ref), channel_id=1, source_target_pairs={{0,3},{1,0},{2,1},{3,2},{4,7},{5,4},{6,5},{7,6},{8,11},{9,8},{10,9... | collective-permute-start | bytes 811016 | tf_op jit(solution)/shard_map/ppermute | solution.py:334
  83.7 5.9 %collective-permute-done.4.a_ref.refs_1_ = bf16[528,256]{1,0:T(8,128)(2,1)S(1)} collective-permute-done((bf16[528,256]{1,0:T(8,128)(2,1)S(1)}, bf16[528,256]{1,0:T(8,128)(2,1)S(1)}, u32[]{:S(2)}, u32[]{:S(2)}) %collective-permute-start.4) | collective-permute-done | bytes 270368 | tf_op jit(solution)/shard_map/ppermute | solution.py:334
  93.2 1.7 collective-permute-start.11
  94.9 2.0 %collective-permute-start.12 = (f32[1,2048]{1,0:T(1,128)S(1)}, f32[1,2048]{1,0:T(1,128)S(1)}, u32[]{:S(2)}, u32[]{:S(2)}) collective-permute-start(f32[1,2048]{1,0:T(1,128)S(1)} %constant_dynamic-update-slice_fusion.refs_4_), channel_id=1, source_target_pairs={{0,3},{1,0},{2,1},{3,2},{4,7},{5,4},{6,5},{7,6},{8,11},{9,8},{10,9... | collective-permute-start | bytes 24584 | tf_op jit(solution)/shard_map/ppermute | solution.py:340
  99.1 2.8 %collective-permute-start.14 = (bf16[256,256]{1,0:T(8,128)(2,1)S(1)}, bf16[256,256]{1,0:T(8,128)(2,1)S(1)}, u32[]{:S(2)}, u32[]{:S(2)}) collective-permute-start(bf16[256,256]{1,0:T(8,128)(2,1)S(1)} %get-tuple-element.69), channel_id=1, source_target_pairs={{0,28},{4,0},{8,4},{12,8},{16,12},{20,16},{24,20},{28,24},{1,29},{... | collective-permute-start | bytes 393224 | tf_op jit(solution)/shard_map/ppermute | solution.py:348
  103.8 4.4 %collective-permute-done.13 = bf16[256,256]{1,0:T(8,128)(2,1)S(1)} collective-permute-done((bf16[256,256]{1,0:T(8,128)(2,1)S(1)}, bf16[256,256]{1,0:T(8,128)(2,1)S(1)}, u32[]{:S(2)}, u32[]{:S(2)}) %collective-permute-start.13) | collective-permute-done | bytes 131104 | tf_op jit(solution)/shard_map/ppermute | solution.py:347
  111.0 2.5 %collective-permute-done.16 = bf16[512,256]{1,0:T(8,128)(2,1)S(1)} collective-permute-done((bf16[512,256]{1,0:T(8,128)(2,1)S(1)}, bf16[512,256]{1,0:T(8,128)(2,1)S(1)}, u32[]{:S(2)}, u32[]{:S(2)}) %collective-permute-start.16) | collective-permute-done | bytes 262176 | tf_op jit(solution)/shard_map/ppermute | solution.py:348
  113.6 1.5 collective-permute-done.15
  116.8 1.8 mix.5
  118.5 3.4 %collective-permute-done.18 = bf16[512,256]{1,0:T(8,128)(2,1)S(1)} collective-permute-done((bf16[512,256]{1,0:T(8,128)(2,1)S(1)}, bf16[512,256]{1,0:T(8,128)(2,1)S(1)}, u32[]{:S(2)}, u32[]{:S(2)}) %collective-permute-start.18) | collective-permute-done | bytes 262176 | tf_op jit(solution)/shard_map/ppermute | solution.py:348
  123.5 2.5 %collective-permute-start.20 = (bf16[512,256]{1,0:T(8,128)(2,1)S(1)}, bf16[512,256]{1,0:T(8,128)(2,1)S(1)}, u32[]{:S(2)}, u32[]{:S(2)}) collective-permute-start(bf16[512,256]{1,0:T(8,128)(2,1)S(1)} %add_convert_fusion.1), channel_id=1, source_target_pairs={{0,28},{4,0},{8,4},{12,8},{16,12},{20,16},{24,20},{28,24},{1,29},{... | collective-permute-start | bytes 786440 | tf_op jit(solution)/shard_map/ppermute | solution.py:357
  126.0 6.3 %collective-permute-done.19.up_ref = bf16[512,256]{1,0:T(8,128)(2,1)S(1)} collective-permute-done((bf16[512,256]{1,0:T(8,128)(2,1)S(1)}, bf16[512,256]{1,0:T(8,128)(2,1)S(1)}, u32[]{:S(2)}, u32[]{:S(2)}) %collective-permute-start.19) | collective-permute-done | bytes 262176 | tf_op jit(solution)/shard_map/ppermute | solution.py:356
  132.3 1.6 finish.1
  133.9 8.2 %collective-permute-start.21 = (f32[512,256]{1,0:T(8,128)S(1)}, f32[512,256]{1,0:T(8,128)S(1)}, u32[]{:S(2)}, u32[]{:S(2)}) collective-permute-start(f32[512,256]{1,0:T(8,128)S(1)} %get-tuple-element.82), channel_id=1, source_target_pairs={{0,32},{32,0},{1,33},{33,1},{2,34},{34,2},{3,35},{35,3},{4,36},{36... | collective-permute-start | bytes 1572872 | tf_op jit(solution)/shard_map/ppermute | solution.py:294
  142.1 1.5 collective-permute-done.21
  143.7 14.2 %all_to_all.36 = bf16[16,32,256]{2,1,0:T(8,128)(2,1)S(1)} all-to-all(bf16[16,32,256]{2,1,0:T(8,128)(2,1)S(1)} %bitcast.19), channel_id=1, replica_groups=mesh['y'=4,'core'=2,'z'=8,'x'=4] {'y','x'}, dimensions={0} | all-to-all | bytes 524288 | tf_op jit(solution)/shard_map/all_to_all | solution.py:296
  158.1 5.4 %collective-permute-start.23 = (f32[32,256]{1,0:T(8,128)S(1)}, f32[32,256]{1,0:T(8,128)S(1)}, u32[]{:S(2)}, u32[]{:S(2)}) collective-permute-start(f32[32,256]{1,0:T(8,128)S(1)} %convert_reduce_fusion), channel_id=1, source_target_pairs={{0,8},{4,12},{8,0},{12,4},{16,24},{20,28},{24,16},{28,20},{1,9},{5... | collective-permute-start | bytes 98312 | tf_op jit(solution)/shard_map/ppermute | solution.py:298
  163.5 1.6 collective-permute-done.23
  165.2 2.9 %collective-permute-done.24 = f32[32,256]{1,0:T(8,128)S(1)} collective-permute-done((f32[32,256]{1,0:T(8,128)S(1)}, f32[32,256]{1,0:T(8,128)S(1)}, u32[]{:S(2)}, u32[]{:S(2)}) %collective-permute-start.24) | collective-permute-done | bytes 32800 | tf_op jit(solution)/shard_map/ppermute | solution.py:298
  170.4 4.4 %collective-permute-done.25 = f32[32,256]{1,0:T(8,128)S(1)} collective-permute-done((f32[32,256]{1,0:T(8,128)S(1)}, f32[32,256]{1,0:T(8,128)S(1)}, u32[]{:S(2)}, u32[]{:S(2)}) %collective-permute-start.25) | collective-permute-done | bytes 32800 | tf_op jit(solution)/shard_map/ppermute | solution.py:300
  174.9 10.1 %all_to_all.37 = bf16[16,32,256]{2,1,0:T(8,128)(2,1)S(1)} all-to-all(bf16[16,32,256]{2,1,0:T(8,128)(2,1)S(1)} %broadcast_in_dim.5), channel_id=1, replica_groups=mesh['y'=4,'core'=2,'z'=8,'x'=4] {'y','x'}, dimensions={0} | all-to-all | bytes 524288 | tf_op jit(solution)/shard_map/all_to_all | solution.py:303
  185.0 5.8 %collective-permute-start.26 = (bf16[512,256]{1,0:T(8,128)(2,1)S(1)}, bf16[512,256]{1,0:T(8,128)(2,1)S(1)}, u32[]{:S(2)}, u32[]{:S(2)}) collective-permute-start(bf16[512,256]{1,0:T(8,128)(2,1)S(1)} %bitcast.20), channel_id=1, source_target_pairs={{0,32},{32,0},{1,33},{33,1},{2,34},{34,2},{3,35},{35,3},{4,36},{36... | collective-permute-start | bytes 786440 | tf_op jit(solution)/shard_map/ppermute | solution.py:304
  (77 shorter events, 24.8 us)
Async XLA Ops:
  3.3 23.1 %collective-permute-start = (bf16[512,256]{1,0:T(8,128)(2,1)}, bf16[512,256]{1,0:T(8,128)(2,1)S(1)}, u32[]{:S(2)}, u32[]{:S(2)}) collective-permute-start(bf16[512,256]{1,0:T(8,128)(2,1)} %get-tuple-element.51.refs_0_), channel_id=1, source_target_pairs={{0,4},{4,8},{8,12},{12,16},{16,20},{20,24},{24,28},{28,0},{1,5},{5... | collective-permute-start | bytes 786440 | tf_op jit(solution)/shard_map/ppermute | solution.py:317
  5.9 20.6 %collective-permute-start.1 = (bf16[512,256]{1,0:T(8,128)(2,1)}, bf16[512,256]{1,0:T(8,128)(2,1)S(1)}, u32[]{:S(2)}, u32[]{:S(2)}) collective-permute-start(bf16[512,256]{1,0:T(8,128)(2,1)} %get-tuple-element.51.refs_0_), channel_id=1, source_target_pairs={{0,28},{4,0},{8,4},{12,8},{16,12},{20,16},{24,20},{28,24},{1,29},{... | collective-permute-start | bytes 786440 | tf_op jit(solution)/shard_map/ppermute | solution.py:318
  26.5 14.1 %collective-permute-start.2 = (bf16[512,256]{1,0:T(8,128)(2,1)S(1)}, bf16[512,256]{1,0:T(8,128)(2,1)S(1)}, u32[]{:S(2)}, u32[]{:S(2)}) collective-permute-start(bf16[512,256]{1,0:T(8,128)(2,1)S(1)} %collective-permute-done.refs_7_), channel_id=1, source_target_pairs={{0,4},{4,8},{8,12},{12,16},{16,20},{20,24},{24,28},{28,0},{1,5},{5... | collective-permute-start | bytes 786440 | tf_op jit(solution)/shard_map/ppermute | solution.py:321
  26.8 13.7 %collective-permute-start.3 = (bf16[512,256]{1,0:T(8,128)(2,1)S(1)}, bf16[512,256]{1,0:T(8,128)(2,1)S(1)}, u32[]{:S(2)}, u32[]{:S(2)}) collective-permute-start(bf16[512,256]{1,0:T(8,128)(2,1)S(1)} %collective-permute-done.1.refs_1_), channel_id=1, source_target_pairs={{0,28},{4,0},{8,4},{12,8},{16,12},{20,16},{24,20},{28,24},{1,29},{... | collective-permute-start | bytes 786440 | tf_op jit(solution)/shard_map/ppermute | solution.py:322
  29.2 44.8 %copy-start.4 = (bf16[512]{0:T(512)(128)(2,1)S(1)}, bf16[512]{0:T(512)(128)(2,1)}, u32[]{:S(2)}) copy-start(bf16[512]{0:T(512)(128)(2,1)} %param.13) | copy-start | bytes 3076
  29.2 44.9 %copy-start.3 = (s32[512,1]{0,1:T(1,128)S(1)}, s32[512,1]{0,1:T(1,128)}, u32[]{:S(2)}) copy-start(s32[512,1]{0,1:T(1,128)} %param.11) | copy-start | bytes 6148
  29.2 51.6 %copy-start.1 = (bf16[512,256]{1,0:T(8,128)(2,1)S(1)}, bf16[512,256]{1,0:T(8,128)(2,1)}, u32[]{:S(2)}) copy-start(bf16[512,256]{1,0:T(8,128)(2,1)} %get-tuple-element.51.refs_0_) | copy-start | bytes 786436
  40.5 33.6 %all-to-all-start.1 = ((bf16[32,64,256]{2,1,0:T(8,128)(2,1)}), bf16[32,64,256]{2,1,0:T(8,128)(2,1)S(1)}, u32[]{:S(2)}, u32[]{:S(2)}) async-start(bf16[32,64,256]{2,1,0:T(8,128)(2,1)} %bitcast.18), calls=%async_computation.1 | async-start | bytes 2097152 | tf_op jit(solution)/shard_map/all_to_all | solution.py:330
  44.5 29.6 %collective-permute-start.8 = (bf16[512,256]{1,0:T(8,128)(2,1)S(1)}, bf16[512,256]{1,0:T(8,128)(2,1)S(1)}, u32[]{:S(2)}, u32[]{:S(2)}) collective-permute-start(bf16[512,256]{1,0:T(8,128)(2,1)S(1)} %collective-permute-done.2.refs_6_), channel_id=1, source_target_pairs={{0,4},{4,8},{8,12},{12,16},{16,20},{20,24},{24,28},{28,0},{1,5},{5... | collective-permute-start | bytes 786440 | tf_op jit(solution)/shard_map/ppermute | solution.py:325
  45.7 35.1 %collective-permute-start.7 = (bf16[512,256]{1,0:T(8,128)(2,1)S(1)}, bf16[512,256]{1,0:T(8,128)(2,1)S(1)}, u32[]{:S(2)}, u32[]{:S(2)}) collective-permute-start(bf16[512,256]{1,0:T(8,128)(2,1)S(1)} %collective-permute-done.3.refs_2_), channel_id=1, source_target_pairs={{0,28},{4,0},{8,4},{12,8},{16,12},{20,16},{24,20},{28,24},{1,29},{... | collective-permute-start | bytes 786440 | tf_op jit(solution)/shard_map/ppermute | solution.py:326
  74.1 6.8 %collective-permute-start.9 = (bf16[512,256]{1,0:T(8,128)(2,1)S(1)}, bf16[512,256]{1,0:T(8,128)(2,1)S(1)}, u32[]{:S(2)}, u32[]{:S(2)}) collective-permute-start(bf16[512,256]{1,0:T(8,128)(2,1)S(1)} %collective-permute-done.8.refs_5_), channel_id=1, source_target_pairs={{0,4},{4,8},{8,12},{12,16},{16,20},{20,24},{24,28},{28,0},{1,5},{5... | collective-permute-start | bytes 786440 | tf_op jit(solution)/shard_map/ppermute | solution.py:327
  75.4 7.0 %collective-permute-start.5 = (bf16[528,256]{1,0:T(8,128)(2,1)S(1)}, bf16[528,256]{1,0:T(8,128)(2,1)S(1)}, u32[]{:S(2)}, u32[]{:S(2)}) collective-permute-start(bf16[528,256]{1,0:T(8,128)(2,1)S(1)} %pick.1.a_ref.refs_0_.message_ref), channel_id=1, source_target_pairs={{0,2},{1,3},{2,0},{3,1},{4,6},{5,7},{6,4},{7,5},{8,10},{9,11},{10,... | collective-permute-start | bytes 811016 | tf_op jit(solution)/shard_map/ppermute | solution.py:334
  78.1 11.4 %collective-permute-start.4 = (bf16[528,256]{1,0:T(8,128)(2,1)S(1)}, bf16[528,256]{1,0:T(8,128)(2,1)S(1)}, u32[]{:S(2)}, u32[]{:S(2)}) collective-permute-start(bf16[528,256]{1,0:T(8,128)(2,1)S(1)} %pick.1.a_ref.refs_0_.message_ref), channel_id=1, source_target_pairs={{0,1},{1,2},{2,3},{3,0},{4,5},{5,6},{6,7},{7,4},{8,9},{9,10},{10,1... | collective-permute-start | bytes 811016 | tf_op jit(solution)/shard_map/ppermute | solution.py:334
  78.5 12.4 %collective-permute-start.6 = (bf16[528,256]{1,0:T(8,128)(2,1)S(1)}, bf16[528,256]{1,0:T(8,128)(2,1)S(1)}, u32[]{:S(2)}, u32[]{:S(2)}) collective-permute-start(bf16[528,256]{1,0:T(8,128)(2,1)S(1)} %pick.1.a_ref.refs_0_.message_ref), channel_id=1, source_target_pairs={{0,3},{1,0},{2,1},{3,2},{4,7},{5,4},{6,5},{7,6},{8,11},{9,8},{10,9... | collective-permute-start | bytes 811016 | tf_op jit(solution)/shard_map/ppermute | solution.py:334
  92.2 4.7 %collective-permute-start.10 = (f32[1,2048]{1,0:T(1,128)S(1)}, f32[1,2048]{1,0:T(1,128)S(1)}, u32[]{:S(2)}, u32[]{:S(2)}) collective-permute-start(f32[1,2048]{1,0:T(1,128)S(1)} %constant_dynamic-update-slice_fusion.refs_4_), channel_id=1, source_target_pairs={{0,1},{1,2},{2,3},{3,0},{4,5},{5,6},{6,7},{7,4},{8,9},{9,10},{10,1... | collective-permute-start | bytes 24584 | tf_op jit(solution)/shard_map/ppermute | solution.py:340
  93.2 4.0 %collective-permute-start.11 = (f32[1,2048]{1,0:T(1,128)S(1)}, f32[1,2048]{1,0:T(1,128)S(1)}, u32[]{:S(2)}, u32[]{:S(2)}) collective-permute-start(f32[1,2048]{1,0:T(1,128)S(1)} %constant_dynamic-update-slice_fusion.refs_4_), channel_id=1, source_target_pairs={{0,2},{1,3},{2,0},{3,1},{4,6},{5,7},{6,4},{7,5},{8,10},{9,11},{10,... | collective-permute-start | bytes 24584 | tf_op jit(solution)/shard_map/ppermute | solution.py:340
  94.9 2.8 %collective-permute-start.12 = (f32[1,2048]{1,0:T(1,128)S(1)}, f32[1,2048]{1,0:T(1,128)S(1)}, u32[]{:S(2)}, u32[]{:S(2)}) collective-permute-start(f32[1,2048]{1,0:T(1,128)S(1)} %constant_dynamic-update-slice_fusion.refs_4_), channel_id=1, source_target_pairs={{0,3},{1,0},{2,1},{3,2},{4,7},{5,4},{6,5},{7,6},{8,11},{9,8},{10,9... | collective-permute-start | bytes 24584 | tf_op jit(solution)/shard_map/ppermute | solution.py:340
  99.1 4.7 %collective-permute-start.14 = (bf16[256,256]{1,0:T(8,128)(2,1)S(1)}, bf16[256,256]{1,0:T(8,128)(2,1)S(1)}, u32[]{:S(2)}, u32[]{:S(2)}) collective-permute-start(bf16[256,256]{1,0:T(8,128)(2,1)S(1)} %get-tuple-element.69), channel_id=1, source_target_pairs={{0,28},{4,0},{8,4},{12,8},{16,12},{20,16},{24,20},{28,24},{1,29},{... | collective-permute-start | bytes 393224 | tf_op jit(solution)/shard_map/ppermute | solution.py:348
  103.1 5.1 %collective-permute-start.13 = (bf16[256,256]{1,0:T(8,128)(2,1)S(1)}, bf16[256,256]{1,0:T(8,128)(2,1)S(1)}, u32[]{:S(2)}, u32[]{:S(2)}) collective-permute-start(bf16[256,256]{1,0:T(8,128)(2,1)S(1)} %get-tuple-element.66), channel_id=1, source_target_pairs={{0,4},{4,8},{8,12},{12,16},{16,20},{20,24},{24,28},{28,0},{1,5},{5... | collective-permute-start | bytes 393224 | tf_op jit(solution)/shard_map/ppermute | solution.py:347
  108.3 5.3 %collective-permute-start.16 = (bf16[512,256]{1,0:T(8,128)(2,1)S(1)}, bf16[512,256]{1,0:T(8,128)(2,1)S(1)}, u32[]{:S(2)}, u32[]{:S(2)}) collective-permute-start(bf16[512,256]{1,0:T(8,128)(2,1)S(1)} %pad_maximum_fusion.1), channel_id=1, source_target_pairs={{0,28},{4,0},{8,4},{12,8},{16,12},{20,16},{24,20},{28,24},{1,29},{... | collective-permute-start | bytes 786440 | tf_op jit(solution)/shard_map/ppermute | solution.py:348
  108.3 6.8 %collective-permute-start.15 = (bf16[512,256]{1,0:T(8,128)(2,1)S(1)}, bf16[512,256]{1,0:T(8,128)(2,1)S(1)}, u32[]{:S(2)}, u32[]{:S(2)}) collective-permute-start(bf16[512,256]{1,0:T(8,128)(2,1)S(1)} %pad_maximum_fusion), channel_id=1, source_target_pairs={{0,4},{4,8},{8,12},{12,16},{16,20},{20,24},{24,28},{28,0},{1,5},{5... | collective-permute-start | bytes 786440 | tf_op jit(solution)/shard_map/ppermute | solution.py:347
  115.2 17.1 %copy-start = (bf16[1024,256]{1,0:T(8,128)(2,1)S(1)}, bf16[1024,256]{1,0:T(8,128)(2,1)}, u32[]{:S(2)}) copy-start(bf16[1024,256]{1,0:T(8,128)(2,1)} %weight_ref.1) | copy-start | bytes 1572868
  115.2 6.7 %collective-permute-start.18 = (bf16[512,256]{1,0:T(8,128)(2,1)S(1)}, bf16[512,256]{1,0:T(8,128)(2,1)S(1)}, u32[]{:S(2)}, u32[]{:S(2)}) collective-permute-start(bf16[512,256]{1,0:T(8,128)(2,1)S(1)} %add_convert_fusion.3), channel_id=1, source_target_pairs={{0,28},{4,0},{8,4},{12,8},{16,12},{20,16},{24,20},{28,24},{1,29},{... | collective-permute-start | bytes 786440 | tf_op jit(solution)/shard_map/ppermute | solution.py:348
  115.3 7.8 %collective-permute-start.17 = (bf16[512,256]{1,0:T(8,128)(2,1)S(1)}, bf16[512,256]{1,0:T(8,128)(2,1)S(1)}, u32[]{:S(2)}, u32[]{:S(2)}) collective-permute-start(bf16[512,256]{1,0:T(8,128)(2,1)S(1)} %add_convert_fusion.4), channel_id=1, source_target_pairs={{0,4},{4,8},{8,12},{12,16},{16,20},{20,24},{24,28},{28,0},{1,5},{5... | collective-permute-start | bytes 786440 | tf_op jit(solution)/shard_map/ppermute | solution.py:347
  123.2 9.1 %collective-permute-start.19 = (bf16[512,256]{1,0:T(8,128)(2,1)S(1)}, bf16[512,256]{1,0:T(8,128)(2,1)S(1)}, u32[]{:S(2)}, u32[]{:S(2)}) collective-permute-start(bf16[512,256]{1,0:T(8,128)(2,1)S(1)} %add_convert_fusion.2), channel_id=1, source_target_pairs={{0,4},{4,8},{8,12},{12,16},{16,20},{20,24},{24,28},{28,0},{1,5},{5... | collective-permute-start | bytes 786440 | tf_op jit(solution)/shard_map/ppermute | solution.py:356
  123.5 8.8 %collective-permute-start.20 = (bf16[512,256]{1,0:T(8,128)(2,1)S(1)}, bf16[512,256]{1,0:T(8,128)(2,1)S(1)}, u32[]{:S(2)}, u32[]{:S(2)}) collective-permute-start(bf16[512,256]{1,0:T(8,128)(2,1)S(1)} %add_convert_fusion.1), channel_id=1, source_target_pairs={{0,28},{4,0},{8,4},{12,8},{16,12},{20,16},{24,20},{28,24},{1,29},{... | collective-permute-start | bytes 786440 | tf_op jit(solution)/shard_map/ppermute | solution.py:357
  133.9 9.8 %collective-permute-start.21 = (f32[512,256]{1,0:T(8,128)S(1)}, f32[512,256]{1,0:T(8,128)S(1)}, u32[]{:S(2)}, u32[]{:S(2)}) collective-permute-start(f32[512,256]{1,0:T(8,128)S(1)} %get-tuple-element.82), channel_id=1, source_target_pairs={{0,32},{32,0},{1,33},{33,1},{2,34},{34,2},{3,35},{35,3},{4,36},{36... | collective-permute-start | bytes 1572872 | tf_op jit(solution)/shard_map/ppermute | solution.py:294
  158.0 5.5 %collective-permute-start.22 = (f32[32,256]{1,0:T(8,128)S(1)}, f32[32,256]{1,0:T(8,128)S(1)}, u32[]{:S(2)}, u32[]{:S(2)}) collective-permute-start(f32[32,256]{1,0:T(8,128)S(1)} %convert_reduce_fusion), channel_id=1, source_target_pairs={{0,4},{4,0},{8,12},{12,8},{16,20},{20,16},{24,28},{28,24},{1,5},{5... | collective-permute-start | bytes 98312 | tf_op jit(solution)/shard_map/ppermute | solution.py:298
  158.1 7.1 %collective-permute-start.23 = (f32[32,256]{1,0:T(8,128)S(1)}, f32[32,256]{1,0:T(8,128)S(1)}, u32[]{:S(2)}, u32[]{:S(2)}) collective-permute-start(f32[32,256]{1,0:T(8,128)S(1)} %convert_reduce_fusion), channel_id=1, source_target_pairs={{0,8},{4,12},{8,0},{12,4},{16,24},{20,28},{24,16},{28,20},{1,9},{5... | collective-permute-start | bytes 98312 | tf_op jit(solution)/shard_map/ppermute | solution.py:298
  163.5 4.6 %collective-permute-start.24 = (f32[32,256]{1,0:T(8,128)S(1)}, f32[32,256]{1,0:T(8,128)S(1)}, u32[]{:S(2)}, u32[]{:S(2)}) collective-permute-start(f32[32,256]{1,0:T(8,128)S(1)} %convert_reduce_fusion), channel_id=1, source_target_pairs={{0,12},{4,8},{8,4},{12,0},{16,28},{20,24},{24,20},{28,16},{1,13},{... | collective-permute-start | bytes 98312 | tf_op jit(solution)/shard_map/ppermute | solution.py:298
  168.1 6.8 %collective-permute-start.25 = (f32[32,256]{1,0:T(8,128)S(1)}, f32[32,256]{1,0:T(8,128)S(1)}, u32[]{:S(2)}, u32[]{:S(2)}) collective-permute-start(f32[32,256]{1,0:T(8,128)S(1)} %add_add_fusion), channel_id=1, source_target_pairs={{0,16},{4,20},{8,24},{12,28},{16,0},{20,4},{24,8},{28,12},{1,17},{... | collective-permute-start | bytes 98312 | tf_op jit(solution)/shard_map/ppermute | solution.py:300
  185.0 7.0 %collective-permute-start.26 = (bf16[512,256]{1,0:T(8,128)(2,1)S(1)}, bf16[512,256]{1,0:T(8,128)(2,1)S(1)}, u32[]{:S(2)}, u32[]{:S(2)}) collective-permute-start(bf16[512,256]{1,0:T(8,128)(2,1)S(1)} %bitcast.20), channel_id=1, source_target_pairs={{0,32},{32,0},{1,33},{33,1},{2,34},{34,2},{3,35},{35,3},{4,36},{36... | collective-permute-start | bytes 786440 | tf_op jit(solution)/shard_map/ppermute | solution.py:304
  (1 other events, 17.1 us)

commit v5 on v2

--- a/solution.py
+++ b/solution.py
@@ -203,25 +203,34 @@
     )(*anchors, *totals)
 
 
-def mix_kernel(which, a_ref, *refs):
-    parts, outs = refs[:NX], refs[NX:]
-    for k, out in zip(which, outs):
+def mix_kernel(a_ref, *refs):
+    parts = refs[:NX]
+    out_ref, up_ref, down_ref = refs[NX:]
+    half = up_ref.shape[0]
+
+    def one(k, carry):
         total = None
         for b, part in enumerate(parts):
             size = part.shape[2]
             term = jnp.dot(part[k], a_ref[b * size : (b + 1) * size, :], preferred_element_type=F32)
             total = term if total is None else total + term
-        out[...] = total.astype(out.dtype)
-
-
-def mix(which, scaled, parts, dtype):
-    shape = jax.ShapeDtypeStruct((parts[0].shape[1], scaled.shape[1]), dtype)
-    return vmem_call(
-        functools.partial(mix_kernel, which),
-        tuple(shape for _ in which),
+        out_ref[k] = total
+        return carry
+
+    lax.fori_loop(0, NZ, one, 0)
+    up_ref[...] = out_ref[NZ // 2, :half].astype(BF)
+    down_ref[...] = out_ref[NZ // 2, half:].astype(BF)
+
+
+def mix(scaled, parts):
+    n, width = parts[0].shape[1], scaled.shape[1]
+    half = jax.ShapeDtypeStruct((n // 2, width), BF)
+    return vmem_call(
+        mix_kernel,
+        (jax.ShapeDtypeStruct((NZ, n, width), F32), half, half),
         "mix",
         in_specs=[IN_VMEM] * (1 + NX),
-        out_specs=tuple(IN_VMEM for _ in which),
+        out_specs=(IN_VMEM,) * 3,
     )(scaled, *parts)
 
 
@@ -240,7 +249,7 @@
     n = up_ref.shape[0]
     feats = feats_ref[...]
     unit, inv = project(feats, weight_ref[...])
-    mixed = own_ref[...] + up_ref[...].astype(F32) + down_ref[...].astype(F32)
+    mixed = own_ref[0] + up_ref[...].astype(F32) + down_ref[...].astype(F32)
     w = column_of((1.0 / TEMPER) * weights_of(message_ref, n))
     grad = mixed - w * message_ref[:n, :].astype(F32)
     along = jnp.sum(unit * grad, axis=1, keepdims=True)
@@ -272,17 +281,17 @@
     rows, width = keep.shape
     v = keep + lax.ppermute(send, "core", flip(NC, 1))
     many = NY * NX
-    v = lax.all_to_all(v, ("y", "x"), 0, 0, tiled=True)
+    v = lax.all_to_all(v.astype(BF), ("y", "x"), 0, 0, tiled=True).astype(F32)
     v = jnp.sum(v.reshape(many, rows // many, width), axis=0)
     got = [lax.ppermute(v, "z", flip(NZ, m)) for m in (1, 2, 3)]
     v = (v + got[0]) + (got[1] + got[2])
     v = v + lax.ppermute(v, "z", flip(NZ, 4))
-    v, beside = lax.optimization_barrier((v, beside))
+    v, beside = lax.optimization_barrier((v.astype(BF), beside))
     v = lax.optimization_barrier(jnp.broadcast_to(v[None], (many,) + v.shape))
     v = lax.all_to_all(v.reshape(rows, width), ("y", "x"), 0, 0, tiled=True)
     other = lax.ppermute(v, "core", flip(NC, 1))
     low, high = jnp.where(core == 0, v, other), jnp.where(core == 0, other, v)
-    return jnp.concatenate([low, high], axis=0), beside
+    return jnp.concatenate([low, high], axis=0).astype(F32), beside
 
 
 def local(features, weight, support_queue, owner_shard, slot_row, loss_weight):
@@ -319,10 +328,9 @@
     everyone = [total] + [lax.ppermute(total, "x", shift(NX, k)) for k in (1, 2, 3)]
     scaled = scale(blocks, everyone, n)
 
-    (far,) = mix((4,), scaled, parts, BF)
-    up, down = far[: n // 2], far[n // 2 :]
+    mixed, up, down = mix(scaled, parts)
     for d in (3, 2, 1):
-        up_part, down_part = mix((d, NZ - d), scaled, parts, F32)
+        up_part, down_part = mixed[d], mixed[NZ - d]
         up = lax.ppermute(up, "z", shift(NZ, 1)).astype(F32)
         down = lax.ppermute(down, "z", shift(NZ, -1)).astype(F32)
         if d == 3:
@@ -330,12 +338,11 @@
             down = jnp.concatenate([down_part[: n // 2], down + down_part[n // 2 :]], axis=0)
         else:
             up, down = up + up_part, down + down_part
-        up, down = up.astype(BF), down.astype(BF)
-    (own,) = mix((0,), scaled, parts, F32)
+        up, down = lax.optimization_barrier((up.astype(BF), down.astype(BF)))
     up = lax.ppermute(up, "z", shift(NZ, 1))
     down = lax.ppermute(down, "z", shift(NZ, -1))
 
-    grad_proj, keep, send = finish(core, up, down, own, message, features, weight)
+    grad_proj, keep, send = finish(core, up, down, mixed, message, features, weight)
     grad_feats = jnp.dot(grad_proj, weight.T, preferred_element_type=F32).astype(BF)
     grad_weight, grad_feats = sum_everywhere(keep, send, core, grad_feats)
     return (grad_feats, grad_weight)

time: 201 us -> 198 us (0.985)
  waiting for transfers between devices: 53 us -> 63.2 us
  local copies, waits for them, and re-layouts: 20.9 us -> 13.7 us
  blocking collectives: 45.7 us -> 40.6 us
    unnamed x29 -> x17, local copies, waits for them, and re-layouts: 9.45 us -> 2.24 us
    ppermute x1, waiting for transfers between devices: 0.01 us -> 5.98 us  [local(): up = lax.ppermute(up, 'z', shift(NZ, 1))]
    ppermute x3, waiting for transfers between devices: 4.48 us -> 9.94 us  [local(): up = lax.ppermute(up, 'z', shift(NZ, 1)).astype(F32)]
    ppermute x3, starting transfers between devices: 9.08 us -> 3.7 us  [local(): down = lax.ppermute(down, 'z', shift(NZ, -1)).astype(F32)]
    ppermute x3, starting transfers between devices: 0.47 us -> 5.04 us  [local(): up = lax.ppermute(up, 'z', shift(NZ, 1)).astype(F32)]
    ppermute x1, starting transfers between devices: 3.19 us -> 0.41 us  [local(): down = lax.ppermute(down, 'z', shift(NZ, -1))]
    all_to_all x1, blocking collectives: 16.7 us -> 13.9 us  [sum_everywhere(): v = lax.all_to_all(v.astype(BF), ('y', 'x'), 0, 0, tiled=True).astype(F32)]
    all_to_all x1, blocking collectives: 12.5 us -> 10.1 us  [sum_everywhere(): v = lax.all_to_all(v.reshape(rows, width), ('y', 'x'), 0, 0, tiled=True)]
  transfers between devices with their start and end apart: 28 -> 28, of which waited for: 16 -> 17; matrix products, arithmetic and copies ran while one was open for 7% -> 7% of each run, Pallas kernels for 5% -> 3%
where the time goes in v5:
time: 198 us; the launch traced here: 197 us
  waiting for transfers between devices  63.2 us (32%)
  starting transfers between devices  58.5 us (30%)
  blocking collectives  40.6 us (21%)
  Pallas kernels  17.1 us (9%)
  local copies, waits for them, and re-layouts  13.7 us (7%)
    ppermute x1, waiting for transfers between devices, local(): views[5] = lax.ppermute(views[6], 'z', shift(NZ, 1))  26.8 us
    all_to_all x1, blocking collectives, local(): lax.all_to_all(wanted, QUEUE, split_axis=0, concat_axis=0, tiled=True)  16.6 us
    all_to_all x1, blocking collectives, sum_everywhere(): v = lax.all_to_all(v.astype(BF), ('y', 'x'), 0, 0, tiled=True).astype(F32)  13.9 us
    gather x1, local copies, waits for them, and re-layouts, local(): picked = support_queue[asked]  11.3 us
    all_to_all x1, blocking collectives, sum_everywhere(): v = lax.all_to_all(v.reshape(rows, width), ('y', 'x'), 0, 0, tiled=True)  10.1 us
    ppermute x3, waiting for transfers between devices, local(): up = lax.ppermute(up, 'z', shift(NZ, 1)).astype(F32)  9.94 us
    ppermute x1, starting transfers between devices, sum_everywhere(): v = keep + lax.ppermute(send, 'core', flip(NC, 1))  9.13 us
    ppermute x3, waiting for transfers between devices, local(): lax.ppermute(message, 'x', shift(NX, k))  6.1 us
  transfers between devices with their start and end apart: 28, of which 17 were waited for; matrix products, arithmetic and copies ran while one was open for 7% of the time, Pallas kernels for 3%

profile of v5, /device:TPU:1, one launch (start us, length us, event | category | flops | bytes accessed | tf_op | source)
XLA Modules:
  0.0 197.2 jit_solution(4847242527912060734)
XLA Ops:
  0.6 2.7 %begin.1 = (bf16[512,256]{1,0:T(8,128)(2,1)}, s32[32,64]{1,0:T(8,128)}) custom-call(bf16[512,1024]{1,0:T(8,128)(2,1)} %feats_ref.1, bf16[1024,256]{1,0:T(8,128)(2,1)} %weight_ref.1, s32[1,512]{1,0:T(1,128)} %bitcast.44, s32[1,512]{1,0:T(1,128)} %bitcast.51), custom_call_target="tpu_custom_call" | custom-call | tf_op jit(solution)/shard_map/begin/pallas_call | solution.py:100
  3.3 2.5 %collective-permute-start = (bf16[512,256]{1,0:T(8,128)(2,1)}, bf16[512,256]{1,0:T(8,128)(2,1)S(1)}, u32[]{:S(2)}, u32[]{:S(2)}) collective-permute-start(bf16[512,256]{1,0:T(8,128)(2,1)} %get-tuple-element.45.refs_0_), channel_id=1, source_target_pairs={{0,4},{4,8},{8,12},{12,16},{16,20},{20,24},{24,28},{28,0},{1,5},{5... | collective-permute-start | bytes 786440 | tf_op jit(solution)/shard_map/ppermute | solution.py:305
  5.9 4.0 %collective-permute-start.1 = (bf16[512,256]{1,0:T(8,128)(2,1)}, bf16[512,256]{1,0:T(8,128)(2,1)S(1)}, u32[]{:S(2)}, u32[]{:S(2)}) collective-permute-start(bf16[512,256]{1,0:T(8,128)(2,1)} %get-tuple-element.45.refs_0_), channel_id=1, source_target_pairs={{0,28},{4,0},{8,4},{12,8},{16,12},{20,16},{24,20},{28,24},{1,29},{... | collective-permute-start | bytes 786440 | tf_op jit(solution)/shard_map/ppermute | solution.py:306
  9.9 16.6 %all_to_all.35 = s32[32,1,64]{2,1,0:T(1,128)S(1)} all-to-all(s32[32,1,64]{2,1,0:T(1,128)} %bitcast.50), channel_id=1, replica_groups=mesh['y'=4,'core'=2,'z'=8,'x'=4] {'z','x'}, dimensions={0} | all-to-all | bytes 16384 | tf_op jit(solution)/shard_map/all_to_all | solution.py:307
  26.8 2.3 %collective-permute-start.3 = (bf16[512,256]{1,0:T(8,128)(2,1)S(1)}, bf16[512,256]{1,0:T(8,128)(2,1)S(1)}, u32[]{:S(2)}, u32[]{:S(2)}) collective-permute-start(bf16[512,256]{1,0:T(8,128)(2,1)S(1)} %collective-permute-done.1.refs_1_), channel_id=1, source_target_pairs={{0,28},{4,0},{8,4},{12,8},{16,12},{20,16},{24,20},{28,24},{1,29},{... | collective-permute-start | bytes 786440 | tf_op jit(solution)/shard_map/ppermute | solution.py:310
  29.2 11.3 %gather_fusion = bf16[2048,256]{1,0:T(8,128)(2,1)} fusion(bf16[8192,256]{1,0:T(8,128)(2,1)} %param.10, s32[2048]{0:T(1024)S(1)} %broadcast_clamp_fusion), kind=kCustom, calls=%fused_computation | custom fusion | bytes 2105344 | tf_op jit(solution)/shard_map/gather | solution.py:311
  40.5 3.9 %all-to-all-start.1 = ((bf16[32,64,256]{2,1,0:T(8,128)(2,1)}), bf16[32,64,256]{2,1,0:T(8,128)(2,1)S(1)}, u32[]{:S(2)}, u32[]{:S(2)}) async-start(bf16[32,64,256]{2,1,0:T(8,128)(2,1)} %bitcast.46), calls=%async_computation.1 | async-start | bytes 2097152 | tf_op jit(solution)/shard_map/all_to_all | solution.py:318
  47.2 26.8 %collective-permute-done.8.refs_5_ = bf16[512,256]{1,0:T(8,128)(2,1)S(1)} collective-permute-done((bf16[512,256]{1,0:T(8,128)(2,1)S(1)}, bf16[512,256]{1,0:T(8,128)(2,1)S(1)}, u32[]{:S(2)}, u32[]{:S(2)}) %collective-permute-start.8) | collective-permute-done | bytes 262176 | tf_op jit(solution)/shard_map/ppermute | solution.py:313
  75.4 2.7 %collective-permute-start.5 = (bf16[528,256]{1,0:T(8,128)(2,1)S(1)}, bf16[528,256]{1,0:T(8,128)(2,1)S(1)}, u32[]{:S(2)}, u32[]{:S(2)}) collective-permute-start(bf16[528,256]{1,0:T(8,128)(2,1)S(1)} %pick.1.a_ref.refs_0_.message_ref), channel_id=1, source_target_pairs={{0,2},{1,3},{2,0},{3,1},{4,6},{5,7},{6,4},{7,5},{8,10},{9,11},{10,... | collective-permute-start | bytes 811016 | tf_op jit(solution)/shard_map/ppermute | solution.py:322
  78.5 2.3 %collective-permute-start.6 = (bf16[528,256]{1,0:T(8,128)(2,1)S(1)}, bf16[528,256]{1,0:T(8,128)(2,1)S(1)}, u32[]{:S(2)}, u32[]{:S(2)}) collective-permute-start(bf16[528,256]{1,0:T(8,128)(2,1)S(1)} %pick.1.a_ref.refs_0_.message_ref), channel_id=1, source_target_pairs={{0,3},{1,0},{2,1},{3,2},{4,7},{5,4},{6,5},{7,6},{8,11},{9,8},{10,9... | collective-permute-start | bytes 811016 | tf_op jit(solution)/shard_map/ppermute | solution.py:322
  83.7 5.9 %collective-permute-done.4.a_ref.refs_1_ = bf16[528,256]{1,0:T(8,128)(2,1)S(1)} collective-permute-done((bf16[528,256]{1,0:T(8,128)(2,1)S(1)}, bf16[528,256]{1,0:T(8,128)(2,1)S(1)}, u32[]{:S(2)}, u32[]{:S(2)}) %collective-permute-start.4) | collective-permute-done | bytes 270368 | tf_op jit(solution)/shard_map/ppermute | solution.py:322
  93.2 1.7 collective-permute-start.11
  94.9 2.0 collective-permute-start.12
  98.3 5.7 %mix.1 = (f32[8,512,256]{2,1,0:T(8,128)S(1)}, bf16[256,256]{1,0:T(8,128)(2,1)S(1)}, bf16[256,256]{1,0:T(8,128)(2,1)S(1)}) custom-call(bf16[2048,256]{1,0:T(8,128)(2,1)S(1)} %scale.1.a_ref, bf16[8,512,512]{2,1,0:T(8,128)(2,1)S(1)} %get-tuple-element.56.refs_0_, bf16[8,512,512]{2,1,0:T(8,128)(2,1)S(1)} %get-tuple-element.57.refs_1_, ...), custom_call_target="tpu_custom_call" | custom-call | tf_op jit(solution)/shard_map/mix/pallas_call | solution.py:228
  107.2 2.0 %collective-permute-done.13 = bf16[256,256]{1,0:T(8,128)(2,1)S(1)} collective-permute-done((bf16[256,256]{1,0:T(8,128)(2,1)S(1)}, bf16[256,256]{1,0:T(8,128)(2,1)S(1)}, u32[]{:S(2)}, u32[]{:S(2)}) %collective-permute-start.13) | collective-permute-done | bytes 131104 | tf_op jit(solution)/shard_map/ppermute | solution.py:334
  109.3 1.8 collective-permute-start.15
  112.2 3.7 %collective-permute-done.15 = bf16[512,256]{1,0:T(8,128)(2,1)S(1)} collective-permute-done((bf16[512,256]{1,0:T(8,128)(2,1)S(1)}, bf16[512,256]{1,0:T(8,128)(2,1)S(1)}, u32[]{:S(2)}, u32[]{:S(2)}) %collective-permute-start.15) | collective-permute-done | bytes 262176 | tf_op jit(solution)/shard_map/ppermute | solution.py:334
  116.4 2.1 %collective-permute-start.17 = (bf16[512,256]{1,0:T(8,128)(2,1)S(1)}, bf16[512,256]{1,0:T(8,128)(2,1)S(1)}, u32[]{:S(2)}, u32[]{:S(2)}) collective-permute-start(bf16[512,256]{1,0:T(8,128)(2,1)S(1)} %get-tuple-element.65), channel_id=1, source_target_pairs={{0,4},{4,8},{8,12},{12,16},{16,20},{20,24},{24,28},{28,0},{1,5},{5... | collective-permute-start | bytes 786440 | tf_op jit(solution)/shard_map/ppermute | solution.py:334
  119.4 4.3 %collective-permute-done.17 = bf16[512,256]{1,0:T(8,128)(2,1)S(1)} collective-permute-done((bf16[512,256]{1,0:T(8,128)(2,1)S(1)}, bf16[512,256]{1,0:T(8,128)(2,1)S(1)}, u32[]{:S(2)}, u32[]{:S(2)}) %collective-permute-start.17) | collective-permute-done | bytes 262176 | tf_op jit(solution)/shard_map/ppermute | solution.py:334
  124.9 2.3 %collective-permute-start.19 = (bf16[512,256]{1,0:T(8,128)(2,1)S(1)}, bf16[512,256]{1,0:T(8,128)(2,1)S(1)}, u32[]{:S(2)}, u32[]{:S(2)}) collective-permute-start(bf16[512,256]{1,0:T(8,128)(2,1)S(1)} %get-tuple-element.67), channel_id=1, source_target_pairs={{0,4},{4,8},{8,12},{12,16},{16,20},{20,24},{24,28},{28,0},{1,5},{5... | collective-permute-start | bytes 786440 | tf_op jit(solution)/shard_map/ppermute | solution.py:342
  127.7 6.0 %collective-permute-done.19.up_ref = bf16[512,256]{1,0:T(8,128)(2,1)S(1)} collective-permute-done((bf16[512,256]{1,0:T(8,128)(2,1)S(1)}, bf16[512,256]{1,0:T(8,128)(2,1)S(1)}, u32[]{:S(2)}, u32[]{:S(2)}) %collective-permute-start.19) | collective-permute-done | bytes 262176 | tf_op jit(solution)/shard_map/ppermute | solution.py:342
  133.7 1.9 collective-permute-done.20.down_ref
  135.6 2.2 %copy-done.1 = f32[8,512,256]{2,1,0:T(8,128)S(1)} copy-done((f32[8,512,256]{2,1,0:T(8,128)S(1)}, f32[8,512,256]{2,1,0:T(8,128)}, u32[]{:S(2)}) %copy-start.1) | copy-done | bytes 4194328
  139.4 9.1 %collective-permute-start.21 = (f32[512,256]{1,0:T(8,128)S(1)}, f32[512,256]{1,0:T(8,128)S(1)}, u32[]{:S(2)}, u32[]{:S(2)}) collective-permute-start(f32[512,256]{1,0:T(8,128)S(1)} %get-tuple-element.70), channel_id=1, source_target_pairs={{0,32},{32,0},{1,33},{33,1},{2,34},{34,2},{3,35},{35,3},{4,36},{36... | collective-permute-start | bytes 1572872 | tf_op jit(solution)/shard_map/ppermute | solution.py:282
  150.1 13.9 %all_to_all.36 = bf16[16,32,256]{2,1,0:T(8,128)(2,1)S(1)} all-to-all(bf16[16,32,256]{2,1,0:T(8,128)(2,1)S(1)} %bitcast.47), channel_id=1, replica_groups=mesh['y'=4,'core'=2,'z'=8,'x'=4] {'y','x'}, dimensions={0} | all-to-all | bytes 524288 | tf_op jit(solution)/shard_map/all_to_all | solution.py:284
  165.5 2.1 %collective-permute-start.23 = (f32[32,256]{1,0:T(8,128)S(1)}, f32[32,256]{1,0:T(8,128)S(1)}, u32[]{:S(2)}, u32[]{:S(2)}) collective-permute-start(f32[32,256]{1,0:T(8,128)S(1)} %convert_reduce_fusion), channel_id=1, source_target_pairs={{0,8},{4,12},{8,0},{12,4},{16,24},{20,28},{24,16},{28,20},{1,9},{5... | collective-permute-start | bytes 98312 | tf_op jit(solution)/shard_map/ppermute | solution.py:286
  167.7 1.7 collective-permute-done.23
  169.5 2.7 %collective-permute-done.24 = f32[32,256]{1,0:T(8,128)S(1)} collective-permute-done((f32[32,256]{1,0:T(8,128)S(1)}, f32[32,256]{1,0:T(8,128)S(1)}, u32[]{:S(2)}, u32[]{:S(2)}) %collective-permute-start.24) | collective-permute-done | bytes 32800 | tf_op jit(solution)/shard_map/ppermute | solution.py:286
  172.2 2.3 %collective-permute-start.25 = (f32[32,256]{1,0:T(8,128)S(1)}, f32[32,256]{1,0:T(8,128)S(1)}, u32[]{:S(2)}, u32[]{:S(2)}) collective-permute-start(f32[32,256]{1,0:T(8,128)S(1)} %add_add_fusion), channel_id=1, source_target_pairs={{0,16},{4,20},{8,24},{12,28},{16,0},{20,4},{24,8},{28,12},{1,17},{... | collective-permute-start | bytes 98312 | tf_op jit(solution)/shard_map/ppermute | solution.py:288
  176.0 3.0 %collective-permute-done.25 = f32[32,256]{1,0:T(8,128)S(1)} collective-permute-done((f32[32,256]{1,0:T(8,128)S(1)}, f32[32,256]{1,0:T(8,128)S(1)}, u32[]{:S(2)}, u32[]{:S(2)}) %collective-permute-start.25) | collective-permute-done | bytes 32800 | tf_op jit(solution)/shard_map/ppermute | solution.py:288
  179.0 10.1 %all_to_all.37 = bf16[16,32,256]{2,1,0:T(8,128)(2,1)S(1)} all-to-all(bf16[16,32,256]{2,1,0:T(8,128)(2,1)S(1)} %broadcast_in_dim.5), channel_id=1, replica_groups=mesh['y'=4,'core'=2,'z'=8,'x'=4] {'y','x'}, dimensions={0} | all-to-all | bytes 524288 | tf_op jit(solution)/shard_map/all_to_all | solution.py:291
  189.1 5.8 %collective-permute-start.26 = (bf16[512,256]{1,0:T(8,128)(2,1)S(1)}, bf16[512,256]{1,0:T(8,128)(2,1)S(1)}, u32[]{:S(2)}, u32[]{:S(2)}) collective-permute-start(bf16[512,256]{1,0:T(8,128)(2,1)S(1)} %bitcast.48), channel_id=1, source_target_pairs={{0,32},{32,0},{1,33},{33,1},{2,34},{34,2},{3,35},{35,3},{4,36},{36... | collective-permute-start | bytes 786440 | tf_op jit(solution)/shard_map/ppermute | solution.py:292
  (74 shorter events, 28.6 us)
Async XLA Ops:
  3.3 23.1 %collective-permute-start = (bf16[512,256]{1,0:T(8,128)(2,1)}, bf16[512,256]{1,0:T(8,128)(2,1)S(1)}, u32[]{:S(2)}, u32[]{:S(2)}) collective-permute-start(bf16[512,256]{1,0:T(8,128)(2,1)} %get-tuple-element.45.refs_0_), channel_id=1, source_target_pairs={{0,4},{4,8},{8,12},{12,16},{16,20},{20,24},{24,28},{28,0},{1,5},{5... | collective-permute-start | bytes 786440 | tf_op jit(solution)/shard_map/ppermute | solution.py:305
  5.9 20.6 %collective-permute-start.1 = (bf16[512,256]{1,0:T(8,128)(2,1)}, bf16[512,256]{1,0:T(8,128)(2,1)S(1)}, u32[]{:S(2)}, u32[]{:S(2)}) collective-permute-start(bf16[512,256]{1,0:T(8,128)(2,1)} %get-tuple-element.45.refs_0_), channel_id=1, source_target_pairs={{0,28},{4,0},{8,4},{12,8},{16,12},{20,16},{24,20},{28,24},{1,29},{... | collective-permute-start | bytes 786440 | tf_op jit(solution)/shard_map/ppermute | solution.py:306
  26.5 14.1 %collective-permute-start.2 = (bf16[512,256]{1,0:T(8,128)(2,1)S(1)}, bf16[512,256]{1,0:T(8,128)(2,1)S(1)}, u32[]{:S(2)}, u32[]{:S(2)}) collective-permute-start(bf16[512,256]{1,0:T(8,128)(2,1)S(1)} %collective-permute-done.refs_7_), channel_id=1, source_target_pairs={{0,4},{4,8},{8,12},{12,16},{16,20},{20,24},{24,28},{28,0},{1,5},{5... | collective-permute-start | bytes 786440 | tf_op jit(solution)/shard_map/ppermute | solution.py:309
  26.8 13.7 %collective-permute-start.3 = (bf16[512,256]{1,0:T(8,128)(2,1)S(1)}, bf16[512,256]{1,0:T(8,128)(2,1)S(1)}, u32[]{:S(2)}, u32[]{:S(2)}) collective-permute-start(bf16[512,256]{1,0:T(8,128)(2,1)S(1)} %collective-permute-done.1.refs_1_), channel_id=1, source_target_pairs={{0,28},{4,0},{8,4},{12,8},{16,12},{20,16},{24,20},{28,24},{1,29},{... | collective-permute-start | bytes 786440 | tf_op jit(solution)/shard_map/ppermute | solution.py:310
  29.2 44.8 %copy-start.6 = (bf16[512]{0:T(512)(128)(2,1)S(1)}, bf16[512]{0:T(512)(128)(2,1)}, u32[]{:S(2)}) copy-start(bf16[512]{0:T(512)(128)(2,1)} %param.13) | copy-start | bytes 3076
  29.2 44.9 %copy-start.5 = (s32[512,1]{0,1:T(1,128)S(1)}, s32[512,1]{0,1:T(1,128)}, u32[]{:S(2)}) copy-start(s32[512,1]{0,1:T(1,128)} %param.11) | copy-start | bytes 6148
  29.2 51.6 %copy-start.3 = (bf16[512,256]{1,0:T(8,128)(2,1)S(1)}, bf16[512,256]{1,0:T(8,128)(2,1)}, u32[]{:S(2)}) copy-start(bf16[512,256]{1,0:T(8,128)(2,1)} %get-tuple-element.45.refs_0_) | copy-start | bytes 786436
  40.5 33.6 %all-to-all-start.1 = ((bf16[32,64,256]{2,1,0:T(8,128)(2,1)}), bf16[32,64,256]{2,1,0:T(8,128)(2,1)S(1)}, u32[]{:S(2)}, u32[]{:S(2)}) async-start(bf16[32,64,256]{2,1,0:T(8,128)(2,1)} %bitcast.46), calls=%async_computation.1 | async-start | bytes 2097152 | tf_op jit(solution)/shard_map/all_to_all | solution.py:318
  44.5 29.6 %collective-permute-start.8 = (bf16[512,256]{1,0:T(8,128)(2,1)S(1)}, bf16[512,256]{1,0:T(8,128)(2,1)S(1)}, u32[]{:S(2)}, u32[]{:S(2)}) collective-permute-start(bf16[512,256]{1,0:T(8,128)(2,1)S(1)} %collective-permute-done.2.refs_6_), channel_id=1, source_target_pairs={{0,4},{4,8},{8,12},{12,16},{16,20},{20,24},{24,28},{28,0},{1,5},{5... | collective-permute-start | bytes 786440 | tf_op jit(solution)/shard_map/ppermute | solution.py:313
  45.7 35.1 %collective-permute-start.7 = (bf16[512,256]{1,0:T(8,128)(2,1)S(1)}, bf16[512,256]{1,0:T(8,128)(2,1)S(1)}, u32[]{:S(2)}, u32[]{:S(2)}) collective-permute-start(bf16[512,256]{1,0:T(8,128)(2,1)S(1)} %collective-permute-done.3.refs_2_), channel_id=1, source_target_pairs={{0,28},{4,0},{8,4},{12,8},{16,12},{20,16},{24,20},{28,24},{1,29},{... | collective-permute-start | bytes 786440 | tf_op jit(solution)/shard_map/ppermute | solution.py:314
  74.1 6.8 %collective-permute-start.9 = (bf16[512,256]{1,0:T(8,128)(2,1)S(1)}, bf16[512,256]{1,0:T(8,128)(2,1)S(1)}, u32[]{:S(2)}, u32[]{:S(2)}) collective-permute-start(bf16[512,256]{1,0:T(8,128)(2,1)S(1)} %collective-permute-done.8.refs_5_), channel_id=1, source_target_pairs={{0,4},{4,8},{8,12},{12,16},{16,20},{20,24},{24,28},{28,0},{1,5},{5... | collective-permute-start | bytes 786440 | tf_op jit(solution)/shard_map/ppermute | solution.py:315
  75.4 7.0 %collective-permute-start.5 = (bf16[528,256]{1,0:T(8,128)(2,1)S(1)}, bf16[528,256]{1,0:T(8,128)(2,1)S(1)}, u32[]{:S(2)}, u32[]{:S(2)}) collective-permute-start(bf16[528,256]{1,0:T(8,128)(2,1)S(1)} %pick.1.a_ref.refs_0_.message_ref), channel_id=1, source_target_pairs={{0,2},{1,3},{2,0},{3,1},{4,6},{5,7},{6,4},{7,5},{8,10},{9,11},{10,... | collective-permute-start | bytes 811016 | tf_op jit(solution)/shard_map/ppermute | solution.py:322
  78.1 11.4 %collective-permute-start.4 = (bf16[528,256]{1,0:T(8,128)(2,1)S(1)}, bf16[528,256]{1,0:T(8,128)(2,1)S(1)}, u32[]{:S(2)}, u32[]{:S(2)}) collective-permute-start(bf16[528,256]{1,0:T(8,128)(2,1)S(1)} %pick.1.a_ref.refs_0_.message_ref), channel_id=1, source_target_pairs={{0,1},{1,2},{2,3},{3,0},{4,5},{5,6},{6,7},{7,4},{8,9},{9,10},{10,1... | collective-permute-start | bytes 811016 | tf_op jit(solution)/shard_map/ppermute | solution.py:322
  78.5 12.4 %collective-permute-start.6 = (bf16[528,256]{1,0:T(8,128)(2,1)S(1)}, bf16[528,256]{1,0:T(8,128)(2,1)S(1)}, u32[]{:S(2)}, u32[]{:S(2)}) collective-permute-start(bf16[528,256]{1,0:T(8,128)(2,1)S(1)} %pick.1.a_ref.refs_0_.message_ref), channel_id=1, source_target_pairs={{0,3},{1,0},{2,1},{3,2},{4,7},{5,4},{6,5},{7,6},{8,11},{9,8},{10,9... | collective-permute-start | bytes 811016 | tf_op jit(solution)/shard_map/ppermute | solution.py:322
  92.2 4.7 %collective-permute-start.10 = (f32[1,2048]{1,0:T(1,128)S(1)}, f32[1,2048]{1,0:T(1,128)S(1)}, u32[]{:S(2)}, u32[]{:S(2)}) collective-permute-start(f32[1,2048]{1,0:T(1,128)S(1)} %constant_dynamic-update-slice_fusion.refs_4_), channel_id=1, source_target_pairs={{0,1},{1,2},{2,3},{3,0},{4,5},{5,6},{6,7},{7,4},{8,9},{9,10},{10,1... | collective-permute-start | bytes 24584 | tf_op jit(solution)/shard_map/ppermute | solution.py:328
  93.2 4.0 %collective-permute-start.11 = (f32[1,2048]{1,0:T(1,128)S(1)}, f32[1,2048]{1,0:T(1,128)S(1)}, u32[]{:S(2)}, u32[]{:S(2)}) collective-permute-start(f32[1,2048]{1,0:T(1,128)S(1)} %constant_dynamic-update-slice_fusion.refs_4_), channel_id=1, source_target_pairs={{0,2},{1,3},{2,0},{3,1},{4,6},{5,7},{6,4},{7,5},{8,10},{9,11},{10,... | collective-permute-start | bytes 24584 | tf_op jit(solution)/shard_map/ppermute | solution.py:328
  94.9 2.8 %collective-permute-start.12 = (f32[1,2048]{1,0:T(1,128)S(1)}, f32[1,2048]{1,0:T(1,128)S(1)}, u32[]{:S(2)}, u32[]{:S(2)}) collective-permute-start(f32[1,2048]{1,0:T(1,128)S(1)} %constant_dynamic-update-slice_fusion.refs_4_), channel_id=1, source_target_pairs={{0,3},{1,0},{2,1},{3,2},{4,7},{5,4},{6,5},{7,6},{8,11},{9,8},{10,9... | collective-permute-start | bytes 24584 | tf_op jit(solution)/shard_map/ppermute | solution.py:328
  104.1 5.1 %collective-permute-start.13 = (bf16[256,256]{1,0:T(8,128)(2,1)S(1)}, bf16[256,256]{1,0:T(8,128)(2,1)S(1)}, u32[]{:S(2)}, u32[]{:S(2)}) collective-permute-start(bf16[256,256]{1,0:T(8,128)(2,1)S(1)} %get-tuple-element.60), channel_id=1, source_target_pairs={{0,4},{4,8},{8,12},{12,16},{16,20},{20,24},{24,28},{28,0},{1,5},{5... | collective-permute-start | bytes 393224 | tf_op jit(solution)/shard_map/ppermute | solution.py:334
  105.3 3.9 %collective-permute-start.14 = (bf16[256,256]{1,0:T(8,128)(2,1)S(1)}, bf16[256,256]{1,0:T(8,128)(2,1)S(1)}, u32[]{:S(2)}, u32[]{:S(2)}) collective-permute-start(bf16[256,256]{1,0:T(8,128)(2,1)S(1)} %get-tuple-element.62), channel_id=1, source_target_pairs={{0,28},{4,0},{8,4},{12,8},{16,12},{20,16},{24,20},{28,24},{1,29},{... | collective-permute-start | bytes 393224 | tf_op jit(solution)/shard_map/ppermute | solution.py:335
  107.1 28.5 %copy-start.2 = (bf16[1024,256]{1,0:T(8,128)(2,1)S(1)}, bf16[1024,256]{1,0:T(8,128)(2,1)}, u32[]{:S(2)}) copy-start(bf16[1024,256]{1,0:T(8,128)(2,1)} %weight_ref.1) | copy-start | bytes 1572868
  109.3 6.6 %collective-permute-start.15 = (bf16[512,256]{1,0:T(8,128)(2,1)S(1)}, bf16[512,256]{1,0:T(8,128)(2,1)S(1)}, u32[]{:S(2)}, u32[]{:S(2)}) collective-permute-start(bf16[512,256]{1,0:T(8,128)(2,1)S(1)} %get-tuple-element.63), channel_id=1, source_target_pairs={{0,4},{4,8},{8,12},{12,16},{16,20},{20,24},{24,28},{28,0},{1,5},{5... | collective-permute-start | bytes 786440 | tf_op jit(solution)/shard_map/ppermute | solution.py:334
  111.1 5.2 %collective-permute-start.16 = (bf16[512,256]{1,0:T(8,128)(2,1)S(1)}, bf16[512,256]{1,0:T(8,128)(2,1)S(1)}, u32[]{:S(2)}, u32[]{:S(2)}) collective-permute-start(bf16[512,256]{1,0:T(8,128)(2,1)S(1)} %get-tuple-element.64), channel_id=1, source_target_pairs={{0,28},{4,0},{8,4},{12,8},{16,12},{20,16},{24,20},{28,24},{1,29},{... | collective-permute-start | bytes 786440 | tf_op jit(solution)/shard_map/ppermute | solution.py:335
  116.4 7.2 %collective-permute-start.17 = (bf16[512,256]{1,0:T(8,128)(2,1)S(1)}, bf16[512,256]{1,0:T(8,128)(2,1)S(1)}, u32[]{:S(2)}, u32[]{:S(2)}) collective-permute-start(bf16[512,256]{1,0:T(8,128)(2,1)S(1)} %get-tuple-element.65), channel_id=1, source_target_pairs={{0,4},{4,8},{8,12},{12,16},{16,20},{20,24},{24,28},{28,0},{1,5},{5... | collective-permute-start | bytes 786440 | tf_op jit(solution)/shard_map/ppermute | solution.py:334
  118.5 6.3 %collective-permute-start.18 = (bf16[512,256]{1,0:T(8,128)(2,1)S(1)}, bf16[512,256]{1,0:T(8,128)(2,1)S(1)}, u32[]{:S(2)}, u32[]{:S(2)}) collective-permute-start(bf16[512,256]{1,0:T(8,128)(2,1)S(1)} %get-tuple-element.66), channel_id=1, source_target_pairs={{0,28},{4,0},{8,4},{12,8},{16,12},{20,16},{24,20},{28,24},{1,29},{... | collective-permute-start | bytes 786440 | tf_op jit(solution)/shard_map/ppermute | solution.py:335
  124.9 8.7 %collective-permute-start.19 = (bf16[512,256]{1,0:T(8,128)(2,1)S(1)}, bf16[512,256]{1,0:T(8,128)(2,1)S(1)}, u32[]{:S(2)}, u32[]{:S(2)}) collective-permute-start(bf16[512,256]{1,0:T(8,128)(2,1)S(1)} %get-tuple-element.67), channel_id=1, source_target_pairs={{0,4},{4,8},{8,12},{12,16},{16,20},{20,24},{24,28},{28,0},{1,5},{5... | collective-permute-start | bytes 786440 | tf_op jit(solution)/shard_map/ppermute | solution.py:342
  127.3 8.3 %collective-permute-start.20 = (bf16[512,256]{1,0:T(8,128)(2,1)S(1)}, bf16[512,256]{1,0:T(8,128)(2,1)S(1)}, u32[]{:S(2)}, u32[]{:S(2)}) collective-permute-start(bf16[512,256]{1,0:T(8,128)(2,1)S(1)} %get-tuple-element.68), channel_id=1, source_target_pairs={{0,28},{4,0},{8,4},{12,8},{16,12},{20,16},{24,20},{28,24},{1,29},{... | collective-permute-start | bytes 786440 | tf_op jit(solution)/shard_map/ppermute | solution.py:343
  139.4 10.7 %collective-permute-start.21 = (f32[512,256]{1,0:T(8,128)S(1)}, f32[512,256]{1,0:T(8,128)S(1)}, u32[]{:S(2)}, u32[]{:S(2)}) collective-permute-start(f32[512,256]{1,0:T(8,128)S(1)} %get-tuple-element.70), channel_id=1, source_target_pairs={{0,32},{32,0},{1,33},{33,1},{2,34},{34,2},{3,35},{35,3},{4,36},{36... | collective-permute-start | bytes 1572872 | tf_op jit(solution)/shard_map/ppermute | solution.py:282
  164.1 3.6 %collective-permute-start.22 = (f32[32,256]{1,0:T(8,128)S(1)}, f32[32,256]{1,0:T(8,128)S(1)}, u32[]{:S(2)}, u32[]{:S(2)}) collective-permute-start(f32[32,256]{1,0:T(8,128)S(1)} %convert_reduce_fusion), channel_id=1, source_target_pairs={{0,4},{4,0},{8,12},{12,8},{16,20},{20,16},{24,28},{28,24},{1,5},{5... | collective-permute-start | bytes 98312 | tf_op jit(solution)/shard_map/ppermute | solution.py:286
  165.5 4.0 %collective-permute-start.23 = (f32[32,256]{1,0:T(8,128)S(1)}, f32[32,256]{1,0:T(8,128)S(1)}, u32[]{:S(2)}, u32[]{:S(2)}) collective-permute-start(f32[32,256]{1,0:T(8,128)S(1)} %convert_reduce_fusion), channel_id=1, source_target_pairs={{0,8},{4,12},{8,0},{12,4},{16,24},{20,28},{24,16},{28,20},{1,9},{5... | collective-permute-start | bytes 98312 | tf_op jit(solution)/shard_map/ppermute | solution.py:286
  167.6 4.6 %collective-permute-start.24 = (f32[32,256]{1,0:T(8,128)S(1)}, f32[32,256]{1,0:T(8,128)S(1)}, u32[]{:S(2)}, u32[]{:S(2)}) collective-permute-start(f32[32,256]{1,0:T(8,128)S(1)} %convert_reduce_fusion), channel_id=1, source_target_pairs={{0,12},{4,8},{8,4},{12,0},{16,28},{20,24},{24,20},{28,16},{1,13},{... | collective-permute-start | bytes 98312 | tf_op jit(solution)/shard_map/ppermute | solution.py:286
  172.2 6.8 %collective-permute-start.25 = (f32[32,256]{1,0:T(8,128)S(1)}, f32[32,256]{1,0:T(8,128)S(1)}, u32[]{:S(2)}, u32[]{:S(2)}) collective-permute-start(f32[32,256]{1,0:T(8,128)S(1)} %add_add_fusion), channel_id=1, source_target_pairs={{0,16},{4,20},{8,24},{12,28},{16,0},{20,4},{24,8},{28,12},{1,17},{... | collective-permute-start | bytes 98312 | tf_op jit(solution)/shard_map/ppermute | solution.py:288
  189.1 7.0 %collective-permute-start.26 = (bf16[512,256]{1,0:T(8,128)(2,1)S(1)}, bf16[512,256]{1,0:T(8,128)(2,1)S(1)}, u32[]{:S(2)}, u32[]{:S(2)}) collective-permute-start(bf16[512,256]{1,0:T(8,128)(2,1)S(1)} %bitcast.48), channel_id=1, source_target_pairs={{0,32},{32,0},{1,33},{33,1},{2,34},{34,2},{3,35},{35,3},{4,36},{36... | collective-permute-start | bytes 786440 | tf_op jit(solution)/shard_map/ppermute | solution.py:292
  (3 other events, 51.3 us)
